TPU v7x, 256 devices: a whole 4x4x8 slice. The times are simulated.
256 devices in a mesh: pcol: 32 (over z, x), prow: 8 (over y, core).
Axes of the slice: x: 4, y: 4, z: 8, core: 2. Of those that a mesh axis runs over, the one named last changes fastest.
Arguments:
- matrix: float32 [8, 8, 128, 2, 32, 128], P(None, 'prow', None, None, 'pcol'), may hold values from -1 to 32, as said below
- node_width: int32 [64], replicated, may hold values from 32 to 128, as said below
- block_pattern: int32 [64, 64], replicated, may hold values from 0 to 1, as said below
- pivot_row_targets: int32 [4, 128], replicated, may hold values from 0 to 8191, as said below
- panel_order: int32 [4], replicated, may hold values from 0 to 63, as said below
Outputs:
- factored: float32 [8, 8, 128, 2, 32, 128], P(None, 'prow', None, None, 'pcol')
Inputs may be any that keep to these rules, and one draw needn't show every extreme that they name: `panel_order`: 4 different supernode blocks. `node_width`: rows and columns of a block at or past its supernode's width are padding. `block_pattern`: every diagonal block is 1, and so is every block from which a panel takes a pivot row in the panel's block column. With p = panel_order[k]: pivot_row_targets[k, r] is p * 128 + r itself, or, only where r < node_width[p], a row within the width of a block that is no panel; all 512 entries are different. `matrix`: once a panel's rows are exchanged, and before any panel's update, each diagonal entry of its diagonal block is larger than the sum of the magnitudes of the other entries of that block in its row and in its column.
All inputs are finite; a program needn't handle non-finite values.
Results may differ from a plain program's by a relative error of at most 0.0001.
Values sent between devices are 32-bit elements; how exact they have to be, the bound alone decides.
No kernel may reach another device: no remote copies, remote signals or barrier semaphores. Data moves between devices by JAX's collectives and lax.ppermute only.
A program may use at most 64 MiB of HBM per device.

v0:
```python
import jax
import jax.numpy as jnp
from jax import lax
from jax.sharding import PartitionSpec as P

highest_pivot = lax.Precision.HIGHEST


def from_root(block, axis, owner):
    block = jnp.where(lax.axis_index(axis) == owner, block, jnp.zeros_like(block))
    return lax.psum(block, axis)


def invert_block(corner):
    identity = jnp.eye(corner.shape[0], dtype=jnp.float32)
    approx = identity / jnp.diagonal(corner)[None, :]
    for sweep_count in range(8):
        approx = jnp.dot(
            approx,
            2.0 * identity - jnp.dot(corner, approx, precision=highest_pivot),
            precision=highest_pivot,
        )
    return approx


def body(matrix, node_width, block_pattern, pivot_row_targets, panel_order):
    rows_here = matrix.shape[0]
    size = matrix.shape[2]
    cols_here = matrix.shape[3]
    row_count = lax.axis_size("prow")
    col_count = lax.axis_size("pcol")
    my_row = lax.axis_index("prow")
    my_col = lax.axis_index("pcol")
    offsets = jnp.arange(size, dtype=jnp.int32)
    row_blocks = jnp.arange(rows_here, dtype=jnp.int32) * row_count + my_row
    col_blocks = jnp.arange(cols_here, dtype=jnp.int32) * col_count + my_col
    row_width = lax.dynamic_index_in_dim(
        node_width.reshape(rows_here, row_count), my_row, 1, keepdims=False
    )
    col_width = lax.dynamic_index_in_dim(
        node_width.reshape(cols_here, col_count), my_col, 1, keepdims=False
    )
    pattern_rows = lax.dynamic_index_in_dim(
        block_pattern.reshape(rows_here, row_count, cols_here * col_count),
        my_row,
        1,
        keepdims=False,
    )
    pattern_local = lax.dynamic_index_in_dim(
        pattern_rows.reshape(rows_here, cols_here, col_count), my_col, 2, keepdims=False
    )
    row_live = offsets[None, :] < row_width[:, None]
    col_live = offsets[None, :] < col_width[:, None]
    kept_mask = (
        (pattern_local[:, None, :, None] > 0)
        & row_live[:, :, None, None]
        & col_live[None, None, :, :]
    )
    same_block = (row_blocks[:, None] == col_blocks[None, :])[:, None, :, None]
    diagonal = offsets[None, :, None, None] == offsets[None, None, None, :]
    padding = same_block & diagonal & (~row_live)[:, :, None, None]
    working = jnp.where(kept_mask, matrix.reshape(rows_here, size, cols_here, size), 0.0)
    working = jnp.where(padding, 1.0, working)
    outside = rows_here * size
    for panel_step in range(pivot_row_targets.shape[0]):
        panel_block = panel_order[panel_step]
        owner_row = panel_block % row_count
        local_row = panel_block // row_count
        owner_col = panel_block % col_count
        local_col = panel_block // col_count
        earlier = panel_order[:panel_step]
        row_pending = ~jnp.any(row_blocks[:, None] == earlier[None, :], axis=1) & (
            row_blocks != panel_block
        )
        col_open = ~jnp.any(col_blocks[:, None] == earlier[None, :], axis=1) & (
            col_blocks != panel_block
        )
        targets = pivot_row_targets[panel_step]
        target_block = targets // size
        owned_here = target_block % row_count == my_row
        target_local = target_block // row_count * size + targets % size
        row_major = working.reshape(rows_here * size, cols_here * size)
        picked = jnp.where(owned_here[:, None], row_major[target_local], 0.0)
        home_rows = lax.dynamic_slice_in_dim(row_major, local_row * size, size, 0)
        home_rows = jnp.where(my_row == owner_row, home_rows, 0.0)
        picked, home_rows = lax.psum((picked, home_rows), "prow")
        moved_rows = owned_here & (targets != panel_block * size + offsets)
        index_home = jnp.where(my_row == owner_row, local_row * size + offsets, outside)
        index_away = jnp.where(moved_rows, target_local, outside)
        row_major = row_major.at[jnp.concatenate([index_home, index_away])].set(
            jnp.concatenate([picked, home_rows]), mode="drop"
        )
        working = row_major.reshape(rows_here, size, cols_here, size)
        column_segment = lax.dynamic_index_in_dim(working, local_col, 2, keepdims=False)
        upper_rows = picked.reshape(size, cols_here, size)
        corner = lax.dynamic_index_in_dim(upper_rows, local_col, 1, keepdims=False)
        diagonal_inverse = invert_block(corner)
        lower_factor = jnp.einsum(
            "oyi,ip->oyp", column_segment, diagonal_inverse, precision=highest_pivot
        )
        lower_factor = from_root(lower_factor, "pcol", owner_col)
        lower_factor = jnp.where(row_pending[:, None, None], lower_factor, 0.0)
        upper_rows = jnp.where(col_open[None, :, None], upper_rows, 0.0)
        working = working - jnp.einsum(
            "tab,bsc->tasc", lower_factor, upper_rows, precision=highest_pivot
        )
        old_column = lax.dynamic_index_in_dim(working, local_col, 2, keepdims=True)
        update_writes = (row_pending & (my_col == owner_col))[:, None, None, None]
        new_column = jnp.where(update_writes, lower_factor[:, :, None, :], old_column)
        working = lax.dynamic_update_index_in_dim(working, new_column, local_col, 2)
    return working.reshape(matrix.shape)


def solution(mesh):
    return jax.shard_map(
        body,
        mesh=mesh,
        in_specs=(P(None, "prow", None, None, "pcol", None), P(), P(), P(), P()),
        out_specs=P(None, "prow", None, None, "pcol", None),
        check_vma=False,
    )
```

profile of v0, /device:TPU:1, one launch (start us, length us, event | category | flops | bytes accessed | tf_op | source)
XLA Modules:
  0.0 926.6 jit_solution(12123004667934547882)
XLA Ops:
  21.8 64.4 %all-reduce.27.cloned.1.call-done = (f32[128,256]{1,0:T(8,128)}, f32[128,256]{1,0:T(8,128)}) async-done(((f32[128,256]{1,0:T(8,128)}, f32[128,256]{1,0:T(8,128)}), (f32[128,256]{1,0:T(8,128)}, f32[128,256]{1,0:T(8,128)})) %all-reduce.27.cloned.1.call-update) | async-done | bytes 262160 | tf_op jit(solution)/shard_map/psum | solution.py:86
  87.3 1.8 scatter_custom_fusion
  89.8 1.2 gather_fusion.1
  95.0 1.4 convolution_select_fusion.3
  97.8 1.3 broadcast_and_fusion.4
  99.1 141.4 %all-reduce.13.cloned.1.call-done = f32[8,128,128]{2,1,0:T(8,128)} async-done(((f32[8,128,128]{2,1,0:T(8,128)}), f32[8,128,128]{2,1,0:T(8,128)}) %all-reduce.13.cloned.1.call-update) | async-done | bytes 524304 | tf_op jit(solution)/shard_map/psum | solution.py:11
  240.5 2.2 convolution_subtract_fusion.3
  246.1 1.3 compare_and_fusion.4
  250.6 60.2 %all-reduce.25.cloned.1.call-done = (f32[128,256]{1,0:T(8,128)}, f32[128,256]{1,0:T(8,128)}) async-done(((f32[128,256]{1,0:T(8,128)}, f32[128,256]{1,0:T(8,128)}), (f32[128,256]{1,0:T(8,128)}, f32[128,256]{1,0:T(8,128)})) %all-reduce.25.cloned.1.call-update) | async-done | bytes 262160 | tf_op jit(solution)/shard_map/psum | solution.py:86
  311.9 2.0 scatter_custom_fusion.1
  319.7 1.4 convolution_select_fusion.2
  321.2 144.0 %all-reduce.15.cloned.1.call-done = f32[8,128,128]{2,1,0:T(8,128)} async-done(((f32[8,128,128]{2,1,0:T(8,128)}), f32[8,128,128]{2,1,0:T(8,128)}) %all-reduce.15.cloned.1.call-update) | async-done | bytes 524304 | tf_op jit(solution)/shard_map/psum | solution.py:11
  465.3 2.2 convolution_subtract_fusion.2
  473.4 62.1 %all-reduce.23.cloned.1.call-done = (f32[128,256]{1,0:T(8,128)}, f32[128,256]{1,0:T(8,128)}) async-done(((f32[128,256]{1,0:T(8,128)}, f32[128,256]{1,0:T(8,128)}), (f32[128,256]{1,0:T(8,128)}, f32[128,256]{1,0:T(8,128)})) %all-reduce.23.cloned.1.call-update) | async-done | bytes 262160 | tf_op jit(solution)/shard_map/psum | solution.py:86
  536.6 1.8 scatter_custom_fusion.2
  544.3 1.4 convolution_select_fusion.1
  547.2 142.6 %all-reduce.17.cloned.1.call-done = f32[8,128,128]{2,1,0:T(8,128)} async-done(((f32[8,128,128]{2,1,0:T(8,128)}), f32[8,128,128]{2,1,0:T(8,128)}) %all-reduce.17.cloned.1.call-update) | async-done | bytes 524304 | tf_op jit(solution)/shard_map/psum | solution.py:11
  689.9 2.2 convolution_subtract_fusion.1
  695.6 64.5 %all-reduce.21.cloned.1.call-done = (f32[128,256]{1,0:T(8,128)}, f32[128,256]{1,0:T(8,128)}) async-done(((f32[128,256]{1,0:T(8,128)}, f32[128,256]{1,0:T(8,128)}), (f32[128,256]{1,0:T(8,128)}, f32[128,256]{1,0:T(8,128)})) %all-reduce.21.cloned.1.call-update) | async-done | bytes 262160 | tf_op jit(solution)/shard_map/psum | solution.py:86
  761.2 1.8 scatter_custom_fusion.3
  768.9 1.4 convolution_select_fusion
  771.6 142.8 %all-reduce.19.cloned.1.call-done = f32[8,128,128]{2,1,0:T(8,128)} async-done(((f32[8,128,128]{2,1,0:T(8,128)}), f32[8,128,128]{2,1,0:T(8,128)}) %all-reduce.19.cloned.1.call-update) | async-done | bytes 524304 | tf_op jit(solution)/shard_map/psum | solution.py:11
  914.5 2.1 convolution_subtract_fusion
  917.8 2.0 copy.165
  (207 shorter events, 49.3 us)
Async XLA Ops:
  6.5 7.7 copy-start
  6.5 79.7 %all-reduce.27.cloned.1.call-start = ((), (), s32[]{:S(2)}) async-start(), calls=%async_computation.7 | async-start | bytes 524288 | tf_op jit(solution)/shard_map/psum | solution.py:86
  6.5 0.7 copy-start.15
  10.5 0.7 copy-start.14
  15.4 1.3 copy-start.9
  19.2 221.3 %all-reduce.13.cloned.1.call-start = ((), (), s32[]{:S(2)}) async-start(), calls=%async_computation | async-start | bytes 1048576 | tf_op jit(solution)/shard_map/psum | solution.py:11
  86.2 1.0 copy-start.5
  86.2 1.1 copy-start.10
  96.3 214.5 %all-reduce.25.cloned.1.call-start = ((), (), s32[]{:S(2)}) async-start(), calls=%async_computation.6 | async-start | bytes 524288 | tf_op jit(solution)/shard_map/psum | solution.py:86
  240.5 2.2 copy-start.2
  246.1 219.2 %all-reduce.15.cloned.1.call-start = ((), (), s32[]{:S(2)}) async-start(), calls=%async_computation.1 | async-start | bytes 1048576 | tf_op jit(solution)/shard_map/psum | solution.py:11
  310.8 1.0 copy-start.7
  310.8 1.1 copy-start.12
  321.1 214.4 %all-reduce.23.cloned.1.call-start = ((), (), s32[]{:S(2)}) async-start(), calls=%async_computation.5 | async-start | bytes 524288 | tf_op jit(solution)/shard_map/psum | solution.py:86
  465.3 2.2 copy-start.1
  470.8 219.1 %all-reduce.17.cloned.1.call-start = ((), (), s32[]{:S(2)}) async-start(), calls=%async_computation.2 | async-start | bytes 1048576 | tf_op jit(solution)/shard_map/psum | solution.py:11
  535.5 1.0 copy-start.6
  535.5 1.1 copy-start.11
  545.7 214.5 %all-reduce.21.cloned.1.call-start = ((), (), s32[]{:S(2)}) async-start(), calls=%async_computation.4 | async-start | bytes 524288 | tf_op jit(solution)/shard_map/psum | solution.py:86
  689.9 2.2 copy-start.3
  695.4 219.0 %all-reduce.19.cloned.1.call-start = ((), (), s32[]{:S(2)}) async-start(), calls=%async_computation.3 | async-start | bytes 1048576 | tf_op jit(solution)/shard_map/psum | solution.py:11
  760.1 1.0 copy-start.8
  760.1 1.1 copy-start.13
  916.6 1.0 copy-start.4
  (1 other events, 0.7 us)
Sparse Core Ops, SparseCore 0:
  19.3 66.8 all-reduce.26
  96.5 144.0 all-reduce.12
  246.2 64.5 all-reduce.24
  321.3 143.9 all-reduce.14
  470.9 64.5 all-reduce.22
  545.8 144.0 all-reduce.16
  695.5 64.5 all-reduce.20
  770.4 144.0 all-reduce.18
where the time goes:
time: 931 us; the launch traced here: 927 us
  waiting for transfers between devices  822 us (88%)
  between operations  27.5 us (3%)
  local copies, waits for them, and re-layouts  27.3 us (3%)
  matrix products  27.2 us (3%)
  other arithmetic  21.8 us (2%)
    psum x4, waiting for transfers between devices, from_root(): return lax.psum(block, axis)  571 us
    psum x4, waiting for transfers between devices, body(): picked, home_rows = lax.psum((picked, home_rows), 'prow')  251 us
  transfers between devices with their start and end apart: 8, of which 8 were waited for; matrix products, arithmetic and copies ran while one was open for 1% of the time, Pallas kernels for 0%

commit v1 on v0

v1 whole, which is shorter than its diff:
```python
import functools

import jax
import jax.numpy as jnp
from jax import lax
from jax.experimental import pallas as pl
from jax.experimental.pallas import tpu as pltpu
from jax.sharding import Mesh, PartitionSpec as P

B = 128
PANELS = 4
S = PANELS * B
BR = 8
N_PROW = 8
N_PCOL = 32
NZ, NX, NY, NC = 8, 4, 4, 2
ROWS = BR * B
CHUNK = ROWS // N_PCOL
VMEM_LIMIT = 40 * 1024 * 1024
HIGHEST = lax.Precision.HIGHEST
F32 = jnp.float32
BF16 = jnp.bfloat16


def iota(shape, dim):
    return lax.broadcasted_iota(jnp.int32, shape, dim)


def dot_full(a, b):
    return jnp.dot(a, b, precision=HIGHEST, preferred_element_type=F32)


def dot_bf16(a, b):
    return jnp.dot(a, b, preferred_element_type=F32)


def split2(v):
    high = v.astype(BF16)
    low = (v - high.astype(F32)).astype(BF16)
    return high, low


def split3(v):
    high = v.astype(BF16)
    rest = v - high.astype(F32)
    middle = rest.astype(BF16)
    low = (rest - middle.astype(F32)).astype(BF16)
    return high, middle, low


def dot3(a, b):
    return dot_bf16(a[0], b[0]) + (dot_bf16(a[0], b[1]) + dot_bf16(a[1], b[0]))


def kept(value, here, row_width, col_width, same_block, row_start):
    rows = iota(value.shape, 0) + row_start
    cols = iota(value.shape, 1)
    value = jnp.where(here & (rows < row_width) & (cols < col_width), value, 0.0)
    return jnp.where(same_block & (rows == cols) & (rows >= row_width), 1.0, value)


def own_rows_kernel(pos, order, width, pattern, target_col, raw, pivots, homes, rows):
    r = pos[0]
    q = pos[1]
    for t in range(BR):
        block_row = t * N_PROW + r
        for s in range(2):
            block_col = s * N_PCOL + q
            rows[t * B : (t + 1) * B, s * B : (s + 1) * B] = kept(
                raw[pl.ds(t * 2 * B + s, B, stride=2), :],
                pattern[block_row, block_col] > 0,
                width[block_row],
                width[block_col],
                block_row == block_col,
                0,
            )
    gather_rows(target_col, rows, pivots, 2 * B)
    for k in range(PANELS):
        p = order[k]
        here = (p % N_PROW) == r
        block = rows[pl.ds(pl.multiple_of((p // N_PROW) * B, B), B), :]
        homes[k * B : (k + 1) * B, :] = jnp.where(here, block, 0.0)


def gather_rows(target_col, rows, out, columns):
    high, middle, low = split3(rows[...])
    for i in range(0, S, B):
        hot = iota((B, ROWS), 1) == target_col[i : i + B, :]
        hot = jnp.where(hot, 1.0, 0.0).astype(BF16)
        out[i : i + B, :] = dot_bf16(hot, high) + (dot_bf16(hot, middle) + dot_bf16(hot, low))


def select_kernel(pos, order, width, pattern, spread, out):
    r = pos[0]
    z = pos[2]
    x = pos[3]
    block_row = z * N_PROW + r
    for k in range(PANELS):
        p = order[k]
        source = p % N_PCOL
        value = jnp.where(
            p >= N_PCOL,
            spread[source, pl.ds(1, CHUNK, stride=2), :],
            spread[source, pl.ds(0, CHUNK, stride=2), :],
        )
        out[:, k * B : (k + 1) * B] = kept(
            value, pattern[block_row, p] > 0, width[block_row], width[p], block_row == p, x * CHUNK
        )


def natural_order(pos, parts, rows):
    z = pos[2]
    x = pos[3]
    for u in range(NX):
        for s in range(NZ):
            t = lax.rem(z - s + NZ, NZ)
            j = lax.rem(x - u + NX, NX)
            start = pl.multiple_of(t * B + j * CHUNK, CHUNK)
            rows[pl.ds(start, CHUNK), :] = parts[u][s]


def panel_rows_kernel(pos, order, target_col, part0, part1, part2, part3, mine, other, home_mine, home_other, rows, pivots, homes):
    r = pos[0]
    c = pos[4]
    natural_order(pos, (part0, part1, part2, part3), rows)
    gather_rows(target_col, rows, pivots, S)
    for k in range(PANELS):
        p = order[k]
        here = (p % N_PROW) == r
        block = rows[pl.ds(pl.multiple_of((p // N_PROW) * B, B), B), :]
        homes[k * B : (k + 1) * B, :] = jnp.where(here, block, 0.0)
    half = S // 2
    first = pl.multiple_of(c * half, half)
    second = pl.multiple_of((1 - c) * half, half)
    mine[...] = pivots[pl.ds(first, half), :]
    other[...] = pivots[pl.ds(second, half), :]
    home_mine[...] = homes[pl.ds(first, half), :]
    home_other[...] = homes[pl.ds(second, half), :]


def invert(corner, work, pivot_rows, out):
    row = iota((B, B), 0)
    col = iota((B, B), 1)
    eye = jnp.where(row == col, 1.0, 0.0)
    diagonal = jnp.where(row == col, corner, 0.0)
    by_col = 1.0 / jnp.sum(diagonal, axis=0, keepdims=True)
    by_row = 1.0 / jnp.sum(diagonal, axis=1, keepdims=True)
    residual = eye - corner * by_col
    approx = by_row * (eye + residual)

    def sweep(state):
        count, error, approx = state
        residual = eye - dot_full(corner, approx)
        return count + 1, jnp.max(jnp.abs(residual)), approx + dot_full(approx, residual)

    def again(state):
        count, error, approx = state
        return (count < 16) & jnp.logical_not(error < 1e-5)

    count, error, approx = lax.while_loop(again, sweep, (0, jnp.float32(1.0), approx))
    out[...] = approx

    @pl.when(jnp.logical_not(error < 1e-5))
    def _():
        work[:, :B] = corner
        work[:, B:] = eye
        row1 = iota((B, 1), 0)
        lane = iota((1, 2 * B), 1)

        def step(i, used):
            column = jnp.sum(jnp.where(iota((B, 2 * B), 1) == i, work[...], 0.0), axis=1, keepdims=True)
            size = jnp.where(used > 0.0, -1.0, jnp.abs(column))
            biggest = jnp.max(size)
            at = jnp.min(jnp.where(size == biggest, row1, B - 1))
            pivot_rows[i] = at
            line = jnp.sum(jnp.where(row1 == at, work[...], 0.0), axis=0, keepdims=True)
            line = line / jnp.sum(jnp.where(lane == i, line, 0.0))
            work[...] = jnp.where(row1 == at, line, work[...] - column * line)
            return jnp.where(row1 == at, 1.0, used)

        lax.fori_loop(0, B, step, jnp.zeros((B, 1), F32))

        def place(i, carry):
            line = jnp.sum(jnp.where(row1 == pivot_rows[i], work[:, B:], 0.0), axis=0, keepdims=True)
            out[...] = jnp.where(row1 == i, line, out[...])
            return carry

        lax.fori_loop(0, B, place, 0)


def corner_kernel(pos, a, b, other_a, other_b, own, factor, upper, inverses, work, pivot_rows):
    c = pos[4]
    half = S // 2
    first = pl.multiple_of(c * half, half)
    second = pl.multiple_of((1 - c) * half, half)
    factor[pl.ds(first, B), :] = a[...]
    factor[pl.ds(first + B, B), :] = b[...]
    factor[pl.ds(second, B), :] = other_a[...]
    factor[pl.ds(second + B, B), :] = other_b[...]
    upper[...] = own[...]
    for k in range(PANELS):
        here = slice(k * B, (k + 1) * B)
        later = slice((k + 1) * B, S)
        invert(factor[here, here], work, pivot_rows, inverses.at[k])
        if k + 1 < PANELS:
            lower = dot_full(factor[later, here], inverses[k])
            factor[later, here] = lower
            factor[later, later] = factor[later, later] - dot_full(lower, factor[here, later])
            upper[later, :] = upper[later, :] - dot_full(lower, upper[here, :])


def update_kernel(
    pos, order, width, pattern, target_row, raw, part0, part1, part2, part3,
    home_a, home_b, home_other_a, home_other_b, home_own, factor, upper, inverses,
    out, lower, final_homes,
):
    r = pos[0]
    q = pos[1]
    c = pos[4]
    half = S // 2
    natural_order(pos, (part0, part1, part2, part3), lower)
    first = pl.multiple_of(ROWS + c * half, half)
    second = pl.multiple_of(ROWS + (1 - c) * half, half)
    lower[pl.ds(first, B), :] = home_a[...]
    lower[pl.ds(first + B, B), :] = home_b[...]
    lower[pl.ds(second, B), :] = home_other_a[...]
    lower[pl.ds(second + B, B), :] = home_other_b[...]

    inverse_parts = [split2(inverses[k]) for k in range(PANELS)]
    factor_parts = [split2(factor[: k * B, k * B : (k + 1) * B]) for k in range(1, PANELS)]
    step_rows = 2 * B

    def solve(i, carry):
        here = pl.ds(pl.multiple_of(i * step_rows, step_rows), step_rows)
        for k in range(PANELS):
            value = lower[here, k * B : (k + 1) * B]
            if k:
                value = value - dot3(split2(lower[here, : k * B]), factor_parts[k - 1])
            lower[here, k * B : (k + 1) * B] = dot3(split2(value), inverse_parts[k])
        return carry

    lax.fori_loop(0, (ROWS + S) // step_rows, solve, 0)

    upper_parts = split2(upper[...])
    panel_of = []
    for s in range(2):
        found = jnp.int32(-1)
        for k in range(PANELS):
            found = jnp.where(order[k] == s * N_PCOL + q, k, found)
        panel_of.append(found)

    def finish(value, rows, s):
        at = pl.multiple_of(jnp.maximum(panel_of[s], 0) * B, B)
        return jnp.where(panel_of[s] >= 0, lower[rows, pl.ds(at, B)], value)

    for k in range(PANELS):
        rows = pl.ds(ROWS + k * B, B)
        here = slice(k * B, (k + 1) * B)
        value = home_own[here, :] - dot3(split2(lower[rows, :]), upper_parts)
        for s in range(2):
            final_homes[here, s * B : (s + 1) * B] = finish(value[:, s * B : (s + 1) * B], rows, s)
    home_parts = split3(final_homes[...])

    for t in range(BR):
        block_row = t * N_PROW + r
        rows = pl.ds(t * B, B)
        taken = dot3(split2(lower[rows, :]), upper_parts)
        hot = (iota((B, S), 0) + t * B) == target_row[...]
        hot = jnp.where(hot, 1.0, 0.0)
        replaced = jnp.max(hot, axis=1, keepdims=True) > 0.0
        hot = hot.astype(BF16)
        moved = dot_bf16(hot, home_parts[0]) + (dot_bf16(hot, home_parts[1]) + dot_bf16(hot, home_parts[2]))
        for s in range(2):
            block_col = s * N_PCOL + q
            cols = slice(s * B, (s + 1) * B)
            place = pl.ds(t * 2 * B + s, B, stride=2)
            value = kept(
                raw[place, :],
                pattern[block_row, block_col] > 0,
                width[block_row],
                width[block_col],
                block_row == block_col,
                0,
            )
            value = finish(value - taken[:, cols], rows, s)
            out[place, :] = jnp.where(replaced, moved[:, cols], value)
            for k in range(PANELS):

                @pl.when(order[k] == block_row)
                def _():
                    at = pl.multiple_of(jnp.maximum(panel_of[s], 0) * B, B)
                    here = slice(k * B, (k + 1) * B)
                    out[place, :] = jnp.where(panel_of[s] >= 0, factor[here, pl.ds(at, B)], upper[here, cols])


def call(kernel, smem, vmem, out_shapes, scratch):
    single = isinstance(out_shapes[0], int)
    shapes = [out_shapes] if single else list(out_shapes)
    in_specs = [pl.BlockSpec(memory_space=pltpu.SMEM)] * len(smem)
    in_specs += [pl.BlockSpec(memory_space=pltpu.VMEM)] * len(vmem)
    result = pl.pallas_call(
        kernel,
        out_shape=[jax.ShapeDtypeStruct(s, F32) for s in shapes],
        in_specs=in_specs,
        out_specs=[pl.BlockSpec(memory_space=pltpu.VMEM)] * len(shapes),
        scratch_shapes=scratch,
        compiler_params=pltpu.CompilerParams(vmem_limit_bytes=VMEM_LIMIT),
    )(*smem, *vmem)
    return result[0] if single else result


def shift(value, axis, size, by):
    return lax.ppermute(value, axis, [(i, (i + by) % size) for i in range(size)])


def merge_rows(mine, other):
    merged = mine + shift(other, "c", NC, 1)
    a = merged[:B]
    b = merged[B:]
    near = [(i, i ^ 1) for i in range(NY)]
    wrap = [(i, NY - 1 - i) for i in range(NY)]
    a = a + lax.ppermute(a, "y", near)
    b = b + lax.ppermute(b, "y", wrap)
    a = a + lax.ppermute(a, "y", wrap)
    b = b + lax.ppermute(b, "y", near)
    return a, b, shift(a, "c", NC, 1), shift(b, "c", NC, 1)


def body(matrix, node_width, block_pattern, pivot_row_targets, panel_order):
    z = lax.axis_index("z")
    x = lax.axis_index("x")
    c = lax.axis_index("c")
    r = lax.axis_index("y") * NC + c
    pos = jnp.stack([r, z * NX + x, z, x, c]).astype(jnp.int32)
    raw = matrix.reshape(ROWS * 2, B)
    targets = pivot_row_targets.reshape(-1)
    target_block = targets // B
    local = jnp.where(target_block % N_PROW == r, target_block // N_PROW * B + targets % B, -1)
    target_col = local.reshape(S, 1)
    target_row = local.reshape(1, S)

    spread = lax.all_to_all(raw.reshape(N_PCOL, CHUNK * 2, B), ("z", "x"), 0, 0)
    pivots, homes = call(
        own_rows_kernel,
        [pos, panel_order, node_width, block_pattern],
        [target_col, raw],
        [(S, 2 * B), (S, 2 * B)],
        [pltpu.VMEM((ROWS, 2 * B), F32)],
    )
    pivots, homes = lax.psum((pivots, homes), ("y", "c"))

    strip = call(
        select_kernel, [pos, panel_order, node_width, block_pattern], [spread], (CHUNK, S), []
    )
    strips = jnp.stack([strip] + [shift(strip, "z", NZ, s) for s in range(1, NZ)])
    parts = [strips] + [shift(strips, "x", NX, u) for u in range(1, NX)]

    mine, other, home_mine, home_other = call(
        panel_rows_kernel,
        [pos, panel_order],
        [target_col, *parts],
        [(S // 2, S)] * 4,
        [pltpu.VMEM((ROWS, S), F32), pltpu.VMEM((S, S), F32), pltpu.VMEM((S, S), F32)],
    )
    corner_rows = merge_rows(mine, other)
    home_rows = merge_rows(home_mine, home_other)
    factor, upper, inverses = call(
        corner_kernel,
        [pos],
        [*corner_rows, pivots],
        [(S, S), (S, 2 * B), (PANELS, B, B)],
        [pltpu.VMEM((B, 2 * B), F32), pltpu.SMEM((B,), jnp.int32)],
    )
    out = call(
        update_kernel,
        [pos, panel_order, node_width, block_pattern],
        [target_row, raw, *parts, *home_rows, homes, factor, upper, inverses],
        (ROWS * 2, B),
        [pltpu.VMEM((ROWS + S, S), F32), pltpu.VMEM((S, 2 * B), F32)],
    )
    return out.reshape(matrix.shape)


def solution(mesh):
    fine = Mesh(mesh.devices.reshape(NZ, NX, NY, NC), ("z", "x", "y", "c"))
    spec = P(None, ("y", "c"), None, None, ("z", "x"), None)
    return jax.shard_map(
        body,
        mesh=fine,
        in_specs=(spec, P(), P(), P(), P()),
        out_specs=spec,
        check_vma=False,
    )
```

time: 931 us -> 209 us (0.22)
  waiting for transfers between devices: 822 us -> 104 us
  starting transfers between devices: 0.52 us -> 48.3 us
  Pallas kernels: 0 us -> 31.7 us
  matrix products: 27.2 us -> 0 us
  local copies, waits for them, and re-layouts: 27.3 us -> 4.95 us
  other arithmetic: 21.8 us -> 5.24 us
  between operations: 27.5 us -> 13.6 us
    psum x8 -> x1, waiting for transfers between devices: 822 us -> 45.2 us  [body(): pivots, homes = lax.psum((pivots, homes), ('y', 'c'))]
    ppermute x0 -> x24, starting transfers between devices: none -> 36.4 us  [the longest x16 28 us: shift(): lax.ppermute(value, axis, [(i, (i + by) % size) for i in range(size)])]
    ppermute x0 -> x24, waiting for transfers between devices: none -> 32.6 us  [the longest x16 29.5 us: shift(): lax.ppermute(value, axis, [(i, (i + by) % size) for i in range(size)])]
    pallas_call x0 -> x5, Pallas kernels: none -> 31.7 us  [call(): pl.pallas_call(kernel, out_shape=[jax.ShapeDtypeStruct(s, F32) for s in s...]
    dot_general x72 -> x0, matrix products: 27.2 us -> none  [the longest x4 8.67 us: body(): jnp.einsum('tab,bsc->tasc', lower_factor, upper_rows, precision=highest_p...]
    all_to_all x0 -> x1, waiting for transfers between devices: none -> 26 us  [body(): spread = lax.all_to_all(raw.reshape(N_PCOL, CHUNK * 2, B), ('z', 'x'), 0, 0)]
    all_to_all x0 -> x1, starting transfers between devices: none -> 11.9 us  [body(): spread = lax.all_to_all(raw.reshape(N_PCOL, CHUNK * 2, B), ('z', 'x'), 0, 0)]
  transfers between devices with their start and end apart: 8 -> 26, of which waited for: 8 -> 13; matrix products, arithmetic and copies ran while one was open for 1% -> 4% of each run, Pallas kernels for 0% -> 6%
where the time goes in v1:
time: 209 us; the launch traced here: 208 us
  waiting for transfers between devices  104 us (50%)
  starting transfers between devices  48.3 us (23%)
  Pallas kernels  31.7 us (15%)
  between operations  13.6 us (7%)
  other arithmetic  5.24 us (3%)
  local copies, waits for them, and re-layouts  4.95 us (2%)
    psum x1, waiting for transfers between devices, body(): pivots, homes = lax.psum((pivots, homes), ('y', 'c'))  45.2 us
    pallas_call x5, Pallas kernels, call(): pl.pallas_call(kernel, out_shape=[jax.ShapeDtypeStruct(s, F32) for s in s...  31.7 us
    ppermute x16, waiting for transfers between devices, shift(): lax.ppermute(value, axis, [(i, (i + by) % size) for i in range(size)])  29.5 us
    ppermute x16, starting transfers between devices, shift(): lax.ppermute(value, axis, [(i, (i + by) % size) for i in range(size)])  28 us
    all_to_all x1, waiting for transfers between devices, body(): spread = lax.all_to_all(raw.reshape(N_PCOL, CHUNK * 2, B), ('z', 'x'), 0, 0)  26 us
    all_to_all x1, starting transfers between devices, body(): spread = lax.all_to_all(raw.reshape(N_PCOL, CHUNK * 2, B), ('z', 'x'), 0, 0)  11.9 us
  transfers between devices with their start and end apart: 26, of which 13 were waited for; matrix products, arithmetic and copies ran while one was open for 4% of the time, Pallas kernels for 6%

profile of v1, /device:TPU:1, one launch (start us, length us, event | category | flops | bytes accessed | tf_op | source)
XLA Modules:
  0.0 207.7 jit_solution(7444319317363287970)
XLA Ops:
  6.5 11.9 %all-to-all-start = ((f32[32,64,128]{2,1,0:T(8,128)}), f32[32,64,128]{2,1,0:T(8,128)S(1)}, u32[]{:S(2)}, u32[]{:S(2)}) async-start(f32[32,64,128]{2,1,0:T(8,128)} %bitcast.28), calls=%async_computation | async-start | bytes 2097152 | tf_op jit(solution)/shard_map/all_to_all | solution.py:342
  18.6 26.0 %all-to-all-done.spread = f32[32,64,128]{2,1,0:T(8,128)S(1)} async-done(((f32[32,64,128]{2,1,0:T(8,128)}), f32[32,64,128]{2,1,0:T(8,128)S(1)}, u32[]{:S(2)}, u32[]{:S(2)}) %all-to-all-start) | async-done | bytes 1048608 | tf_op jit(solution)/shard_map/all_to_all | solution.py:342
  46.4 2.4 %collective-permute-start.1 = (f32[32,512]{1,0:T(8,128)S(1)}, f32[32,512]{1,0:T(8,128)S(1)}, u32[]{:S(2)}, u32[]{:S(2)}) collective-permute-start(f32[32,512]{1,0:T(8,128)S(1)} %shard_map.55), channel_id=1, source_target_pairs={{0,64},{32,96},{64,128},{96,160},{128,192},{160,224},{192,0},{224,... | collective-permute-start | bytes 196616 | tf_op jit(solution)/shard_map/ppermute | solution.py:313
  48.8 2.0 collective-permute-start.2
  50.8 3.6 %collective-permute-start.3 = (f32[32,512]{1,0:T(8,128)S(1)}, f32[32,512]{1,0:T(8,128)S(1)}, u32[]{:S(2)}, u32[]{:S(2)}) collective-permute-start(f32[32,512]{1,0:T(8,128)S(1)} %shard_map.55), channel_id=1, source_target_pairs={{0,128},{32,160},{64,192},{96,224},{128,0},{160,32},{192,64},{224,... | collective-permute-start | bytes 196616 | tf_op jit(solution)/shard_map/ppermute | solution.py:313
  59.8 2.2 %collective-permute-done.5 = f32[32,512]{1,0:T(8,128)S(1)} collective-permute-done((f32[32,512]{1,0:T(8,128)S(1)}, f32[32,512]{1,0:T(8,128)S(1)}, u32[]{:S(2)}, u32[]{:S(2)}) %collective-permute-start.5) | collective-permute-done | bytes 65568 | tf_op jit(solution)/shard_map/ppermute | solution.py:313
  62.0 3.8 %collective-permute-done.6 = f32[32,512]{1,0:T(8,128)S(1)} collective-permute-done((f32[32,512]{1,0:T(8,128)S(1)}, f32[32,512]{1,0:T(8,128)S(1)}, u32[]{:S(2)}, u32[]{:S(2)}) %collective-permute-start.6) | collective-permute-done | bytes 65568 | tf_op jit(solution)/shard_map/ppermute | solution.py:313
  67.1 1.9 collective-permute-start.8
  71.1 7.7 %collective-permute-done.7.part1 = f32[8,32,512]{2,1,0:T(8,128)S(1)} collective-permute-done((f32[8,32,512]{2,1,0:T(8,128)S(1)}, f32[8,32,512]{2,1,0:T(8,128)S(1)}, u32[]{:S(2)}, u32[]{:S(2)}) %collective-permute-start.7) | collective-permute-done | bytes 524320 | tf_op jit(solution)/shard_map/ppermute | solution.py:313
  78.8 10.8 %collective-permute-done.8.part2 = f32[8,32,512]{2,1,0:T(8,128)S(1)} collective-permute-done((f32[8,32,512]{2,1,0:T(8,128)S(1)}, f32[8,32,512]{2,1,0:T(8,128)S(1)}, u32[]{:S(2)}, u32[]{:S(2)}) %collective-permute-start.8) | collective-permute-done | bytes 524320 | tf_op jit(solution)/shard_map/ppermute | solution.py:313
  89.6 2.1 %collective-permute-done.9.part3 = f32[8,32,512]{2,1,0:T(8,128)S(1)} collective-permute-done((f32[8,32,512]{2,1,0:T(8,128)S(1)}, f32[8,32,512]{2,1,0:T(8,128)S(1)}, u32[]{:S(2)}, u32[]{:S(2)}) %collective-permute-start.9) | collective-permute-done | bytes 524320 | tf_op jit(solution)/shard_map/ppermute | solution.py:313
  91.7 3.0 %shard_map.56 = (f32[256,512]{1,0:T(8,128)S(1)}, f32[256,512]{1,0:T(8,128)S(1)}, f32[256,512]{1,0:T(8,128)S(1)}, f32[256,512]{1,0:T(8,128)S(1)}) custom-call(s32[5]{0:T(128)S(1)} %stack.50.pos, s32[4]{0:T(128)S(1)} %copy-done.6, s32[512,1]{1,0:T(8,128)S(1)} %fusion.3.target_col, f32[8,32,512]{2,1,0:T(8,128)S(1)} %bitcast_dynamic-update-slice_fusion.part0, ...), custom_call_target="tpu_custom_call" | custom-call | tf_op jit(solution)/shard_map/pallas_call | solution.py:301
  100.3 1.9 collective-permute-start.20
  104.3 2.6 %shard_map.57 = (f32[512,256]{1,0:T(8,128)S(1)}, f32[512,256]{1,0:T(8,128)S(1)}) custom-call(s32[5]{0:T(128)S(1)} %stack.50.pos, s32[4]{0:T(128)S(1)} %copy-done.6, s32[64]{0:T(128)S(1)} %copy-done.7, s32[64,64]{1,0:T(8,128)S(1)} %copy-done.5, s32[512,1]{1,0:T(8,128)S(1)} %fusion.3.target_col, f32[2048,128]{1,0:T(8,128)S(1)} %bitcast.29), custom_call_target="tpu_custom_call" | custom-call | tf_op jit(solution)/shard_map/pallas_call | solution.py:301
  110.6 1.9 collective-permute-start.19
  112.5 2.2 %collective-permute-done.13 = f32[128,512]{1,0:T(8,128)} collective-permute-done((f32[128,512]{1,0:T(8,128)}, f32[128,512]{1,0:T(8,128)}, u32[]{:S(2)}, u32[]{:S(2)}) %collective-permute-start.13) | collective-permute-done | bytes 262176 | tf_op jit(solution)/shard_map/ppermute | solution.py:323
  115.8 2.0 collective-permute-start.12
  118.5 2.9 %collective-permute-start.23 = (f32[128,512]{1,0:T(8,128)}, f32[128,512]{1,0:T(8,128)}, u32[]{:S(2)}, u32[]{:S(2)}) collective-permute-start(f32[128,512]{1,0:T(8,128)} %add.148.b), channel_id=1, source_target_pairs={{0,1},{1,0},{2,3},{3,2},{4,5},{5,4},{6,7},{7,6},{8,9},{9,8},{10,11... | collective-permute-start | bytes 786440 | tf_op jit(solution)/shard_map/ppermute | solution.py:313
  122.2 2.0 collective-permute-start.22
  124.2 2.4 %collective-permute-start.16 = (f32[128,512]{1,0:T(8,128)S(1)}, f32[128,512]{1,0:T(8,128)}, u32[]{:S(2)}, u32[]{:S(2)}) collective-permute-start(f32[128,512]{1,0:T(8,128)S(1)} %add.143.home_b), channel_id=1, source_target_pairs={{0,1},{1,0},{2,3},{3,2},{4,5},{5,4},{6,7},{7,6},{8,9},{9,8},{10,11... | collective-permute-start | bytes 786440 | tf_op jit(solution)/shard_map/ppermute | solution.py:313
  127.7 1.8 collective-permute-start.15
  129.5 45.2 %all-reduce.3.cloned.1.call-done = (f32[512,256]{1,0:T(8,128)}, f32[512,256]{1,0:T(8,128)}) async-done(((f32[512,256]{1,0:T(8,128)}, f32[512,256]{1,0:T(8,128)}), (f32[512,256]{1,0:T(8,128)}, f32[512,256]{1,0:T(8,128)})) %all-reduce.3.cloned.1.call-update) | async-done | bytes 1048592 | tf_op jit(solution)/shard_map/psum | solution.py:350
  175.8 9.1 %shard_map.58 = (f32[512,512]{1,0:T(8,128)S(1)}, f32[512,256]{1,0:T(8,128)S(1)}, f32[4,128,128]{2,1,0:T(8,128)S(1)}) custom-call(s32[5]{0:T(128)S(1)} %stack.50.pos, f32[128,512]{1,0:T(8,128)} %add.146.a, f32[128,512]{1,0:T(8,128)} %add.148.b, f32[128,512]{1,0:T(8,128)} %collective-permute-done.22.other_a, f32[128,512]{1,0:T(8,128)} %collective-permute-done.23.other_b, ...), custom_call_target="tpu_custom_call" | custom-call | tf_op jit(solution)/shard_map/pallas_call | solution.py:301
  184.9 15.9 %shard_map.59 = f32[2048,128]{1,0:T(8,128)} custom-call(s32[5]{0:T(128)S(1)} %stack.50.pos, s32[4]{0:T(128)S(1)} %copy-done.6, s32[64]{0:T(128)S(1)} %copy-done.7, s32[64,64]{1,0:T(8,128)S(1)} %copy-done.5, s32[1,512]{1,0:T(1,128)S(1)} %compare_select_fusion.target_row, f32[2048,128]{1,0:T(8,128)S(1)} %bitcast.30, ...), custom_call_target="tpu_custom_call" | custom-call | tf_op jit(solution)/shard_map/pallas_call | solution.py:301
  (80 shorter events, 26.8 us)
Async XLA Ops:
  6.5 38.1 %all-to-all-start = ((f32[32,64,128]{2,1,0:T(8,128)}), f32[32,64,128]{2,1,0:T(8,128)S(1)}, u32[]{:S(2)}, u32[]{:S(2)}) async-start(f32[32,64,128]{2,1,0:T(8,128)} %bitcast.28), calls=%async_computation | async-start | bytes 2097152 | tf_op jit(solution)/shard_map/all_to_all | solution.py:342
  18.4 156.3 %all-reduce.3.cloned.1.call-start = ((), (), s32[]{:S(2)}) async-start(), calls=%async_computation.1 | async-start | bytes 2097152 | tf_op jit(solution)/shard_map/psum | solution.py:350
  45.8 9.3 %collective-permute-start = (f32[32,512]{1,0:T(8,128)S(1)}, f32[32,512]{1,0:T(8,128)S(1)}, u32[]{:S(2)}, u32[]{:S(2)}) collective-permute-start(f32[32,512]{1,0:T(8,128)S(1)} %shard_map.55), channel_id=1, source_target_pairs={{0,32},{32,64},{64,96},{96,128},{128,160},{160,192},{192,224},{224... | collective-permute-start | bytes 196616 | tf_op jit(solution)/shard_map/ppermute | solution.py:313
  46.4 10.4 %collective-permute-start.1 = (f32[32,512]{1,0:T(8,128)S(1)}, f32[32,512]{1,0:T(8,128)S(1)}, u32[]{:S(2)}, u32[]{:S(2)}) collective-permute-start(f32[32,512]{1,0:T(8,128)S(1)} %shard_map.55), channel_id=1, source_target_pairs={{0,64},{32,96},{64,128},{96,160},{128,192},{160,224},{192,0},{224,... | collective-permute-start | bytes 196616 | tf_op jit(solution)/shard_map/ppermute | solution.py:313
  48.8 9.3 %collective-permute-start.2 = (f32[32,512]{1,0:T(8,128)S(1)}, f32[32,512]{1,0:T(8,128)S(1)}, u32[]{:S(2)}, u32[]{:S(2)}) collective-permute-start(f32[32,512]{1,0:T(8,128)S(1)} %shard_map.55), channel_id=1, source_target_pairs={{0,96},{32,128},{64,160},{96,192},{128,224},{160,0},{192,32},{224,... | collective-permute-start | bytes 196616 | tf_op jit(solution)/shard_map/ppermute | solution.py:313
  50.8 8.4 %collective-permute-start.3 = (f32[32,512]{1,0:T(8,128)S(1)}, f32[32,512]{1,0:T(8,128)S(1)}, u32[]{:S(2)}, u32[]{:S(2)}) collective-permute-start(f32[32,512]{1,0:T(8,128)S(1)} %shard_map.55), channel_id=1, source_target_pairs={{0,128},{32,160},{64,192},{96,224},{128,0},{160,32},{192,64},{224,... | collective-permute-start | bytes 196616 | tf_op jit(solution)/shard_map/ppermute | solution.py:313
  55.1 6.9 %collective-permute-start.5 = (f32[32,512]{1,0:T(8,128)S(1)}, f32[32,512]{1,0:T(8,128)S(1)}, u32[]{:S(2)}, u32[]{:S(2)}) collective-permute-start(f32[32,512]{1,0:T(8,128)S(1)} %shard_map.55), channel_id=1, source_target_pairs={{0,192},{32,224},{64,0},{96,32},{128,64},{160,96},{192,128},{224,1... | collective-permute-start | bytes 196616 | tf_op jit(solution)/shard_map/ppermute | solution.py:313
  56.8 9.0 %collective-permute-start.6 = (f32[32,512]{1,0:T(8,128)S(1)}, f32[32,512]{1,0:T(8,128)S(1)}, u32[]{:S(2)}, u32[]{:S(2)}) collective-permute-start(f32[32,512]{1,0:T(8,128)S(1)} %shard_map.55), channel_id=1, source_target_pairs={{0,224},{32,0},{64,32},{96,64},{128,96},{160,128},{192,160},{224,1... | collective-permute-start | bytes 196616 | tf_op jit(solution)/shard_map/ppermute | solution.py:313
  65.8 13.0 %collective-permute-start.7 = (f32[8,32,512]{2,1,0:T(8,128)S(1)}, f32[8,32,512]{2,1,0:T(8,128)S(1)}, u32[]{:S(2)}, u32[]{:S(2)}) collective-permute-start(f32[8,32,512]{2,1,0:T(8,128)S(1)} %bitcast_dynamic-update-slice_fusion.part0), channel_id=1, source_target_pairs={{0,8},{8,16},{16,24},{24,0},{1,9},{9,17},{17,25},{25,1},{2,10},{10... | collective-permute-start | bytes 1572872 | tf_op jit(solution)/shard_map/ppermute | solution.py:313
  67.1 22.5 %collective-permute-start.8 = (f32[8,32,512]{2,1,0:T(8,128)S(1)}, f32[8,32,512]{2,1,0:T(8,128)S(1)}, u32[]{:S(2)}, u32[]{:S(2)}) collective-permute-start(f32[8,32,512]{2,1,0:T(8,128)S(1)} %bitcast_dynamic-update-slice_fusion.part0), channel_id=1, source_target_pairs={{0,16},{8,24},{16,0},{24,8},{1,17},{9,25},{17,1},{25,9},{2,18},{10... | collective-permute-start | bytes 1572872 | tf_op jit(solution)/shard_map/ppermute | solution.py:313
  69.0 22.7 %collective-permute-start.9 = (f32[8,32,512]{2,1,0:T(8,128)S(1)}, f32[8,32,512]{2,1,0:T(8,128)S(1)}, u32[]{:S(2)}, u32[]{:S(2)}) collective-permute-start(f32[8,32,512]{2,1,0:T(8,128)S(1)} %bitcast_dynamic-update-slice_fusion.part0), channel_id=1, source_target_pairs={{0,24},{8,0},{16,8},{24,16},{1,25},{9,1},{17,9},{25,17},{2,26},{10... | collective-permute-start | bytes 1572872 | tf_op jit(solution)/shard_map/ppermute | solution.py:313
  96.4 5.9 %collective-permute-start.10 = (f32[256,512]{1,0:T(8,128)S(1)}, f32[256,512]{1,0:T(8,128)S(1)}, u32[]{:S(2)}, u32[]{:S(2)}) collective-permute-start(f32[256,512]{1,0:T(8,128)S(1)} %get-tuple-element.15), channel_id=1, source_target_pairs={{0,1},{1,0},{2,3},{3,2},{4,5},{5,4},{6,7},{7,6},{8,9},{9,8},{10,11... | collective-permute-start | bytes 1572872 | tf_op jit(solution)/shard_map/ppermute | solution.py:313
  99.0 9.5 %collective-permute-start.18 = (f32[128,512]{1,0:T(8,128)}, f32[128,512]{1,0:T(8,128)}, u32[]{:S(2)}, u32[]{:S(2)}) collective-permute-start(f32[128,512]{1,0:T(8,128)} %get-tuple-element.28), channel_id=1, source_target_pairs={{0,2},{2,0},{4,6},{6,4},{1,3},{3,1},{5,7},{7,5},{8,10},{10,8},{12,... | collective-permute-start | bytes 786440 | tf_op jit(solution)/shard_map/ppermute | solution.py:322
  100.3 8.7 %collective-permute-start.20 = (f32[128,512]{1,0:T(8,128)}, f32[128,512]{1,0:T(8,128)}, u32[]{:S(2)}, u32[]{:S(2)}) collective-permute-start(f32[128,512]{1,0:T(8,128)} %get-tuple-element.27), channel_id=1, source_target_pairs={{0,6},{2,4},{4,2},{6,0},{1,7},{3,5},{5,3},{7,1},{8,14},{10,12},{12... | collective-permute-start | bytes 786440 | tf_op jit(solution)/shard_map/ppermute | solution.py:323
  103.3 9.2 %collective-permute-start.11 = (f32[128,512]{1,0:T(8,128)}, f32[128,512]{1,0:T(8,128)S(1)}, u32[]{:S(2)}, u32[]{:S(2)}) collective-permute-start(f32[128,512]{1,0:T(8,128)} %get-tuple-element.32), channel_id=1, source_target_pairs={{0,2},{2,0},{4,6},{6,4},{1,3},{3,1},{5,7},{7,5},{8,10},{10,8},{12,... | collective-permute-start | bytes 786440 | tf_op jit(solution)/shard_map/ppermute | solution.py:322
  103.7 11.0 %collective-permute-start.13 = (f32[128,512]{1,0:T(8,128)}, f32[128,512]{1,0:T(8,128)}, u32[]{:S(2)}, u32[]{:S(2)}) collective-permute-start(f32[128,512]{1,0:T(8,128)} %get-tuple-element.31), channel_id=1, source_target_pairs={{0,6},{2,4},{4,2},{6,0},{1,7},{3,5},{5,3},{7,1},{8,14},{10,12},{12... | collective-permute-start | bytes 786440 | tf_op jit(solution)/shard_map/ppermute | solution.py:323
  110.3 7.5 %collective-permute-start.21 = (f32[128,512]{1,0:T(8,128)S(1)}, f32[128,512]{1,0:T(8,128)S(1)}, u32[]{:S(2)}, u32[]{:S(2)}) collective-permute-start(f32[128,512]{1,0:T(8,128)S(1)} %get-tuple-element.25), channel_id=1, source_target_pairs={{0,2},{2,0},{4,6},{6,4},{1,3},{3,1},{5,7},{7,5},{8,10},{10,8},{12,... | collective-permute-start | bytes 786440 | tf_op jit(solution)/shard_map/ppermute | solution.py:325
  110.6 10.9 %collective-permute-start.19 = (f32[128,512]{1,0:T(8,128)S(1)}, f32[128,512]{1,0:T(8,128)S(1)}, u32[]{:S(2)}, u32[]{:S(2)}) collective-permute-start(f32[128,512]{1,0:T(8,128)S(1)} %get-tuple-element.26), channel_id=1, source_target_pairs={{0,6},{2,4},{4,2},{6,0},{1,7},{3,5},{5,3},{7,1},{8,14},{10,12},{12... | collective-permute-start | bytes 786440 | tf_op jit(solution)/shard_map/ppermute | solution.py:324
  115.7 8.5 %collective-permute-start.14 = (f32[128,512]{1,0:T(8,128)S(1)}, f32[128,512]{1,0:T(8,128)S(1)}, u32[]{:S(2)}, u32[]{:S(2)}) collective-permute-start(f32[128,512]{1,0:T(8,128)S(1)} %get-tuple-element.29), channel_id=1, source_target_pairs={{0,2},{2,0},{4,6},{6,4},{1,3},{3,1},{5,7},{7,5},{8,10},{10,8},{12,... | collective-permute-start | bytes 786440 | tf_op jit(solution)/shard_map/ppermute | solution.py:325
  115.8 11.2 %collective-permute-start.12 = (f32[128,512]{1,0:T(8,128)S(1)}, f32[128,512]{1,0:T(8,128)S(1)}, u32[]{:S(2)}, u32[]{:S(2)}) collective-permute-start(f32[128,512]{1,0:T(8,128)S(1)} %get-tuple-element.30), channel_id=1, source_target_pairs={{0,6},{2,4},{4,2},{6,0},{1,7},{3,5},{5,3},{7,1},{8,14},{10,12},{12... | collective-permute-start | bytes 786440 | tf_op jit(solution)/shard_map/ppermute | solution.py:324
  118.5 56.2 %collective-permute-start.23 = (f32[128,512]{1,0:T(8,128)}, f32[128,512]{1,0:T(8,128)}, u32[]{:S(2)}, u32[]{:S(2)}) collective-permute-start(f32[128,512]{1,0:T(8,128)} %add.148.b), channel_id=1, source_target_pairs={{0,1},{1,0},{2,3},{3,2},{4,5},{5,4},{6,7},{7,6},{8,9},{9,8},{10,11... | collective-permute-start | bytes 786440 | tf_op jit(solution)/shard_map/ppermute | solution.py:313
  122.2 52.6 %collective-permute-start.22 = (f32[128,512]{1,0:T(8,128)}, f32[128,512]{1,0:T(8,128)}, u32[]{:S(2)}, u32[]{:S(2)}) collective-permute-start(f32[128,512]{1,0:T(8,128)} %add.146.a), channel_id=1, source_target_pairs={{0,1},{1,0},{2,3},{3,2},{4,5},{5,4},{6,7},{7,6},{8,9},{9,8},{10,11... | collective-permute-start | bytes 786440 | tf_op jit(solution)/shard_map/ppermute | solution.py:313
  124.2 60.7 %collective-permute-start.16 = (f32[128,512]{1,0:T(8,128)S(1)}, f32[128,512]{1,0:T(8,128)}, u32[]{:S(2)}, u32[]{:S(2)}) collective-permute-start(f32[128,512]{1,0:T(8,128)S(1)} %add.143.home_b), channel_id=1, source_target_pairs={{0,1},{1,0},{2,3},{3,2},{4,5},{5,4},{6,7},{7,6},{8,9},{9,8},{10,11... | collective-permute-start | bytes 786440 | tf_op jit(solution)/shard_map/ppermute | solution.py:313
  127.7 57.2 %collective-permute-start.15 = (f32[128,512]{1,0:T(8,128)}, f32[128,512]{1,0:T(8,128)}, u32[]{:S(2)}, u32[]{:S(2)}) collective-permute-start(f32[128,512]{1,0:T(8,128)} %add.141.home_a), channel_id=1, source_target_pairs={{0,1},{1,0},{2,3},{3,2},{4,5},{5,4},{6,7},{7,6},{8,9},{9,8},{10,11... | collective-permute-start | bytes 786440 | tf_op jit(solution)/shard_map/ppermute | solution.py:313
  (14 other events, 113.7 us)
Sparse Core Ops, SparseCore 0:
  108.6 66.0 all-reduce.2

commit v2 on v1

v2 whole, which is shorter than its diff:
```python
import jax
import jax.numpy as jnp
from jax import lax
from jax.experimental import pallas as pl
from jax.experimental.pallas import tpu as pltpu
from jax.sharding import Mesh, PartitionSpec as P

B = 128
PANELS = 4
S = PANELS * B
BR = 8
N_PROW = 8
N_PCOL = 32
NZ, NX, NY, NC = 8, 4, 4, 2
ROWS = BR * B
CHUNK = ROWS // N_PCOL
VMEM_LIMIT = 40 * 1024 * 1024
HIGHEST = lax.Precision.HIGHEST
F32 = jnp.float32
BF16 = jnp.bfloat16


def iota(shape, dim):
    return lax.broadcasted_iota(jnp.int32, shape, dim)


def dot_full(a, b):
    return jnp.dot(a, b, precision=HIGHEST, preferred_element_type=F32)


def dot_bf16(a, b):
    return jnp.dot(a, b, preferred_element_type=F32)


def split2(v):
    high = v.astype(BF16)
    low = (v - high.astype(F32)).astype(BF16)
    return high, low


def split3(v):
    high = v.astype(BF16)
    rest = v - high.astype(F32)
    middle = rest.astype(BF16)
    low = (rest - middle.astype(F32)).astype(BF16)
    return high, middle, low


def dot3(a, b):
    return dot_bf16(a[0], b[0]) + (dot_bf16(a[0], b[1]) + dot_bf16(a[1], b[0]))


def kept(value, here, row_width, col_width, same_block, row_start):
    rows = iota(value.shape, 0) + row_start
    cols = iota(value.shape, 1)
    value = jnp.where(here & (rows < row_width) & (cols < col_width), value, 0.0)
    return jnp.where(same_block & (rows == cols) & (rows >= row_width), 1.0, value)


def own_rows_kernel(pos, order, width, pattern, target_col, target_row, raw, keep, give, rows):
    r = pos[0]
    q = pos[1]
    c = pos[4]
    y = lax.div(r, NC)
    for t in range(BR):
        block_row = t * N_PROW + r
        for s in range(2):
            block_col = s * N_PCOL + q
            rows[t * B : (t + 1) * B, s * B : (s + 1) * B] = kept(
                raw[pl.ds(t * 2 * B + s, B, stride=2), :],
                pattern[block_row, block_col] > 0,
                width[block_row],
                width[block_col],
                block_row == block_col,
                0,
            )
    part = S // N_PROW
    high, middle, low = split3(rows[...])
    lane = iota((B, ROWS), 1)
    row_id = ((lane // B) * N_PROW + r) * B + lane % B
    for i in range(0, S, B):
        hot = jnp.where(row_id == target_col[i : i + B, :], 1.0, 0.0).astype(BF16)
        picked = dot_bf16(hot, high) + (dot_bf16(hot, middle) + dot_bf16(hot, low))
        place = lax.rem(i // B - y + NY, NY)
        keep[place, :part, :] = jnp.where(c == 0, picked[:part], picked[part:])
        give[place, :part, :] = jnp.where(c == 0, picked[part:], picked[:part])
    for k in range(PANELS):
        p = order[k]
        here = (p % N_PROW) == r
        block = rows[pl.ds(pl.multiple_of((p // N_PROW) * B, B), B), :]
        block = jnp.where(here, block, 0.0)
        place = lax.rem(k - y + NY, NY)
        keep[place, part:, :] = jnp.where(c == 0, block[:part], block[part:])
        give[place, part:, :] = jnp.where(c == 0, block[part:], block[:part])
    for t in range(BR):
        here = slice(t * B, (t + 1) * B)
        taken = is_target(target_row, B, (t * N_PROW + r) * B)
        rows[here, :] = jnp.where(taken, 0.0, rows[here, :])


def is_target(target_row, count, start):
    hot = jnp.where(iota((count, S), 0) + start == target_row[...], 1.0, 0.0)
    return jnp.max(hot, axis=1, keepdims=True) > 0.0


def add_kernel(keep, received, *sums):
    for u in range(NY):
        sums[u][...] = keep[u] + received[u]


def sum_kernel(part0, part1, part2, part3, total, packed):
    value = (part0[...] + part1[...]) + (part2[...] + part3[...])
    total[...] = value
    for s in range(2):
        for i in range(4):
            packed[pl.ds(s * 4 + i, N_PCOL, stride=8), :] = value[
                i * N_PCOL : (i + 1) * N_PCOL, s * B : (s + 1) * B
            ]


def select_few_kernel(order, spread, out):
    pieces = []
    for k in range(PANELS):
        p = order[k]
        block = spread[p % N_PCOL]
        pieces.append(jnp.where(p >= N_PCOL, block[4:], block[:4]))
    value = jnp.concatenate(pieces, axis=0)
    for j in range(N_PCOL):
        out[j] = value


def arrange_kernel(gathered, total, pivots, homes):
    for i in range(2):
        here = slice(i * N_PCOL, (i + 1) * N_PCOL)
        for k in range(PANELS):
            cols = slice(k * B, (k + 1) * B)
            pivots[here, cols] = gathered[pl.ds(k * 4 + i, N_PCOL, stride=16), :]
            homes[here, cols] = gathered[pl.ds(k * 4 + i + 2, N_PCOL, stride=16), :]
    half = S // N_PROW
    pivots[:, S:] = total[:half]
    homes[:, S:] = total[half:]


def select_kernel(pos, order, width, pattern, target_row, spread, out):
    r = pos[0]
    z = pos[2]
    x = pos[3]
    block_row = z * N_PROW + r
    taken = is_target(target_row, CHUNK, block_row * B + x * CHUNK)
    for k in range(PANELS):
        p = order[k]
        source = p % N_PCOL
        value = jnp.where(
            p >= N_PCOL,
            spread[source, pl.ds(1, CHUNK, stride=2), :],
            spread[source, pl.ds(0, CHUNK, stride=2), :],
        )
        value = kept(
            value, pattern[block_row, p] > 0, width[block_row], width[p], block_row == p, x * CHUNK
        )
        out[:, k * B : (k + 1) * B] = jnp.where(taken, 0.0, value)


def natural_order(pos, pairs, out, columns):
    c = pos[4]
    y = lax.div(pos[0], NC)
    part = S // N_PROW
    for u in range(NY):
        other_y = lax.rem(y - u + NY, NY)
        for i in range(NC):
            core = c if i == 0 else 1 - c
            start = pl.multiple_of((other_y * NC + core) * part, part)
            out[pl.ds(start, part), :] = pairs[u][i, :, columns]


def invert(corner, work, pivot_rows, out):
    row = iota((B, B), 0)
    col = iota((B, B), 1)
    eye = jnp.where(row == col, 1.0, 0.0)
    diagonal = jnp.where(row == col, corner, 0.0)
    by_col = 1.0 / jnp.sum(diagonal, axis=0, keepdims=True)
    by_row = 1.0 / jnp.sum(diagonal, axis=1, keepdims=True)
    residual = eye - corner * by_col
    approx = by_row * (eye + residual)

    def sweep(state):
        count, error, approx = state
        residual = eye - dot_full(corner, approx)
        return count + 1, jnp.max(jnp.abs(residual)), approx + dot_full(approx, residual)

    def again(state):
        count, error, approx = state
        return (count < 16) & jnp.logical_not(error < 1e-5)

    count, error, approx = lax.while_loop(again, sweep, (0, jnp.float32(1.0), approx))
    out[...] = approx

    @pl.when(jnp.logical_not(error < 1e-5))
    def _():
        work[:, :B] = corner
        work[:, B:] = eye
        row1 = iota((B, 1), 0)
        lane = iota((1, 2 * B), 1)

        def step(i, used):
            column = jnp.sum(jnp.where(iota((B, 2 * B), 1) == i, work[...], 0.0), axis=1, keepdims=True)
            size = jnp.where(used > 0.0, -1.0, jnp.abs(column))
            biggest = jnp.max(size)
            at = jnp.min(jnp.where(size == biggest, row1, B - 1))
            pivot_rows[i] = at
            line = jnp.sum(jnp.where(row1 == at, work[...], 0.0), axis=0, keepdims=True)
            line = line / jnp.sum(jnp.where(lane == i, line, 0.0))
            work[...] = jnp.where(row1 == at, line, work[...] - column * line)
            return jnp.where(row1 == at, 1.0, used)

        lax.fori_loop(0, B, step, jnp.zeros((B, 1), F32))

        def place(i, carry):
            line = jnp.sum(jnp.where(row1 == pivot_rows[i], work[:, B:], 0.0), axis=0, keepdims=True)
            out[...] = jnp.where(row1 == i, line, out[...])
            return carry

        lax.fori_loop(0, B, place, 0)


def corner_kernel(
    pos, pair0, pair1, pair2, pair3,
    factor, upper, solve_high, solve_low, upper_high, upper_low, inverses, work, solver, pivot_rows,
):
    pairs = (pair0, pair1, pair2, pair3)
    natural_order(pos, pairs, factor, slice(0, S))
    natural_order(pos, pairs, upper, slice(S, S + 2 * B))
    solver[...] = jnp.zeros((S, S), F32)
    for k in range(PANELS):
        here = slice(k * B, (k + 1) * B)
        later = slice((k + 1) * B, S)
        before = slice(0, k * B)
        invert(factor[here, here], work, pivot_rows, inverses)
        inverse = inverses[...]
        solver[here, here] = inverse
        if k + 1 < PANELS:
            lower = dot_full(factor[later, here], inverse)
            factor[later, here] = lower
            factor[later, later] = factor[later, later] - dot_full(lower, factor[here, later])
            upper[later, :] = upper[later, :] - dot_full(lower, upper[here, :])
        if k:
            solver[before, here] = -dot_full(dot_full(solver[before, before], factor[before, here]), inverse)
    high, low = split2(solver[...])
    solve_high[...] = high
    solve_low[...] = low
    high, low = split2(upper[...])
    upper_high[...] = high
    upper_low[...] = low


def update_kernel(
    pos, order, target_row, rows, part0, part1, part2, part3, pair0, pair1, pair2, pair3,
    factor, upper, solve_high, solve_low, upper_high, upper_low,
    out, lower, taken, home_rows, homes,
):
    r = pos[0]
    q = pos[1]
    z = pos[2]
    x = pos[3]
    half = S // 2
    upper_parts = (upper_high[...], upper_low[...])
    solve_first = (solve_high[:half, :half], solve_low[:half, :half])
    solve_second = (solve_high[:, half:], solve_low[:, half:])
    pairs = (pair0, pair1, pair2, pair3)
    natural_order(pos, pairs, home_rows, slice(0, S))
    natural_order(pos, pairs, homes, slice(S, S + 2 * B))

    panel_of = []
    for s in range(2):
        found = jnp.int32(-1)
        for k in range(PANELS):
            found = jnp.where(order[k] == s * N_PCOL + q, k, found)
        panel_of.append(found)

    def solve(value):
        high, low = split2(value)
        first = dot3((high[:, :half], low[:, :half]), solve_first)
        second = dot3((high, low), solve_second)
        value = jnp.concatenate([first, second], axis=1)
        return value, dot3(split2(value), upper_parts)

    for i in range(2):
        here = slice(i * half, (i + 1) * half)
        value, product = solve(home_rows[here, :])
        home_rows[here, :] = value
        homes[here, :] = homes[here, :] - product
    for u, part in enumerate((part0, part1, part2, part3)):
        value, product = solve(part[...].reshape(NZ * CHUNK, S))
        other_x = lax.rem(x - u + NX, NX)
        for i in range(NZ):
            t = lax.rem(z - i + NZ, NZ)
            place = pl.ds(pl.multiple_of(t * B + other_x * CHUNK, CHUNK), CHUNK)
            lower[place, :] = value[i * CHUNK : (i + 1) * CHUNK]
            taken[place, :] = product[i * CHUNK : (i + 1) * CHUNK]

    for s in range(2):
        cols = slice(s * B, (s + 1) * B)

        @pl.when(panel_of[s] >= 0)
        def _():
            at = pl.ds(pl.multiple_of(panel_of[s] * B, B), B)
            homes[:, cols] = home_rows[:, at]
            taken[:, cols] = -lower[:, at]

    home_parts = split3(homes[...])
    for t in range(BR):
        block_row = t * N_PROW + r
        here = slice(t * B, (t + 1) * B)
        hot = (iota((B, S), 0) + block_row * B) == target_row[...]
        hot = jnp.where(hot, 1.0, 0.0).astype(BF16)
        moved = dot_bf16(hot, home_parts[0]) + (dot_bf16(hot, home_parts[1]) + dot_bf16(hot, home_parts[2]))
        for s in range(2):
            cols = slice(s * B, (s + 1) * B)
            value = jnp.where(panel_of[s] >= 0, 0.0, rows[here, cols])
            out[pl.ds(t * 2 * B + s, B, stride=2), :] = (value - taken[here, cols]) + moved[:, cols]

    for k in range(PANELS):

        @pl.when(lax.rem(order[k], N_PROW) == r)
        def _():
            t = lax.div(order[k], N_PROW)
            here = slice(k * B, (k + 1) * B)
            for s in range(2):
                at = pl.multiple_of(jnp.maximum(panel_of[s], 0) * B, B)
                value = jnp.where(
                    panel_of[s] >= 0, factor[here, pl.ds(at, B)], upper[here, s * B : (s + 1) * B]
                )
                out[pl.ds(t * 2 * B + s, B, stride=2), :] = value


def call(kernel, smem, vmem, out_shapes, scratch):
    in_specs = [pl.BlockSpec(memory_space=pltpu.SMEM)] * len(smem)
    in_specs += [pl.BlockSpec(memory_space=pltpu.VMEM)] * len(vmem)
    return pl.pallas_call(
        kernel,
        out_shape=[jax.ShapeDtypeStruct(shape, kind) for kind, shape in out_shapes],
        in_specs=in_specs,
        out_specs=[pl.BlockSpec(memory_space=pltpu.VMEM)] * len(out_shapes),
        scratch_shapes=scratch,
        compiler_params=pltpu.CompilerParams(vmem_limit_bytes=VMEM_LIMIT),
    )(*smem, *vmem)


def shift(value, axis, size, by):
    return lax.ppermute(value, axis, [(i, (i + by) % size) for i in range(size)])


def gather_pairs(value):
    pair = jnp.stack([value, shift(value, "c", NC, 1)])
    return [pair] + [shift(pair, "y", NY, u) for u in range(1, NY)]


def body(matrix, node_width, block_pattern, pivot_row_targets, panel_order):
    z = lax.axis_index("z")
    x = lax.axis_index("x")
    c = lax.axis_index("c")
    r = lax.axis_index("y") * NC + c
    pos = jnp.stack([r, z * NX + x, z, x, c]).astype(jnp.int32)
    raw = matrix.reshape(ROWS * 2, B)
    target_col = pivot_row_targets.reshape(S, 1)
    target_row = pivot_row_targets.reshape(1, S)
    where = [pos, panel_order, node_width, block_pattern]
    part = S // N_PROW

    spread = lax.all_to_all(raw.reshape(N_PCOL, CHUNK * 2, B), ("z", "x"), 0, 0)
    keep, give, rows = call(
        own_rows_kernel,
        where,
        [target_col, target_row, raw],
        [(F32, (NY, 2 * part, 2 * B)), (F32, (NY, 2 * part, 2 * B)), (F32, (ROWS, 2 * B))],
        [],
    )
    sums = call(
        add_kernel, [], [keep, shift(give, "c", NC, 1)], [(F32, (2 * part, 2 * B))] * NY, []
    )
    sums = [sums[0]] + [shift(sums[u], "y", NY, u) for u in range(1, NY)]
    total, packed = call(
        sum_kernel, [], sums, [(F32, (2 * part, 2 * B)), (F32, (N_PCOL * 8, B))], []
    )
    spread, packed = lax.optimization_barrier((spread, packed))
    few = lax.all_to_all(packed.reshape(N_PCOL, 8, B), ("z", "x"), 0, 0)
    (few,) = call(select_few_kernel, [panel_order], [few], [(F32, (N_PCOL, 16, B))], [])
    few = lax.all_to_all(few, ("z", "x"), 0, 0)
    pivots, homes = call(
        arrange_kernel, [], [few.reshape(N_PCOL * 16, B), total], [(F32, (part, S + 2 * B))] * 2, []
    )
    pivots = gather_pairs(pivots)
    homes = gather_pairs(homes)
    solved = call(
        corner_kernel,
        [pos],
        pivots,
        [(F32, (S, S)), (F32, (S, 2 * B)), (BF16, (S, S)), (BF16, (S, S)), (BF16, (S, 2 * B)), (BF16, (S, 2 * B))],
        [
            pltpu.VMEM((B, B), F32),
            pltpu.VMEM((B, 2 * B), F32),
            pltpu.VMEM((S, S), F32),
            pltpu.SMEM((B,), jnp.int32),
        ],
    )

    (strip,) = call(select_kernel, where, [target_row, spread], [(F32, (CHUNK, S))], [])
    strips = jnp.stack([strip] + [shift(strip, "z", NZ, i) for i in range(1, NZ)])
    parts = [strips] + [shift(strips, "x", NX, u) for u in range(1, NX)]
    (out,) = call(
        update_kernel,
        [pos, panel_order],
        [target_row, rows, *parts, *homes, *solved],
        [(F32, (ROWS * 2, B))],
        [
            pltpu.VMEM((ROWS, S), F32),
            pltpu.VMEM((ROWS, 2 * B), F32),
            pltpu.VMEM((S, S), F32),
            pltpu.VMEM((S, 2 * B), F32),
        ],
    )
    return out.reshape(matrix.shape)


def solution(mesh):
    fine = Mesh(mesh.devices.reshape(NZ, NX, NY, NC), ("z", "x", "y", "c"))
    spec = P(None, ("y", "c"), None, None, ("z", "x"), None)
    return jax.shard_map(
        body,
        mesh=fine,
        in_specs=(spec, P(), P(), P(), P()),
        out_specs=spec,
        check_vma=False,
    )
```

time: 209 us -> 134 us (0.64)
  waiting for transfers between devices: 104 us -> 46.2 us
  between operations: 13.6 us -> 0.22 us
  starting transfers between devices: 48.3 us -> 61 us
  Pallas kernels: 31.7 us -> 23.4 us
  other arithmetic: 5.24 us -> 0.05 us
  local copies, waits for them, and re-layouts: 4.95 us -> 1.63 us
    psum x1 -> x0, waiting for transfers between devices: 45.2 us -> none  [body(): pivots, homes = lax.psum((pivots, homes), ('y', 'c'))]
    all_to_all x1, waiting for transfers between devices: 26 us -> 8.53 us  [body(): spread = lax.all_to_all(raw.reshape(N_PCOL, CHUNK * 2, B), ('z', 'x'), 0, 0)]
    all_to_all x0 -> x2, waiting for transfers between devices: none -> 15.1 us  [the longest x1 10.5 us: body(): few = lax.all_to_all(few, ('z', 'x'), 0, 0)]
    ppermute x16 -> x22, starting transfers between devices: 28 us -> 38.7 us  [shift(): lax.ppermute(value, axis, [(i, (i + by) % size) for i in range(size)])]
    all_to_all x0 -> x2, starting transfers between devices: none -> 10.3 us  [the longest x1 6.46 us: body(): few = lax.all_to_all(packed.reshape(N_PCOL, 8, B), ('z', 'x'), 0, 0)]
    ppermute x8 -> x0, starting transfers between devices: 8.44 us -> none  [the longest x2 3.88 us: merge_rows(): a = a + lax.ppermute(a, 'y', wrap)]
    pallas_call x5 -> x8, Pallas kernels: 31.7 us -> 23.4 us  [call(): pl.pallas_call(kernel, out_shape=[jax.ShapeDtypeStruct(shape, kind) for k...]
    ppermute x16 -> x22, waiting for transfers between devices: 29.5 us -> 22.6 us  [shift(): lax.ppermute(value, axis, [(i, (i + by) % size) for i in range(size)])]
  transfers between devices with their start and end apart: 26 -> 25, of which waited for: 13 -> 11; matrix products, arithmetic and copies ran while one was open for 4% -> 0% of each run, Pallas kernels for 6% -> 11%
where the time goes in v2:
time: 134 us; the launch traced here: 133 us
  starting transfers between devices  61 us (46%)
  waiting for transfers between devices  46.2 us (34%)
  Pallas kernels  23.4 us (17%)
  local copies, waits for them, and re-layouts  1.63 us (1%)
    ppermute x22, starting transfers between devices, shift(): lax.ppermute(value, axis, [(i, (i + by) % size) for i in range(size)])  38.7 us
    pallas_call x8, Pallas kernels, call(): pl.pallas_call(kernel, out_shape=[jax.ShapeDtypeStruct(shape, kind) for k...  23.4 us
    ppermute x22, waiting for transfers between devices, shift(): lax.ppermute(value, axis, [(i, (i + by) % size) for i in range(size)])  22.6 us
    all_to_all x1, starting transfers between devices, body(): spread = lax.all_to_all(raw.reshape(N_PCOL, CHUNK * 2, B), ('z', 'x'), 0, 0)  12 us
    all_to_all x1, waiting for transfers between devices, body(): few = lax.all_to_all(few, ('z', 'x'), 0, 0)  10.5 us
    all_to_all x1, waiting for transfers between devices, body(): spread = lax.all_to_all(raw.reshape(N_PCOL, CHUNK * 2, B), ('z', 'x'), 0, 0)  8.53 us
    all_to_all x1, starting transfers between devices, body(): few = lax.all_to_all(packed.reshape(N_PCOL, 8, B), ('z', 'x'), 0, 0)  6.46 us
    all_to_all x1, waiting for transfers between devices, body(): few = lax.all_to_all(packed.reshape(N_PCOL, 8, B), ('z', 'x'), 0, 0)  4.6 us
  transfers between devices with their start and end apart: 25, of which 11 were waited for; matrix products, arithmetic and copies ran while one was open for 0% of the time, Pallas kernels for 11%

profile of v2, /device:TPU:1, one launch (start us, length us, event | category | flops | bytes accessed | tf_op | source)
XLA Modules:
  0.0 132.6 jit_solution(9302870925929695947)
XLA Ops:
  0.0 12.0 %all-to-all-start = ((f32[32,64,128]{2,1,0:T(8,128)}), f32[32,64,128]{2,1,0:T(8,128)S(1)}, u32[]{:S(2)}, u32[]{:S(2)}) async-start(f32[32,64,128]{2,1,0:T(8,128)} %bitcast.34), calls=%async_computation | async-start | bytes 2097152 | tf_op jit(solution)/shard_map/all_to_all | solution.py:370
  13.6 2.7 %shard_map.55 = (f32[4,128,256]{2,1,0:T(8,128)S(1)}, f32[4,128,256]{2,1,0:T(8,128)S(1)}, f32[1024,256]{1,0:T(8,128)S(1)}) custom-call(s32[5]{0:T(128)S(1)} %stack.68.pos, s32[4]{0:T(128)S(1)} %copy-done.3, s32[64]{0:T(128)S(1)} %copy-done.4, s32[64,64]{1,0:T(8,128)S(1)} %copy-done.1, s32[512,1]{1,0:T(8,128)S(1)} %copy.7.target_col, s32[1,512]{1,0:T(1,128)S(1)} %bitcast.40, ...), custom_call_target="tpu_custom_call" | custom-call | tf_op jit(solution)/shard_map/pallas_call | solution.py:339
  17.3 1.5 %collective-permute-done.received = f32[4,128,256]{2,1,0:T(8,128)S(1)} collective-permute-done((f32[4,128,256]{2,1,0:T(8,128)S(1)}, f32[4,128,256]{2,1,0:T(8,128)S(1)}, u32[]{:S(2)}, u32[]{:S(2)}) %collective-permute-start) | collective-permute-done | bytes 524320 | tf_op jit(solution)/shard_map/ppermute | solution.py:350
  20.3 2.6 %collective-permute-start.2 = (f32[128,256]{1,0:T(8,128)S(1)}, f32[128,256]{1,0:T(8,128)S(1)}, u32[]{:S(2)}, u32[]{:S(2)}) collective-permute-start(f32[128,256]{1,0:T(8,128)S(1)} %get-tuple-element.29), channel_id=1, source_target_pairs={{0,4},{2,6},{4,0},{6,2},{1,5},{3,7},{5,1},{7,3},{8,12},{10,14},{12... | collective-permute-start | bytes 393224 | tf_op jit(solution)/shard_map/ppermute | solution.py:350
  25.1 3.9 %collective-permute-done.2.part2 = f32[128,256]{1,0:T(8,128)S(1)} collective-permute-done((f32[128,256]{1,0:T(8,128)S(1)}, f32[128,256]{1,0:T(8,128)S(1)}, u32[]{:S(2)}, u32[]{:S(2)}) %collective-permute-start.2) | collective-permute-done | bytes 131104 | tf_op jit(solution)/shard_map/ppermute | solution.py:350
  29.7 8.5 %all-to-all-done.spread = f32[32,64,128]{2,1,0:T(8,128)S(1)} async-done(((f32[32,64,128]{2,1,0:T(8,128)}), f32[32,64,128]{2,1,0:T(8,128)S(1)}, u32[]{:S(2)}, u32[]{:S(2)}) %all-to-all-start) | async-done | bytes 1048608 | tf_op jit(solution)/shard_map/all_to_all | solution.py:370
  40.0 2.4 %collective-permute-start.5 = (f32[32,512]{1,0:T(8,128)S(1)}, f32[32,512]{1,0:T(8,128)S(1)}, u32[]{:S(2)}, u32[]{:S(2)}) collective-permute-start(f32[32,512]{1,0:T(8,128)S(1)} %shard_map.58), channel_id=1, source_target_pairs={{0,64},{32,96},{64,128},{96,160},{128,192},{160,224},{192,0},{224,... | collective-permute-start | bytes 196616 | tf_op jit(solution)/shard_map/ppermute | solution.py:350
  42.4 2.0 %collective-permute-start.6 = (f32[32,512]{1,0:T(8,128)S(1)}, f32[32,512]{1,0:T(8,128)S(1)}, u32[]{:S(2)}, u32[]{:S(2)}) collective-permute-start(f32[32,512]{1,0:T(8,128)S(1)} %shard_map.58), channel_id=1, source_target_pairs={{0,96},{32,128},{64,160},{96,192},{128,224},{160,0},{192,32},{224,... | collective-permute-start | bytes 196616 | tf_op jit(solution)/shard_map/ppermute | solution.py:350
  44.4 3.6 %collective-permute-start.7 = (f32[32,512]{1,0:T(8,128)S(1)}, f32[32,512]{1,0:T(8,128)S(1)}, u32[]{:S(2)}, u32[]{:S(2)}) collective-permute-start(f32[32,512]{1,0:T(8,128)S(1)} %shard_map.58), channel_id=1, source_target_pairs={{0,128},{32,160},{64,192},{96,224},{128,0},{160,32},{192,64},{224,... | collective-permute-start | bytes 196616 | tf_op jit(solution)/shard_map/ppermute | solution.py:350
  48.7 6.5 %all-to-all-start.1 = ((f32[32,8,128]{2,1,0:T(8,128)}), f32[32,8,128]{2,1,0:T(8,128)S(1)}, u32[]{:S(2)}, u32[]{:S(2)}) async-start(f32[32,8,128]{2,1,0:T(8,128)} %bitcast.17), calls=%async_computation.1 | async-start | bytes 262144 | tf_op jit(solution)/shard_map/all_to_all | solution.py:386
  55.2 3.5 %collective-permute-start.9 = (f32[32,512]{1,0:T(8,128)S(1)}, f32[32,512]{1,0:T(8,128)S(1)}, u32[]{:S(2)}, u32[]{:S(2)}) collective-permute-start(f32[32,512]{1,0:T(8,128)S(1)} %shard_map.58), channel_id=1, source_target_pairs={{0,192},{32,224},{64,0},{96,32},{128,64},{160,96},{192,128},{224,1... | collective-permute-start | bytes 196616 | tf_op jit(solution)/shard_map/ppermute | solution.py:350
  59.9 4.6 %all-to-all-done.1.spread = f32[32,8,128]{2,1,0:T(8,128)S(1)} async-done(((f32[32,8,128]{2,1,0:T(8,128)}), f32[32,8,128]{2,1,0:T(8,128)S(1)}, u32[]{:S(2)}, u32[]{:S(2)}) %all-to-all-start.1) | async-done | bytes 131104 | tf_op jit(solution)/shard_map/all_to_all | solution.py:386
  65.8 3.9 %all-to-all-start.2 = ((f32[32,16,128]{2,1,0:T(8,128)}), f32[32,16,128]{2,1,0:T(8,128)S(1)}, u32[]{:S(2)}, u32[]{:S(2)}) async-start(f32[32,16,128]{2,1,0:T(8,128)} %shard_map.59), calls=%async_computation.2 | async-start | bytes 524288 | tf_op jit(solution)/shard_map/all_to_all | solution.py:388
  69.7 10.5 %all-to-all-done.2 = f32[32,16,128]{2,1,0:T(8,128)S(1)} async-done(((f32[32,16,128]{2,1,0:T(8,128)}), f32[32,16,128]{2,1,0:T(8,128)S(1)}, u32[]{:S(2)}, u32[]{:S(2)}) %all-to-all-start.2) | async-done | bytes 262176 | tf_op jit(solution)/shard_map/all_to_all | solution.py:388
  80.3 6.0 %collective-permute-start.18 = (f32[64,768]{1,0:T(8,128)S(1)}, f32[64,768]{1,0:T(8,128)S(1)}, u32[]{:S(2)}, u32[]{:S(2)}) collective-permute-start(f32[64,768]{1,0:T(8,128)S(1)} %get-tuple-element.36), channel_id=1, source_target_pairs={{0,1},{1,0},{2,3},{3,2},{4,5},{5,4},{6,7},{7,6},{8,9},{9,8},{10,11... | collective-permute-start | bytes 589832 | tf_op jit(solution)/shard_map/ppermute | solution.py:350
  87.5 1.4 %collective-permute-start.19 = (f32[2,64,768]{2,1,0:T(8,128)S(1)}, f32[2,64,768]{2,1,0:T(8,128)S(1)}, u32[]{:S(2)}, u32[]{:S(2)}) collective-permute-start(f32[2,64,768]{2,1,0:T(8,128)S(1)} %pad_maximum_fusion.1.pair0), channel_id=1, source_target_pairs={{0,2},{2,4},{4,6},{6,0},{1,3},{3,5},{5,7},{7,1},{8,10},{10,12},{12... | collective-permute-start | bytes 1179656 | tf_op jit(solution)/shard_map/ppermute | solution.py:350
  88.8 2.6 %collective-permute-start.20 = (f32[2,64,768]{2,1,0:T(8,128)S(1)}, f32[2,64,768]{2,1,0:T(8,128)S(1)}, u32[]{:S(2)}, u32[]{:S(2)}) collective-permute-start(f32[2,64,768]{2,1,0:T(8,128)S(1)} %pad_maximum_fusion.1.pair0), channel_id=1, source_target_pairs={{0,4},{2,6},{4,0},{6,2},{1,5},{3,7},{5,1},{7,3},{8,12},{10,14},{12... | collective-permute-start | bytes 1179656 | tf_op jit(solution)/shard_map/ppermute | solution.py:350
  93.7 7.6 %collective-permute-done.11.part1 = f32[8,32,512]{2,1,0:T(8,128)S(1)} collective-permute-done((f32[8,32,512]{2,1,0:T(8,128)S(1)}, f32[8,32,512]{2,1,0:T(8,128)S(1)}, u32[]{:S(2)}, u32[]{:S(2)}) %collective-permute-start.11) | collective-permute-done | bytes 524320 | tf_op jit(solution)/shard_map/ppermute | solution.py:350
  102.8 1.4 %collective-permute-start.15 = (f32[2,64,768]{2,1,0:T(8,128)S(1)}, f32[2,64,768]{2,1,0:T(8,128)S(1)}, u32[]{:S(2)}, u32[]{:S(2)}) collective-permute-start(f32[2,64,768]{2,1,0:T(8,128)S(1)} %pad_maximum_fusion.pair0), channel_id=1, source_target_pairs={{0,2},{2,4},{4,6},{6,0},{1,3},{3,5},{5,7},{7,1},{8,10},{10,12},{12... | collective-permute-start | bytes 1179656 | tf_op jit(solution)/shard_map/ppermute | solution.py:350
  104.1 4.7 %collective-permute-done.20.pair2 = f32[2,64,768]{2,1,0:T(8,128)S(1)} collective-permute-done((f32[2,64,768]{2,1,0:T(8,128)S(1)}, f32[2,64,768]{2,1,0:T(8,128)S(1)}, u32[]{:S(2)}, u32[]{:S(2)}) %collective-permute-start.20) | collective-permute-done | bytes 393248 | tf_op jit(solution)/shard_map/ppermute | solution.py:350
  109.1 3.0 %collective-permute-start.17 = (f32[2,64,768]{2,1,0:T(8,128)S(1)}, f32[2,64,768]{2,1,0:T(8,128)S(1)}, u32[]{:S(2)}, u32[]{:S(2)}) collective-permute-start(f32[2,64,768]{2,1,0:T(8,128)S(1)} %pad_maximum_fusion.pair0), channel_id=1, source_target_pairs={{0,6},{2,0},{4,2},{6,4},{1,7},{3,1},{5,3},{7,5},{8,14},{10,8},{12,... | collective-permute-start | bytes 1179656 | tf_op jit(solution)/shard_map/ppermute | solution.py:350
  112.1 9.8 %shard_map.61 = (f32[512,512]{1,0:T(8,128)S(1)}, f32[512,256]{1,0:T(8,128)S(1)}, bf16[512,512]{1,0:T(8,128)(2,1)S(1)}, bf16[512,512]{1,0:T(8,128)(2,1)S(1)}, bf1...) custom-call(s32[5]{0:T(128)S(1)} %stack.68.pos, f32[2,64,768]{2,1,0:T(8,128)S(1)} %pad_maximum_fusion.1.pair0, ...), custom_call_target="tpu_custom_call" | custom-call | tf_op jit(solution)/shard_map/pallas_call | solution.py:339
  121.9 2.4 %collective-permute-done.13.part3 = f32[8,32,512]{2,1,0:T(8,128)S(1)} collective-permute-done((f32[8,32,512]{2,1,0:T(8,128)S(1)}, f32[8,32,512]{2,1,0:T(8,128)S(1)}, u32[]{:S(2)}, u32[]{:S(2)}) %collective-permute-start.13) | collective-permute-done | bytes 524320 | tf_op jit(solution)/shard_map/ppermute | solution.py:350
  124.9 7.7 %shard_map.62 = f32[2048,128]{1,0:T(8,128)} custom-call(s32[5]{0:T(128)S(1)} %stack.68.pos, s32[4]{0:T(128)S(1)} %copy-done.3, s32[1,512]{1,0:T(1,128)S(1)} %bitcast.42, f32[1024,256]{1,0:T(8,128)S(1)} %get-tuple-element.24.rows, f32[8,32,512]{2,1,0:T(8,128)S(1)} %bitcast_dynamic-update-slice_fusion.part0, f32[8,32,512]{2,1,0:T(8,128)S(1)} %collective-permute-done.11.part1, ...), custom_call_target="tpu_custom_call" | custom-call | tf_op jit(solution)/shard_map/pallas_call | solution.py:339
  (56 shorter events, 17.6 us)
Async XLA Ops:
  0.0 38.2 %all-to-all-start = ((f32[32,64,128]{2,1,0:T(8,128)}), f32[32,64,128]{2,1,0:T(8,128)S(1)}, u32[]{:S(2)}, u32[]{:S(2)}) async-start(f32[32,64,128]{2,1,0:T(8,128)} %bitcast.34), calls=%async_computation | async-start | bytes 2097152 | tf_op jit(solution)/shard_map/all_to_all | solution.py:370
  18.9 6.1 %collective-permute-start.1 = (f32[128,256]{1,0:T(8,128)S(1)}, f32[128,256]{1,0:T(8,128)S(1)}, u32[]{:S(2)}, u32[]{:S(2)}) collective-permute-start(f32[128,256]{1,0:T(8,128)S(1)} %get-tuple-element.28), channel_id=1, source_target_pairs={{0,2},{2,4},{4,6},{6,0},{1,3},{3,5},{5,7},{7,1},{8,10},{10,12},{12... | collective-permute-start | bytes 393224 | tf_op jit(solution)/shard_map/ppermute | solution.py:350
  20.3 8.7 %collective-permute-start.2 = (f32[128,256]{1,0:T(8,128)S(1)}, f32[128,256]{1,0:T(8,128)S(1)}, u32[]{:S(2)}, u32[]{:S(2)}) collective-permute-start(f32[128,256]{1,0:T(8,128)S(1)} %get-tuple-element.29), channel_id=1, source_target_pairs={{0,4},{2,6},{4,0},{6,2},{1,5},{3,7},{5,1},{7,3},{8,12},{10,14},{12... | collective-permute-start | bytes 393224 | tf_op jit(solution)/shard_map/ppermute | solution.py:350
  22.9 6.1 %collective-permute-start.3 = (f32[128,256]{1,0:T(8,128)S(1)}, f32[128,256]{1,0:T(8,128)S(1)}, u32[]{:S(2)}, u32[]{:S(2)}) collective-permute-start(f32[128,256]{1,0:T(8,128)S(1)} %get-tuple-element.30), channel_id=1, source_target_pairs={{0,6},{2,0},{4,2},{6,4},{1,7},{3,1},{5,3},{7,5},{8,14},{10,8},{12,... | collective-permute-start | bytes 393224 | tf_op jit(solution)/shard_map/ppermute | solution.py:350
  39.4 15.8 %collective-permute-start.4 = (f32[32,512]{1,0:T(8,128)S(1)}, f32[32,512]{1,0:T(8,128)S(1)}, u32[]{:S(2)}, u32[]{:S(2)}) collective-permute-start(f32[32,512]{1,0:T(8,128)S(1)} %shard_map.58), channel_id=1, source_target_pairs={{0,32},{32,64},{64,96},{96,128},{128,160},{160,192},{192,224},{224... | collective-permute-start | bytes 196616 | tf_op jit(solution)/shard_map/ppermute | solution.py:350
  40.0 18.6 %collective-permute-start.5 = (f32[32,512]{1,0:T(8,128)S(1)}, f32[32,512]{1,0:T(8,128)S(1)}, u32[]{:S(2)}, u32[]{:S(2)}) collective-permute-start(f32[32,512]{1,0:T(8,128)S(1)} %shard_map.58), channel_id=1, source_target_pairs={{0,64},{32,96},{64,128},{96,160},{128,192},{160,224},{192,0},{224,... | collective-permute-start | bytes 196616 | tf_op jit(solution)/shard_map/ppermute | solution.py:350
  42.4 17.4 %collective-permute-start.6 = (f32[32,512]{1,0:T(8,128)S(1)}, f32[32,512]{1,0:T(8,128)S(1)}, u32[]{:S(2)}, u32[]{:S(2)}) collective-permute-start(f32[32,512]{1,0:T(8,128)S(1)} %shard_map.58), channel_id=1, source_target_pairs={{0,96},{32,128},{64,160},{96,192},{128,224},{160,0},{192,32},{224,... | collective-permute-start | bytes 196616 | tf_op jit(solution)/shard_map/ppermute | solution.py:350
  44.4 25.3 %collective-permute-start.7 = (f32[32,512]{1,0:T(8,128)S(1)}, f32[32,512]{1,0:T(8,128)S(1)}, u32[]{:S(2)}, u32[]{:S(2)}) collective-permute-start(f32[32,512]{1,0:T(8,128)S(1)} %shard_map.58), channel_id=1, source_target_pairs={{0,128},{32,160},{64,192},{96,224},{128,0},{160,32},{192,64},{224,... | collective-permute-start | bytes 196616 | tf_op jit(solution)/shard_map/ppermute | solution.py:350
  48.0 21.7 %collective-permute-start.8 = (f32[32,512]{1,0:T(8,128)S(1)}, f32[32,512]{1,0:T(8,128)S(1)}, u32[]{:S(2)}, u32[]{:S(2)}) collective-permute-start(f32[32,512]{1,0:T(8,128)S(1)} %shard_map.58), channel_id=1, source_target_pairs={{0,160},{32,192},{64,224},{96,0},{128,32},{160,64},{192,96},{224,1... | collective-permute-start | bytes 196616 | tf_op jit(solution)/shard_map/ppermute | solution.py:350
  48.7 15.8 %all-to-all-start.1 = ((f32[32,8,128]{2,1,0:T(8,128)}), f32[32,8,128]{2,1,0:T(8,128)S(1)}, u32[]{:S(2)}, u32[]{:S(2)}) async-start(f32[32,8,128]{2,1,0:T(8,128)} %bitcast.17), calls=%async_computation.1 | async-start | bytes 262144 | tf_op jit(solution)/shard_map/all_to_all | solution.py:386
  55.2 14.5 %collective-permute-start.9 = (f32[32,512]{1,0:T(8,128)S(1)}, f32[32,512]{1,0:T(8,128)S(1)}, u32[]{:S(2)}, u32[]{:S(2)}) collective-permute-start(f32[32,512]{1,0:T(8,128)S(1)} %shard_map.58), channel_id=1, source_target_pairs={{0,192},{32,224},{64,0},{96,32},{128,64},{160,96},{192,128},{224,1... | collective-permute-start | bytes 196616 | tf_op jit(solution)/shard_map/ppermute | solution.py:350
  58.6 27.7 %collective-permute-start.10 = (f32[32,512]{1,0:T(8,128)S(1)}, f32[32,512]{1,0:T(8,128)S(1)}, u32[]{:S(2)}, u32[]{:S(2)}) collective-permute-start(f32[32,512]{1,0:T(8,128)S(1)} %shard_map.58), channel_id=1, source_target_pairs={{0,224},{32,0},{64,32},{96,64},{128,96},{160,128},{192,160},{224,1... | collective-permute-start | bytes 196616 | tf_op jit(solution)/shard_map/ppermute | solution.py:350
  65.8 14.5 %all-to-all-start.2 = ((f32[32,16,128]{2,1,0:T(8,128)}), f32[32,16,128]{2,1,0:T(8,128)S(1)}, u32[]{:S(2)}, u32[]{:S(2)}) async-start(f32[32,16,128]{2,1,0:T(8,128)} %shard_map.59), calls=%async_computation.2 | async-start | bytes 524288 | tf_op jit(solution)/shard_map/all_to_all | solution.py:388
  80.3 7.1 %collective-permute-start.18 = (f32[64,768]{1,0:T(8,128)S(1)}, f32[64,768]{1,0:T(8,128)S(1)}, u32[]{:S(2)}, u32[]{:S(2)}) collective-permute-start(f32[64,768]{1,0:T(8,128)S(1)} %get-tuple-element.36), channel_id=1, source_target_pairs={{0,1},{1,0},{2,3},{3,2},{4,5},{5,4},{6,7},{7,6},{8,9},{9,8},{10,11... | collective-permute-start | bytes 589832 | tf_op jit(solution)/shard_map/ppermute | solution.py:350
  86.4 15.0 %collective-permute-start.11 = (f32[8,32,512]{2,1,0:T(8,128)S(1)}, f32[8,32,512]{2,1,0:T(8,128)S(1)}, u32[]{:S(2)}, u32[]{:S(2)}) collective-permute-start(f32[8,32,512]{2,1,0:T(8,128)S(1)} %bitcast_dynamic-update-slice_fusion.part0), channel_id=1, source_target_pairs={{0,8},{8,16},{16,24},{24,0},{1,9},{9,17},{17,25},{25,1},{2,10},{10... | collective-permute-start | bytes 1572872 | tf_op jit(solution)/shard_map/ppermute | solution.py:350
  87.5 15.3 %collective-permute-start.19 = (f32[2,64,768]{2,1,0:T(8,128)S(1)}, f32[2,64,768]{2,1,0:T(8,128)S(1)}, u32[]{:S(2)}, u32[]{:S(2)}) collective-permute-start(f32[2,64,768]{2,1,0:T(8,128)S(1)} %pad_maximum_fusion.1.pair0), channel_id=1, source_target_pairs={{0,2},{2,4},{4,6},{6,0},{1,3},{3,5},{5,7},{7,1},{8,10},{10,12},{12... | collective-permute-start | bytes 1179656 | tf_op jit(solution)/shard_map/ppermute | solution.py:350
  88.8 20.0 %collective-permute-start.20 = (f32[2,64,768]{2,1,0:T(8,128)S(1)}, f32[2,64,768]{2,1,0:T(8,128)S(1)}, u32[]{:S(2)}, u32[]{:S(2)}) collective-permute-start(f32[2,64,768]{2,1,0:T(8,128)S(1)} %pad_maximum_fusion.1.pair0), channel_id=1, source_target_pairs={{0,4},{2,6},{4,0},{6,2},{1,5},{3,7},{5,1},{7,3},{8,12},{10,14},{12... | collective-permute-start | bytes 1179656 | tf_op jit(solution)/shard_map/ppermute | solution.py:350
  91.5 17.7 %collective-permute-start.21 = (f32[2,64,768]{2,1,0:T(8,128)S(1)}, f32[2,64,768]{2,1,0:T(8,128)S(1)}, u32[]{:S(2)}, u32[]{:S(2)}) collective-permute-start(f32[2,64,768]{2,1,0:T(8,128)S(1)} %pad_maximum_fusion.1.pair0), channel_id=1, source_target_pairs={{0,6},{2,0},{4,2},{6,4},{1,7},{3,1},{5,3},{7,5},{8,14},{10,8},{12,... | collective-permute-start | bytes 1179656 | tf_op jit(solution)/shard_map/ppermute | solution.py:350
  92.5 8.9 %collective-permute-start.14 = (f32[64,768]{1,0:T(8,128)S(1)}, f32[64,768]{1,0:T(8,128)S(1)}, u32[]{:S(2)}, u32[]{:S(2)}) collective-permute-start(f32[64,768]{1,0:T(8,128)S(1)} %get-tuple-element.35), channel_id=1, source_target_pairs={{0,1},{1,0},{2,3},{3,2},{4,5},{5,4},{6,7},{7,6},{8,9},{9,8},{10,11... | collective-permute-start | bytes 589832 | tf_op jit(solution)/shard_map/ppermute | solution.py:350
  101.4 20.5 %collective-permute-start.12 = (f32[8,32,512]{2,1,0:T(8,128)S(1)}, f32[8,32,512]{2,1,0:T(8,128)S(1)}, u32[]{:S(2)}, u32[]{:S(2)}) collective-permute-start(f32[8,32,512]{2,1,0:T(8,128)S(1)} %bitcast_dynamic-update-slice_fusion.part0), channel_id=1, source_target_pairs={{0,16},{8,24},{16,0},{24,8},{1,17},{9,25},{17,1},{25,9},{2,18},{10... | collective-permute-start | bytes 1572872 | tf_op jit(solution)/shard_map/ppermute | solution.py:350
  101.5 22.9 %collective-permute-start.13 = (f32[8,32,512]{2,1,0:T(8,128)S(1)}, f32[8,32,512]{2,1,0:T(8,128)S(1)}, u32[]{:S(2)}, u32[]{:S(2)}) collective-permute-start(f32[8,32,512]{2,1,0:T(8,128)S(1)} %bitcast_dynamic-update-slice_fusion.part0), channel_id=1, source_target_pairs={{0,24},{8,0},{16,8},{24,16},{1,25},{9,1},{17,9},{25,17},{2,26},{10... | collective-permute-start | bytes 1572872 | tf_op jit(solution)/shard_map/ppermute | solution.py:350
  102.8 21.6 %collective-permute-start.15 = (f32[2,64,768]{2,1,0:T(8,128)S(1)}, f32[2,64,768]{2,1,0:T(8,128)S(1)}, u32[]{:S(2)}, u32[]{:S(2)}) collective-permute-start(f32[2,64,768]{2,1,0:T(8,128)S(1)} %pad_maximum_fusion.pair0), channel_id=1, source_target_pairs={{0,2},{2,4},{4,6},{6,0},{1,3},{3,5},{5,7},{7,1},{8,10},{10,12},{12... | collective-permute-start | bytes 1179656 | tf_op jit(solution)/shard_map/ppermute | solution.py:350
  108.8 16.1 %collective-permute-start.16 = (f32[2,64,768]{2,1,0:T(8,128)S(1)}, f32[2,64,768]{2,1,0:T(8,128)S(1)}, u32[]{:S(2)}, u32[]{:S(2)}) collective-permute-start(f32[2,64,768]{2,1,0:T(8,128)S(1)} %pad_maximum_fusion.pair0), channel_id=1, source_target_pairs={{0,4},{2,6},{4,0},{6,2},{1,5},{3,7},{5,1},{7,3},{8,12},{10,14},{12... | collective-permute-start | bytes 1179656 | tf_op jit(solution)/shard_map/ppermute | solution.py:350
  109.1 15.7 %collective-permute-start.17 = (f32[2,64,768]{2,1,0:T(8,128)S(1)}, f32[2,64,768]{2,1,0:T(8,128)S(1)}, u32[]{:S(2)}, u32[]{:S(2)}) collective-permute-start(f32[2,64,768]{2,1,0:T(8,128)S(1)} %pad_maximum_fusion.pair0), channel_id=1, source_target_pairs={{0,6},{2,0},{4,2},{6,4},{1,7},{3,1},{5,3},{7,5},{8,14},{10,8},{12,... | collective-permute-start | bytes 1179656 | tf_op jit(solution)/shard_map/ppermute | solution.py:350
  (6 other events, 18.3 us)

commit v3 on v2

--- a/solution.py
+++ b/solution.py
@@ -108,40 +108,19 @@
         sums[u][...] = keep[u] + received[u]
 
 
-def sum_kernel(part0, part1, part2, part3, total, packed):
-    value = (part0[...] + part1[...]) + (part2[...] + part3[...])
-    total[...] = value
-    for s in range(2):
-        for i in range(4):
-            packed[pl.ds(s * 4 + i, N_PCOL, stride=8), :] = value[
-                i * N_PCOL : (i + 1) * N_PCOL, s * B : (s + 1) * B
-            ]
-
-
-def select_few_kernel(order, spread, out):
-    pieces = []
-    for k in range(PANELS):
-        p = order[k]
-        block = spread[p % N_PCOL]
-        pieces.append(jnp.where(p >= N_PCOL, block[4:], block[:4]))
-    value = jnp.concatenate(pieces, axis=0)
-    for j in range(N_PCOL):
-        out[j] = value
-
-
-def arrange_kernel(gathered, total, pivots, homes):
-    for i in range(2):
-        here = slice(i * N_PCOL, (i + 1) * N_PCOL)
-        for k in range(PANELS):
-            cols = slice(k * B, (k + 1) * B)
-            pivots[here, cols] = gathered[pl.ds(k * 4 + i, N_PCOL, stride=16), :]
-            homes[here, cols] = gathered[pl.ds(k * 4 + i + 2, N_PCOL, stride=16), :]
-    half = S // N_PROW
-    pivots[:, S:] = total[:half]
-    homes[:, S:] = total[half:]
-
-
-def select_kernel(pos, order, width, pattern, target_row, spread, out):
+def sum_kernel(pos, part0, part1, part2, part3, total, *chunks):
+    x = pos[3]
+    total[...] = (part0[...] + part1[...]) + (part2[...] + part3[...])
+    count = CHUNK // 2
+    for u in range(NX):
+        start = lax.rem(x + u, NX) * count
+        chunks[u][:count, :] = total[pl.ds(pl.multiple_of(start, count), count), :]
+        chunks[u][count:, :] = total[pl.ds(pl.multiple_of(S // N_PROW + start, count), count), :]
+
+
+def select_kernel(
+    pos, order, width, pattern, target_row, spread, chunk0, chunk1, chunk2, chunk3, out
+):
     r = pos[0]
     z = pos[2]
     x = pos[3]
@@ -149,7 +128,8 @@
     taken = is_target(target_row, CHUNK, block_row * B + x * CHUNK)
     for k in range(PANELS):
         p = order[k]
-        source = p % N_PCOL
+        source = lax.rem(p, N_PCOL)
+        cols = slice(k * B, (k + 1) * B)
         value = jnp.where(
             p >= N_PCOL,
             spread[source, pl.ds(1, CHUNK, stride=2), :],
@@ -158,19 +138,75 @@
         value = kept(
             value, pattern[block_row, p] > 0, width[block_row], width[p], block_row == p, x * CHUNK
         )
-        out[:, k * B : (k + 1) * B] = jnp.where(taken, 0.0, value)
-
-
-def natural_order(pos, pairs, out, columns):
+        value = jnp.where(taken, 0.0, value)
+        for j in range(NZ):
+            out[j, :CHUNK, cols] = value
+        value = jnp.zeros((CHUNK, B), F32)
+        for u, chunk in enumerate((chunk0, chunk1, chunk2, chunk3)):
+            here = source == z * NX + lax.rem(x - u + NX, NX)
+            value = jnp.where(here & (p < N_PCOL), chunk[:, :B], value)
+            value = jnp.where(here & (p >= N_PCOL), chunk[:, B:], value)
+        for j in range(NZ):
+            out[j, CHUNK:, cols] = value
+
+
+def split_kernel(pieces, strips, rows):
+    value = pieces[0, CHUNK:, :]
+    for i in range(1, NZ):
+        value = value + pieces[i, CHUNK:, :]
+    rows[...] = value
+    for i in range(NZ):
+        strips[i] = pieces[i, :CHUNK, :]
+
+
+def panel_order_rows(pos, same_core, other_core, first, out):
+    c = pos[4]
+    x = pos[3]
+    y = lax.div(pos[0], NC)
+    count = CHUNK // 2
+    for u in range(NY):
+        other_y = lax.rem(y - u + NY, NY)
+        for core, group in ((c, same_core), (1 - c, other_core)):
+            for j in range(NX):
+                other_x = lax.rem(x - j + NX, NX)
+                start = ((other_y * NC + core) * NX + other_x) * count
+                out[pl.ds(pl.multiple_of(start, count), count), :] = group[u, j, first : first + count, :]
+
+
+def prow_order(pos, same_core, other_core, first, out):
     c = pos[4]
     y = lax.div(pos[0], NC)
     part = S // N_PROW
     for u in range(NY):
         other_y = lax.rem(y - u + NY, NY)
-        for i in range(NC):
-            core = c if i == 0 else 1 - c
+        for core, group in ((c, same_core), (1 - c, other_core)):
             start = pl.multiple_of((other_y * NC + core) * part, part)
-            out[pl.ds(start, part), :] = pairs[u][i, :, columns]
+            out[pl.ds(start, part), :] = group[u, first : first + part, :]
+
+
+def panels_here(pos, order):
+    found = [jnp.int32(-1), jnp.int32(-1)]
+    for s in range(2):
+        for k in range(PANELS):
+            found[s] = jnp.where(order[k] == s * N_PCOL + pos[1], k, found[s])
+    return found
+
+
+def quick_invert(corner):
+    row = iota((B, B), 0)
+    col = iota((B, B), 1)
+    eye = jnp.where(row == col, 1.0, 0.0)
+    diagonal = jnp.where(row == col, corner, 0.0)
+    by_col = 1.0 / jnp.sum(diagonal, axis=0, keepdims=True)
+    by_row = 1.0 / jnp.sum(diagonal, axis=1, keepdims=True)
+    corner_parts = split2(corner)
+    approx = by_row * (eye + (eye - corner * by_col))
+    high, low = split2(approx)
+    residual = eye - dot3(corner_parts, (high, low))
+    approx = approx + dot_bf16(high, residual.astype(BF16))
+    residual = eye - dot_full(corner, approx)
+    error = jnp.sum(residual * residual)
+    return approx + dot_bf16(approx.astype(BF16), residual.astype(BF16)), error
 
 
 def invert(corner, work, pivot_rows, out):
@@ -224,88 +260,81 @@
 
 
 def corner_kernel(
-    pos, pair0, pair1, pair2, pair3,
-    factor, upper, solve_high, solve_low, upper_high, upper_low, inverses, work, solver, pivot_rows,
+    pos, order, few, few_other, owns, owns_other,
+    factor, upper, steps_high, steps_low, inverses, work, solver, steps, pivot_rows,
 ):
-    pairs = (pair0, pair1, pair2, pair3)
-    natural_order(pos, pairs, factor, slice(0, S))
-    natural_order(pos, pairs, upper, slice(S, S + 2 * B))
-    solver[...] = jnp.zeros((S, S), F32)
-    for k in range(PANELS):
-        here = slice(k * B, (k + 1) * B)
-        later = slice((k + 1) * B, S)
-        before = slice(0, k * B)
-        invert(factor[here, here], work, pivot_rows, inverses)
-        inverse = inverses[...]
-        solver[here, here] = inverse
-        if k + 1 < PANELS:
-            lower = dot_full(factor[later, here], inverse)
-            factor[later, here] = lower
-            factor[later, later] = factor[later, later] - dot_full(lower, factor[here, later])
-            upper[later, :] = upper[later, :] - dot_full(lower, upper[here, :])
-        if k:
-            solver[before, here] = -dot_full(dot_full(solver[before, before], factor[before, here]), inverse)
-    high, low = split2(solver[...])
-    solve_high[...] = high
-    solve_low[...] = low
-    high, low = split2(upper[...])
-    upper_high[...] = high
-    upper_low[...] = low
+    def eliminate(invert_block):
+        panel_order_rows(pos, few, few_other, 0, factor)
+        prow_order(pos, owns, owns_other, 0, upper)
+        solver[...] = jnp.zeros((S, S), F32)
+        error = jnp.float32(0.0)
+        for k in range(PANELS):
+            here = slice(k * B, (k + 1) * B)
+            later = slice((k + 1) * B, S)
+            before = slice(0, k * B)
+            inverse, found = invert_block(factor[here, here])
+            error = error + found
+            inverse_parts = split2(inverse)
+            solver[here, here] = inverse
+            if k + 1 < PANELS:
+                lower = dot3(split2(factor[later, here]), inverse_parts)
+                factor[later, here] = lower
+                lower_parts = split2(lower)
+                factor[later, later] = factor[later, later] - dot3(lower_parts, split2(factor[here, later]))
+                upper[later, :] = upper[later, :] - dot3(lower_parts, split2(upper[here, :]))
+            if k:
+                above = dot3(split2(solver[before, before]), split2(factor[before, here]))
+                solver[before, here] = -dot3(split2(above), inverse_parts)
+        return error
+
+    def robust(corner):
+        invert(corner, work, pivot_rows, inverses)
+        return inverses[...], jnp.float32(0.0)
+
+    error = eliminate(quick_invert)
+
+    @pl.when(jnp.logical_not(error < 1e-6))
+    def _():
+        eliminate(robust)
+
+    steps[...] = dot3(split2(solver[...]), split2(upper[...]))
+    found = panels_here(pos, order)
+    for s in range(2):
+
+        @pl.when(found[s] >= 0)
+        def _():
+            steps[:, s * B : (s + 1) * B] = -solver[:, pl.ds(pl.multiple_of(found[s] * B, B), B)]
+
+    high, low = split2(steps[...])
+    steps_high[...] = high
+    steps_low[...] = low
 
 
 def update_kernel(
-    pos, order, target_row, rows, part0, part1, part2, part3, pair0, pair1, pair2, pair3,
-    factor, upper, solve_high, solve_low, upper_high, upper_low,
-    out, lower, taken, home_rows, homes,
+    pos, order, target_row, rows, part0, part1, part2, part3, few, few_other, owns, owns_other,
+    factor, upper, steps_high, steps_low,
+    out, taken, home_rows, homes,
 ):
     r = pos[0]
-    q = pos[1]
-    z = pos[2]
     x = pos[3]
     half = S // 2
-    upper_parts = (upper_high[...], upper_low[...])
-    solve_first = (solve_high[:half, :half], solve_low[:half, :half])
-    solve_second = (solve_high[:, half:], solve_low[:, half:])
-    pairs = (pair0, pair1, pair2, pair3)
-    natural_order(pos, pairs, home_rows, slice(0, S))
-    natural_order(pos, pairs, homes, slice(S, S + 2 * B))
-
-    panel_of = []
-    for s in range(2):
-        found = jnp.int32(-1)
-        for k in range(PANELS):
-            found = jnp.where(order[k] == s * N_PCOL + q, k, found)
-        panel_of.append(found)
-
-    def solve(value):
-        high, low = split2(value)
-        first = dot3((high[:, :half], low[:, :half]), solve_first)
-        second = dot3((high, low), solve_second)
-        value = jnp.concatenate([first, second], axis=1)
-        return value, dot3(split2(value), upper_parts)
+    steps_parts = (steps_high[...], steps_low[...])
+    found = panels_here(pos, order)
+    panel_order_rows(pos, few, few_other, CHUNK // 2, home_rows)
+    prow_order(pos, owns, owns_other, S // N_PROW, homes)
 
     for i in range(2):
         here = slice(i * half, (i + 1) * half)
-        value, product = solve(home_rows[here, :])
-        home_rows[here, :] = value
-        homes[here, :] = homes[here, :] - product
+        product = dot3(split2(home_rows[here, :]), steps_parts)
+        for s in range(2):
+            cols = slice(s * B, (s + 1) * B)
+            homes[here, cols] = jnp.where(found[s] >= 0, 0.0, homes[here, cols]) - product[:, cols]
     for u, part in enumerate((part0, part1, part2, part3)):
-        value, product = solve(part[...].reshape(NZ * CHUNK, S))
+        product = dot3(split2(part[...].reshape(NZ * CHUNK, S)), steps_parts)
         other_x = lax.rem(x - u + NX, NX)
         for i in range(NZ):
-            t = lax.rem(z - i + NZ, NZ)
-            place = pl.ds(pl.multiple_of(t * B + other_x * CHUNK, CHUNK), CHUNK)
-            lower[place, :] = value[i * CHUNK : (i + 1) * CHUNK]
+            place = pl.ds(pl.multiple_of(i * B + other_x * CHUNK, CHUNK), CHUNK)
             taken[place, :] = product[i * CHUNK : (i + 1) * CHUNK]
-
-    for s in range(2):
-        cols = slice(s * B, (s + 1) * B)
-
-        @pl.when(panel_of[s] >= 0)
-        def _():
-            at = pl.ds(pl.multiple_of(panel_of[s] * B, B), B)
-            homes[:, cols] = home_rows[:, at]
-            taken[:, cols] = -lower[:, at]
 
     home_parts = split3(homes[...])
     for t in range(BR):
@@ -316,7 +345,7 @@
         moved = dot_bf16(hot, home_parts[0]) + (dot_bf16(hot, home_parts[1]) + dot_bf16(hot, home_parts[2]))
         for s in range(2):
             cols = slice(s * B, (s + 1) * B)
-            value = jnp.where(panel_of[s] >= 0, 0.0, rows[here, cols])
+            value = jnp.where(found[s] >= 0, 0.0, rows[here, cols])
             out[pl.ds(t * 2 * B + s, B, stride=2), :] = (value - taken[here, cols]) + moved[:, cols]
 
     for k in range(PANELS):
@@ -326,9 +355,9 @@
             t = lax.div(order[k], N_PROW)
             here = slice(k * B, (k + 1) * B)
             for s in range(2):
-                at = pl.multiple_of(jnp.maximum(panel_of[s], 0) * B, B)
+                at = pl.multiple_of(jnp.maximum(found[s], 0) * B, B)
                 value = jnp.where(
-                    panel_of[s] >= 0, factor[here, pl.ds(at, B)], upper[here, s * B : (s + 1) * B]
+                    found[s] >= 0, factor[here, pl.ds(at, B)], upper[here, s * B : (s + 1) * B]
                 )
                 out[pl.ds(t * 2 * B + s, B, stride=2), :] = value
 
@@ -350,9 +379,8 @@
     return lax.ppermute(value, axis, [(i, (i + by) % size) for i in range(size)])
 
 
-def gather_pairs(value):
-    pair = jnp.stack([value, shift(value, "c", NC, 1)])
-    return [pair] + [shift(pair, "y", NY, u) for u in range(1, NY)]
+def gather(value, axis, size):
+    return jnp.stack([value] + [shift(value, axis, size, i) for i in range(1, size)])
 
 
 def body(matrix, node_width, block_pattern, pivot_row_targets, panel_order):
@@ -379,45 +407,46 @@
         add_kernel, [], [keep, shift(give, "c", NC, 1)], [(F32, (2 * part, 2 * B))] * NY, []
     )
     sums = [sums[0]] + [shift(sums[u], "y", NY, u) for u in range(1, NY)]
-    total, packed = call(
-        sum_kernel, [], sums, [(F32, (2 * part, 2 * B)), (F32, (N_PCOL * 8, B))], []
-    )
-    spread, packed = lax.optimization_barrier((spread, packed))
-    few = lax.all_to_all(packed.reshape(N_PCOL, 8, B), ("z", "x"), 0, 0)
-    (few,) = call(select_few_kernel, [panel_order], [few], [(F32, (N_PCOL, 16, B))], [])
-    few = lax.all_to_all(few, ("z", "x"), 0, 0)
-    pivots, homes = call(
-        arrange_kernel, [], [few.reshape(N_PCOL * 16, B), total], [(F32, (part, S + 2 * B))] * 2, []
-    )
-    pivots = gather_pairs(pivots)
-    homes = gather_pairs(homes)
+    total, *chunks = call(
+        sum_kernel,
+        [pos],
+        sums,
+        [(F32, (2 * part, 2 * B))] + [(F32, (CHUNK, 2 * B))] * NX,
+        [],
+    )
+    chunks = [chunks[0]] + [shift(chunks[u], "x", NX, u) for u in range(1, NX)]
+    owns = gather(total, "y", NY)
+    owns_other = shift(owns, "c", NC, 1)
+
+    (pieces,) = call(
+        select_kernel, where, [target_row, spread, *chunks], [(F32, (NZ, 2 * CHUNK, S))], []
+    )
+    pieces = lax.all_to_all(pieces, "z", 0, 0)
+    pieces, owns_other = lax.optimization_barrier((pieces, owns_other))
+    strips, few = call(split_kernel, [], [pieces], [(F32, (NZ, CHUNK, S)), (F32, (CHUNK, S))], [])
+    parts = [strips] + [shift(strips, "x", NX, u) for u in range(1, NX)]
+    few = gather(gather(few, "x", NX), "y", NY)
+    few, parts[1], parts[3] = lax.optimization_barrier((few, parts[1], parts[3]))
+    few_other = shift(few, "c", NC, 1)
     solved = call(
         corner_kernel,
-        [pos],
-        pivots,
-        [(F32, (S, S)), (F32, (S, 2 * B)), (BF16, (S, S)), (BF16, (S, S)), (BF16, (S, 2 * B)), (BF16, (S, 2 * B))],
+        [pos, panel_order],
+        [few, few_other, owns, owns_other],
+        [(F32, (S, S)), (F32, (S, 2 * B)), (BF16, (S, 2 * B)), (BF16, (S, 2 * B))],
         [
             pltpu.VMEM((B, B), F32),
             pltpu.VMEM((B, 2 * B), F32),
             pltpu.VMEM((S, S), F32),
+            pltpu.VMEM((S, 2 * B), F32),
             pltpu.SMEM((B,), jnp.int32),
         ],
     )
-
-    (strip,) = call(select_kernel, where, [target_row, spread], [(F32, (CHUNK, S))], [])
-    strips = jnp.stack([strip] + [shift(strip, "z", NZ, i) for i in range(1, NZ)])
-    parts = [strips] + [shift(strips, "x", NX, u) for u in range(1, NX)]
     (out,) = call(
         update_kernel,
         [pos, panel_order],
-        [target_row, rows, *parts, *homes, *solved],
+        [target_row, rows, *parts, few, few_other, owns, owns_other, *solved],
         [(F32, (ROWS * 2, B))],
-        [
-            pltpu.VMEM((ROWS, S), F32),
-            pltpu.VMEM((ROWS, 2 * B), F32),
-            pltpu.VMEM((S, S), F32),
-            pltpu.VMEM((S, 2 * B), F32),
-        ],
+        [pltpu.VMEM((ROWS, 2 * B), F32), pltpu.VMEM((S, S), F32), pltpu.VMEM((S, 2 * B), F32)],
     )
     return out.reshape(matrix.shape)
 

time: 134 us -> 119 us (0.89)
  starting transfers between devices: 61 us -> 50 us
  waiting for transfers between devices: 46.2 us -> 42.9 us
    all_to_all x1, waiting for transfers between devices: 8.53 us -> 1.19 us  [body(): spread = lax.all_to_all(raw.reshape(N_PCOL, CHUNK * 2, B), ('z', 'x'), 0, 0)]
    ppermute x22 -> x21, starting transfers between devices: 38.7 us -> 32.7 us  [shift(): lax.ppermute(value, axis, [(i, (i + by) % size) for i in range(size)])]
    ppermute x22 -> x21, waiting for transfers between devices: 22.6 us -> 28.4 us  [shift(): lax.ppermute(value, axis, [(i, (i + by) % size) for i in range(size)])]
    all_to_all x2 -> x1, starting transfers between devices: 10.3 us -> 5.31 us  [body(): pieces = lax.all_to_all(pieces, 'z', 0, 0)]
    all_to_all x2 -> x1, waiting for transfers between devices: 15.1 us -> 13.3 us  [body(): pieces = lax.all_to_all(pieces, 'z', 0, 0)]
    pallas_call x8 -> x7, Pallas kernels: 23.4 us -> 23 us  [call(): pl.pallas_call(kernel, out_shape=[jax.ShapeDtypeStruct(shape, kind) for k...]
  transfers between devices with their start and end apart: 25 -> 23, of which waited for: 11 -> 15; matrix products, arithmetic and copies ran while one was open for 0% -> 0% of each run, Pallas kernels for 11% -> 14%
where the time goes in v3:
time: 119 us; the launch traced here: 118 us
  starting transfers between devices  50 us (42%)
  waiting for transfers between devices  42.9 us (36%)
  Pallas kernels  23 us (19%)
  local copies, waits for them, and re-layouts  1.58 us (1%)
    ppermute x21, starting transfers between devices, shift(): lax.ppermute(value, axis, [(i, (i + by) % size) for i in range(size)])  32.7 us
    ppermute x21, waiting for transfers between devices, shift(): lax.ppermute(value, axis, [(i, (i + by) % size) for i in range(size)])  28.4 us
    pallas_call x7, Pallas kernels, call(): pl.pallas_call(kernel, out_shape=[jax.ShapeDtypeStruct(shape, kind) for k...  23 us
    all_to_all x1, waiting for transfers between devices, body(): pieces = lax.all_to_all(pieces, 'z', 0, 0)  13.3 us
    all_to_all x1, starting transfers between devices, body(): spread = lax.all_to_all(raw.reshape(N_PCOL, CHUNK * 2, B), ('z', 'x'), 0, 0)  12 us
    all_to_all x1, starting transfers between devices, body(): pieces = lax.all_to_all(pieces, 'z', 0, 0)  5.31 us
  transfers between devices with their start and end apart: 23, of which 15 were waited for; matrix products, arithmetic and copies ran while one was open for 0% of the time, Pallas kernels for 14%

profile of v3, /device:TPU:1, one launch (start us, length us, event | category | flops | bytes accessed | tf_op | source)
XLA Modules:
  0.0 117.9 jit_solution(17549814680709570487)
XLA Ops:
  0.0 12.0 %all-to-all-start = ((f32[32,64,128]{2,1,0:T(8,128)}), f32[32,64,128]{2,1,0:T(8,128)S(1)}, u32[]{:S(2)}, u32[]{:S(2)}) async-start(f32[32,64,128]{2,1,0:T(8,128)} %bitcast.25), calls=%async_computation | async-start | bytes 2097152 | tf_op jit(solution)/shard_map/all_to_all | solution.py:398
  13.6 2.7 %shard_map.55 = (f32[4,128,256]{2,1,0:T(8,128)S(1)}, f32[4,128,256]{2,1,0:T(8,128)S(1)}, f32[1024,256]{1,0:T(8,128)S(1)}) custom-call(s32[5]{0:T(128)S(1)} %stack.68.pos, s32[4]{0:T(128)S(1)} %copy-done.3, s32[64]{0:T(128)S(1)} %copy-done.4, s32[64,64]{1,0:T(8,128)S(1)} %copy-done.1, s32[512,1]{1,0:T(8,128)S(1)} %copy.7.target_col, s32[1,512]{1,0:T(1,128)S(1)} %bitcast.30, ...), custom_call_target="tpu_custom_call" | custom-call | tf_op jit(solution)/shard_map/pallas_call | solution.py:368
  20.3 2.6 %collective-permute-start.2 = (f32[128,256]{1,0:T(8,128)S(1)}, f32[128,256]{1,0:T(8,128)S(1)}, u32[]{:S(2)}, u32[]{:S(2)}) collective-permute-start(f32[128,256]{1,0:T(8,128)S(1)} %get-tuple-element.33), channel_id=1, source_target_pairs={{0,4},{2,6},{4,0},{6,2},{1,5},{3,7},{5,1},{7,3},{8,12},{10,14},{12... | collective-permute-start | bytes 393224 | tf_op jit(solution)/shard_map/ppermute | solution.py:379
  25.1 3.9 %collective-permute-done.2.part2 = f32[128,256]{1,0:T(8,128)S(1)} collective-permute-done((f32[128,256]{1,0:T(8,128)S(1)}, f32[128,256]{1,0:T(8,128)S(1)}, u32[]{:S(2)}, u32[]{:S(2)}) %collective-permute-start.2) | collective-permute-done | bytes 131104 | tf_op jit(solution)/shard_map/ppermute | solution.py:379
  29.6 1.6 %collective-permute-start.4 = (f32[32,256]{1,0:T(8,128)S(1)}, f32[32,256]{1,0:T(8,128)S(1)}, u32[]{:S(2)}, u32[]{:S(2)}) collective-permute-start(f32[32,256]{1,0:T(8,128)S(1)} %get-tuple-element.36), channel_id=1, source_target_pairs={{0,8},{8,16},{16,24},{24,0},{1,9},{9,17},{17,25},{25,1},{2,10},{10... | collective-permute-start | bytes 98312 | tf_op jit(solution)/shard_map/ppermute | solution.py:379
  31.2 2.4 %collective-permute-start.5 = (f32[32,256]{1,0:T(8,128)S(1)}, f32[32,256]{1,0:T(8,128)S(1)}, u32[]{:S(2)}, u32[]{:S(2)}) collective-permute-start(f32[32,256]{1,0:T(8,128)S(1)} %get-tuple-element.37), channel_id=1, source_target_pairs={{0,16},{8,24},{16,0},{24,8},{1,17},{9,25},{17,1},{25,9},{2,18},{10... | collective-permute-start | bytes 98312 | tf_op jit(solution)/shard_map/ppermute | solution.py:379
  38.2 2.2 %shard_map.58 = f32[8,64,512]{2,1,0:T(8,128)} custom-call(s32[5]{0:T(128)S(1)} %stack.68.pos, s32[4]{0:T(128)S(1)} %copy-done.3, s32[64]{0:T(128)S(1)} %copy-done.4, s32[64,64]{1,0:T(8,128)S(1)} %copy-done.1, s32[1,512]{1,0:T(1,128)S(1)} %bitcast.31, f32[32,64,128]{2,1,0:T(8,128)S(1)} %all-to-all-done.spread, f32[32,256]{1,0:T(8,128)S(1)} %get-tuple-element.35.chunk0, ...), custom_call_target="tpu_custom_call" | custom-call | tf_op jit(solution)/shard_map/pallas_call | solution.py:368
  40.4 5.3 %all-to-all-start.1 = ((f32[8,64,512]{2,1,0:T(8,128)}), f32[8,64,512]{2,1,0:T(8,128)S(1)}, u32[]{:S(2)}, u32[]{:S(2)}) async-start(f32[8,64,512]{2,1,0:T(8,128)} %shard_map.58), calls=%async_computation.1 | async-start | bytes 2097152 | tf_op jit(solution)/shard_map/all_to_all | solution.py:424
  45.7 2.4 %collective-permute-start.9 = (f32[128,256]{1,0:T(8,128)S(1)}, f32[128,256]{1,0:T(8,128)S(1)}, u32[]{:S(2)}, u32[]{:S(2)}) collective-permute-start(f32[128,256]{1,0:T(8,128)S(1)} %get-tuple-element.39), channel_id=1, source_target_pairs={{0,6},{2,0},{4,2},{6,4},{1,7},{3,1},{5,3},{7,5},{8,14},{10,8},{12,... | collective-permute-start | bytes 393224 | tf_op jit(solution)/shard_map/ppermute | solution.py:379
  48.8 2.9 %collective-permute-done.9 = f32[128,256]{1,0:T(8,128)S(1)} collective-permute-done((f32[128,256]{1,0:T(8,128)S(1)}, f32[128,256]{1,0:T(8,128)S(1)}, u32[]{:S(2)}, u32[]{:S(2)}) %collective-permute-start.9) | collective-permute-done | bytes 131104 | tf_op jit(solution)/shard_map/ppermute | solution.py:379
  51.7 1.9 %collective-permute-done.8 = f32[128,256]{1,0:T(8,128)S(1)} collective-permute-done((f32[128,256]{1,0:T(8,128)S(1)}, f32[128,256]{1,0:T(8,128)S(1)}, u32[]{:S(2)}, u32[]{:S(2)}) %collective-permute-start.8) | collective-permute-done | bytes 131104 | tf_op jit(solution)/shard_map/ppermute | solution.py:379
  53.6 1.7 %collective-permute-done.7 = f32[128,256]{1,0:T(8,128)S(1)} collective-permute-done((f32[128,256]{1,0:T(8,128)S(1)}, f32[128,256]{1,0:T(8,128)S(1)}, u32[]{:S(2)}, u32[]{:S(2)}) %collective-permute-start.7) | collective-permute-done | bytes 131104 | tf_op jit(solution)/shard_map/ppermute | solution.py:379
  55.3 3.2 %collective-permute-start.10 = (f32[4,128,256]{2,1,0:T(8,128)S(1)}, f32[4,128,256]{2,1,0:T(8,128)S(1)}, u32[]{:S(2)}, u32[]{:S(2)}) collective-permute-start(f32[4,128,256]{2,1,0:T(8,128)S(1)} %pad_maximum_fusion.1.owns), channel_id=1, source_target_pairs={{0,1},{1,0},{2,3},{3,2},{4,5},{5,4},{6,7},{7,6},{8,9},{9,8},{10,11... | collective-permute-start | bytes 1572872 | tf_op jit(solution)/shard_map/ppermute | solution.py:379
  60.0 13.3 %all-to-all-done.1.pieces = f32[8,64,512]{2,1,0:T(8,128)S(1)} async-done(((f32[8,64,512]{2,1,0:T(8,128)}), f32[8,64,512]{2,1,0:T(8,128)S(1)}, u32[]{:S(2)}, u32[]{:S(2)}) %all-to-all-start.1) | async-done | bytes 1048608 | tf_op jit(solution)/shard_map/all_to_all | solution.py:424
  74.9 2.3 %collective-permute-start.12 = (f32[32,512]{1,0:T(8,128)S(1)}, f32[32,512]{1,0:T(8,128)S(1)}, u32[]{:S(2)}, u32[]{:S(2)}) collective-permute-start(f32[32,512]{1,0:T(8,128)S(1)} %get-tuple-element.42), channel_id=1, source_target_pairs={{0,16},{8,24},{16,0},{24,8},{1,17},{9,25},{17,1},{25,9},{2,18},{10... | collective-permute-start | bytes 196616 | tf_op jit(solution)/shard_map/ppermute | solution.py:379
  77.2 2.7 %collective-permute-start.18 = (f32[8,32,512]{2,1,0:T(8,128)S(1)}, f32[8,32,512]{2,1,0:T(8,128)S(1)}, u32[]{:S(2)}, u32[]{:S(2)}) collective-permute-start(f32[8,32,512]{2,1,0:T(8,128)S(1)} %get-tuple-element.41.part0), channel_id=1, source_target_pairs={{0,24},{8,0},{16,8},{24,16},{1,25},{9,1},{17,9},{25,17},{2,26},{10... | collective-permute-start | bytes 1572872 | tf_op jit(solution)/shard_map/ppermute | solution.py:379
  79.9 1.6 %collective-permute-done.11 = f32[32,512]{1,0:T(8,128)S(1)} collective-permute-done((f32[32,512]{1,0:T(8,128)S(1)}, f32[32,512]{1,0:T(8,128)S(1)}, u32[]{:S(2)}, u32[]{:S(2)}) %collective-permute-start.11) | collective-permute-done | bytes 65568 | tf_op jit(solution)/shard_map/ppermute | solution.py:379
  81.6 3.0 %collective-permute-start.15 = (f32[4,32,512]{2,1,0:T(8,128)S(1)}, f32[4,32,512]{2,1,0:T(8,128)S(1)}, u32[]{:S(2)}, u32[]{:S(2)}) collective-permute-start(f32[4,32,512]{2,1,0:T(8,128)S(1)} %get-tuple-element.52), channel_id=1, source_target_pairs={{0,4},{2,6},{4,0},{6,2},{1,5},{3,7},{5,1},{7,3},{8,12},{10,14},{12... | collective-permute-start | bytes 786440 | tf_op jit(solution)/shard_map/ppermute | solution.py:379
  85.0 2.3 %collective-permute-start.16 = (f32[4,32,512]{2,1,0:T(8,128)S(1)}, f32[4,32,512]{2,1,0:T(8,128)S(1)}, u32[]{:S(2)}, u32[]{:S(2)}) collective-permute-start(f32[4,32,512]{2,1,0:T(8,128)S(1)} %get-tuple-element.52), channel_id=1, source_target_pairs={{0,6},{2,0},{4,2},{6,4},{1,7},{3,1},{5,3},{7,5},{8,14},{10,8},{12,... | collective-permute-start | bytes 786440 | tf_op jit(solution)/shard_map/ppermute | solution.py:379
  88.4 6.8 %collective-permute-done.14 = f32[4,32,512]{2,1,0:T(8,128)S(1)} collective-permute-done((f32[4,32,512]{2,1,0:T(8,128)S(1)}, f32[4,32,512]{2,1,0:T(8,128)S(1)}, u32[]{:S(2)}, u32[]{:S(2)}) %collective-permute-start.14) | collective-permute-done | bytes 262176 | tf_op jit(solution)/shard_map/ppermute | solution.py:379
  95.4 2.7 %collective-permute-start.20 = (f32[4,4,32,512]{3,2,1,0:T(8,128)S(1)}, f32[4,4,32,512]{3,2,1,0:T(8,128)S(1)}, u32[]{:S(2)}, u32[]{:S(2)}) collective-permute-start(f32[4,4,32,512]{3,2,1,0:T(8,128)S(1)} %pad_maximum_fusion.few), channel_id=1, source_target_pairs={{0,1},{1,0},{2,3},{3,2},{4,5},{5,4},{6,7},{7,6},{8,9},{9,8},{10,11... | collective-permute-start | bytes 3145736 | tf_op jit(solution)/shard_map/ppermute | solution.py:379
  98.4 2.0 %collective-permute-done.20.few_other = f32[4,4,32,512]{3,2,1,0:T(8,128)S(1)} collective-permute-done((f32[4,4,32,512]{3,2,1,0:T(8,128)S(1)}, f32[4,4,32,512]{3,2,1,0:T(8,128)S(1)}, u32[]{:S(2)}, u32[]{:S(2)}) %collective-permute-start.20) | collective-permute-done | bytes 1048608 | tf_op jit(solution)/shard_map/ppermute | solution.py:379
  100.4 13.6 %shard_map.60 = (f32[512,512]{1,0:T(8,128)S(1)}, f32[512,256]{1,0:T(8,128)S(1)}, bf16[512,256]{1,0:T(8,128)(2,1)S(1)}, bf16[512,256]{1,0:T(8,128)(2,1)S(1)}) custom-call(s32[5]{0:T(128)S(1)} %stack.68.pos, s32[4]{0:T(128)S(1)} %copy-done.3, f32[4,4,32,512]{3,2,1,0:T(8,128)S(1)} %pad_maximum_fusion.few, ...), custom_call_target="tpu_custom_call" | custom-call | tf_op jit(solution)/shard_map/pallas_call | solution.py:368
  114.0 3.9 %shard_map.61 = f32[2048,128]{1,0:T(8,128)} custom-call(s32[5]{0:T(128)S(1)} %stack.68.pos, s32[4]{0:T(128)S(1)} %copy-done.3, s32[1,512]{1,0:T(1,128)S(1)} %bitcast.32, f32[1024,256]{1,0:T(8,128)S(1)} %get-tuple-element.28.rows, f32[8,32,512]{2,1,0:T(8,128)S(1)} %get-tuple-element.41.part0, f32[8,32,512]{2,1,0:T(8,128)S(1)} %collective-permute-done.17.part1, ...), custom_call_target="tpu_custom_call" | custom-call | tf_op jit(solution)/shard_map/pallas_call | solution.py:368
  (44 shorter events, 18.8 us)
Async XLA Ops:
  0.0 13.0 %copy-start = (f32[8,1,128,2,1,128]{5,4,3,2,1,0:T(1,128)S(1)}, f32[8,1,128,2,1,128]{5,4,3,2,1,0:T(1,128)}, u32[]{:S(2)}) copy-start(f32[8,1,128,2,1,128]{5,4,3,2,1,0:T(1,128)} %param.5) | copy-start | bytes 3145732
  0.0 38.2 %all-to-all-start = ((f32[32,64,128]{2,1,0:T(8,128)}), f32[32,64,128]{2,1,0:T(8,128)S(1)}, u32[]{:S(2)}, u32[]{:S(2)}) async-start(f32[32,64,128]{2,1,0:T(8,128)} %bitcast.25), calls=%async_computation | async-start | bytes 2097152 | tf_op jit(solution)/shard_map/all_to_all | solution.py:398
  16.3 2.6 %collective-permute-start = (f32[4,128,256]{2,1,0:T(8,128)S(1)}, f32[4,128,256]{2,1,0:T(8,128)S(1)}, u32[]{:S(2)}, u32[]{:S(2)}) collective-permute-start(f32[4,128,256]{2,1,0:T(8,128)S(1)} %get-tuple-element.30), channel_id=1, source_target_pairs={{0,1},{1,0},{2,3},{3,2},{4,5},{5,4},{6,7},{7,6},{8,9},{9,8},{10,11... | collective-permute-start | bytes 1572872 | tf_op jit(solution)/shard_map/ppermute | solution.py:379
  18.9 6.1 %collective-permute-start.1 = (f32[128,256]{1,0:T(8,128)S(1)}, f32[128,256]{1,0:T(8,128)S(1)}, u32[]{:S(2)}, u32[]{:S(2)}) collective-permute-start(f32[128,256]{1,0:T(8,128)S(1)} %get-tuple-element.32), channel_id=1, source_target_pairs={{0,2},{2,4},{4,6},{6,0},{1,3},{3,5},{5,7},{7,1},{8,10},{10,12},{12... | collective-permute-start | bytes 393224 | tf_op jit(solution)/shard_map/ppermute | solution.py:379
  20.3 8.7 %collective-permute-start.2 = (f32[128,256]{1,0:T(8,128)S(1)}, f32[128,256]{1,0:T(8,128)S(1)}, u32[]{:S(2)}, u32[]{:S(2)}) collective-permute-start(f32[128,256]{1,0:T(8,128)S(1)} %get-tuple-element.33), channel_id=1, source_target_pairs={{0,4},{2,6},{4,0},{6,2},{1,5},{3,7},{5,1},{7,3},{8,12},{10,14},{12... | collective-permute-start | bytes 393224 | tf_op jit(solution)/shard_map/ppermute | solution.py:379
  22.9 6.1 %collective-permute-start.3 = (f32[128,256]{1,0:T(8,128)S(1)}, f32[128,256]{1,0:T(8,128)S(1)}, u32[]{:S(2)}, u32[]{:S(2)}) collective-permute-start(f32[128,256]{1,0:T(8,128)S(1)} %get-tuple-element.34), channel_id=1, source_target_pairs={{0,6},{2,0},{4,2},{6,4},{1,7},{3,1},{5,3},{7,5},{8,14},{10,8},{12,... | collective-permute-start | bytes 393224 | tf_op jit(solution)/shard_map/ppermute | solution.py:379
  29.6 5.2 %collective-permute-start.4 = (f32[32,256]{1,0:T(8,128)S(1)}, f32[32,256]{1,0:T(8,128)S(1)}, u32[]{:S(2)}, u32[]{:S(2)}) collective-permute-start(f32[32,256]{1,0:T(8,128)S(1)} %get-tuple-element.36), channel_id=1, source_target_pairs={{0,8},{8,16},{16,24},{24,0},{1,9},{9,17},{17,25},{25,1},{2,10},{10... | collective-permute-start | bytes 98312 | tf_op jit(solution)/shard_map/ppermute | solution.py:379
  31.2 4.7 %collective-permute-start.5 = (f32[32,256]{1,0:T(8,128)S(1)}, f32[32,256]{1,0:T(8,128)S(1)}, u32[]{:S(2)}, u32[]{:S(2)}) collective-permute-start(f32[32,256]{1,0:T(8,128)S(1)} %get-tuple-element.37), channel_id=1, source_target_pairs={{0,16},{8,24},{16,0},{24,8},{1,17},{9,25},{17,1},{25,9},{2,18},{10... | collective-permute-start | bytes 98312 | tf_op jit(solution)/shard_map/ppermute | solution.py:379
  33.6 3.5 %collective-permute-start.6 = (f32[32,256]{1,0:T(8,128)S(1)}, f32[32,256]{1,0:T(8,128)S(1)}, u32[]{:S(2)}, u32[]{:S(2)}) collective-permute-start(f32[32,256]{1,0:T(8,128)S(1)} %get-tuple-element.38), channel_id=1, source_target_pairs={{0,24},{8,0},{16,8},{24,16},{1,25},{9,1},{17,9},{25,17},{2,26},{10... | collective-permute-start | bytes 98312 | tf_op jit(solution)/shard_map/ppermute | solution.py:379
  40.4 32.9 %all-to-all-start.1 = ((f32[8,64,512]{2,1,0:T(8,128)}), f32[8,64,512]{2,1,0:T(8,128)S(1)}, u32[]{:S(2)}, u32[]{:S(2)}) async-start(f32[8,64,512]{2,1,0:T(8,128)} %shard_map.58), calls=%async_computation.1 | async-start | bytes 2097152 | tf_op jit(solution)/shard_map/all_to_all | solution.py:424
  45.7 6.0 %collective-permute-start.9 = (f32[128,256]{1,0:T(8,128)S(1)}, f32[128,256]{1,0:T(8,128)S(1)}, u32[]{:S(2)}, u32[]{:S(2)}) collective-permute-start(f32[128,256]{1,0:T(8,128)S(1)} %get-tuple-element.39), channel_id=1, source_target_pairs={{0,6},{2,0},{4,2},{6,4},{1,7},{3,1},{5,3},{7,5},{8,14},{10,8},{12,... | collective-permute-start | bytes 393224 | tf_op jit(solution)/shard_map/ppermute | solution.py:379
  48.1 5.4 %collective-permute-start.8 = (f32[128,256]{1,0:T(8,128)S(1)}, f32[128,256]{1,0:T(8,128)S(1)}, u32[]{:S(2)}, u32[]{:S(2)}) collective-permute-start(f32[128,256]{1,0:T(8,128)S(1)} %get-tuple-element.39), channel_id=1, source_target_pairs={{0,4},{2,6},{4,0},{6,2},{1,5},{3,7},{5,1},{7,3},{8,12},{10,14},{12... | collective-permute-start | bytes 393224 | tf_op jit(solution)/shard_map/ppermute | solution.py:379
  48.5 6.8 %collective-permute-start.7 = (f32[128,256]{1,0:T(8,128)S(1)}, f32[128,256]{1,0:T(8,128)S(1)}, u32[]{:S(2)}, u32[]{:S(2)}) collective-permute-start(f32[128,256]{1,0:T(8,128)S(1)} %get-tuple-element.39), channel_id=1, source_target_pairs={{0,2},{2,4},{4,6},{6,0},{1,3},{3,5},{5,7},{7,1},{8,10},{10,12},{12... | collective-permute-start | bytes 393224 | tf_op jit(solution)/shard_map/ppermute | solution.py:379
  55.3 4.7 %collective-permute-start.10 = (f32[4,128,256]{2,1,0:T(8,128)S(1)}, f32[4,128,256]{2,1,0:T(8,128)S(1)}, u32[]{:S(2)}, u32[]{:S(2)}) collective-permute-start(f32[4,128,256]{2,1,0:T(8,128)S(1)} %pad_maximum_fusion.1.owns), channel_id=1, source_target_pairs={{0,1},{1,0},{2,3},{3,2},{4,5},{5,4},{6,7},{7,6},{8,9},{9,8},{10,11... | collective-permute-start | bytes 1572872 | tf_op jit(solution)/shard_map/ppermute | solution.py:379
  73.4 6.5 %collective-permute-start.13 = (f32[32,512]{1,0:T(8,128)S(1)}, f32[32,512]{1,0:T(8,128)S(1)}, u32[]{:S(2)}, u32[]{:S(2)}) collective-permute-start(f32[32,512]{1,0:T(8,128)S(1)} %get-tuple-element.42), channel_id=1, source_target_pairs={{0,24},{8,0},{16,8},{24,16},{1,25},{9,1},{17,9},{25,17},{2,26},{10... | collective-permute-start | bytes 196616 | tf_op jit(solution)/shard_map/ppermute | solution.py:379
  74.9 5.0 %collective-permute-start.12 = (f32[32,512]{1,0:T(8,128)S(1)}, f32[32,512]{1,0:T(8,128)S(1)}, u32[]{:S(2)}, u32[]{:S(2)}) collective-permute-start(f32[32,512]{1,0:T(8,128)S(1)} %get-tuple-element.42), channel_id=1, source_target_pairs={{0,16},{8,24},{16,0},{24,8},{1,17},{9,25},{17,1},{25,9},{2,18},{10... | collective-permute-start | bytes 196616 | tf_op jit(solution)/shard_map/ppermute | solution.py:379
  77.2 4.3 %collective-permute-start.11 = (f32[32,512]{1,0:T(8,128)S(1)}, f32[32,512]{1,0:T(8,128)S(1)}, u32[]{:S(2)}, u32[]{:S(2)}) collective-permute-start(f32[32,512]{1,0:T(8,128)S(1)} %get-tuple-element.42), channel_id=1, source_target_pairs={{0,8},{8,16},{16,24},{24,0},{1,9},{9,17},{17,25},{25,1},{2,10},{10... | collective-permute-start | bytes 196616 | tf_op jit(solution)/shard_map/ppermute | solution.py:379
  77.2 18.2 %collective-permute-start.18 = (f32[8,32,512]{2,1,0:T(8,128)S(1)}, f32[8,32,512]{2,1,0:T(8,128)S(1)}, u32[]{:S(2)}, u32[]{:S(2)}) collective-permute-start(f32[8,32,512]{2,1,0:T(8,128)S(1)} %get-tuple-element.41.part0), channel_id=1, source_target_pairs={{0,24},{8,0},{16,8},{24,16},{1,25},{9,1},{17,9},{25,17},{2,26},{10... | collective-permute-start | bytes 1572872 | tf_op jit(solution)/shard_map/ppermute | solution.py:379
  79.9 15.5 %collective-permute-start.17 = (f32[8,32,512]{2,1,0:T(8,128)S(1)}, f32[8,32,512]{2,1,0:T(8,128)S(1)}, u32[]{:S(2)}, u32[]{:S(2)}) collective-permute-start(f32[8,32,512]{2,1,0:T(8,128)S(1)} %get-tuple-element.41.part0), channel_id=1, source_target_pairs={{0,8},{8,16},{16,24},{24,0},{1,9},{9,17},{17,25},{25,1},{2,10},{10... | collective-permute-start | bytes 1572872 | tf_op jit(solution)/shard_map/ppermute | solution.py:379
  81.6 6.8 %collective-permute-start.15 = (f32[4,32,512]{2,1,0:T(8,128)S(1)}, f32[4,32,512]{2,1,0:T(8,128)S(1)}, u32[]{:S(2)}, u32[]{:S(2)}) collective-permute-start(f32[4,32,512]{2,1,0:T(8,128)S(1)} %get-tuple-element.52), channel_id=1, source_target_pairs={{0,4},{2,6},{4,0},{6,2},{1,5},{3,7},{5,1},{7,3},{8,12},{10,14},{12... | collective-permute-start | bytes 786440 | tf_op jit(solution)/shard_map/ppermute | solution.py:379
  84.6 10.7 %collective-permute-start.14 = (f32[4,32,512]{2,1,0:T(8,128)S(1)}, f32[4,32,512]{2,1,0:T(8,128)S(1)}, u32[]{:S(2)}, u32[]{:S(2)}) collective-permute-start(f32[4,32,512]{2,1,0:T(8,128)S(1)} %get-tuple-element.52), channel_id=1, source_target_pairs={{0,2},{2,4},{4,6},{6,0},{1,3},{3,5},{5,7},{7,1},{8,10},{10,12},{12... | collective-permute-start | bytes 786440 | tf_op jit(solution)/shard_map/ppermute | solution.py:379
  85.0 10.3 %collective-permute-start.16 = (f32[4,32,512]{2,1,0:T(8,128)S(1)}, f32[4,32,512]{2,1,0:T(8,128)S(1)}, u32[]{:S(2)}, u32[]{:S(2)}) collective-permute-start(f32[4,32,512]{2,1,0:T(8,128)S(1)} %get-tuple-element.52), channel_id=1, source_target_pairs={{0,6},{2,0},{4,2},{6,4},{1,7},{3,1},{5,3},{7,5},{8,14},{10,8},{12,... | collective-permute-start | bytes 786440 | tf_op jit(solution)/shard_map/ppermute | solution.py:379
  95.4 5.0 %collective-permute-start.20 = (f32[4,4,32,512]{3,2,1,0:T(8,128)S(1)}, f32[4,4,32,512]{3,2,1,0:T(8,128)S(1)}, u32[]{:S(2)}, u32[]{:S(2)}) collective-permute-start(f32[4,4,32,512]{3,2,1,0:T(8,128)S(1)} %pad_maximum_fusion.few), channel_id=1, source_target_pairs={{0,1},{1,0},{2,3},{3,2},{4,5},{5,4},{6,7},{7,6},{8,9},{9,8},{10,11... | collective-permute-start | bytes 3145736 | tf_op jit(solution)/shard_map/ppermute | solution.py:379
  98.1 15.9 %collective-permute-start.19 = (f32[8,32,512]{2,1,0:T(8,128)S(1)}, f32[8,32,512]{2,1,0:T(8,128)S(1)}, u32[]{:S(2)}, u32[]{:S(2)}) collective-permute-start(f32[8,32,512]{2,1,0:T(8,128)S(1)} %get-tuple-element.41.part0), channel_id=1, source_target_pairs={{0,16},{8,24},{16,0},{24,8},{1,17},{9,25},{17,1},{25,9},{2,18},{10... | collective-permute-start | bytes 1572872 | tf_op jit(solution)/shard_map/ppermute | solution.py:379
  (4 other events, 2.8 us)

commit v4 on v3

--- a/solution.py
+++ b/solution.py
@@ -118,9 +118,7 @@
         chunks[u][count:, :] = total[pl.ds(pl.multiple_of(S // N_PROW + start, count), count), :]
 
 
-def select_kernel(
-    pos, order, width, pattern, target_row, spread, chunk0, chunk1, chunk2, chunk3, out
-):
+def select_kernel(pos, order, width, pattern, target_row, spread, out):
     r = pos[0]
     z = pos[2]
     x = pos[3]
@@ -129,7 +127,6 @@
     for k in range(PANELS):
         p = order[k]
         source = lax.rem(p, N_PCOL)
-        cols = slice(k * B, (k + 1) * B)
         value = jnp.where(
             p >= N_PCOL,
             spread[source, pl.ds(1, CHUNK, stride=2), :],
@@ -140,23 +137,29 @@
         )
         value = jnp.where(taken, 0.0, value)
         for j in range(NZ):
-            out[j, :CHUNK, cols] = value
+            out[j, :, k * B : (k + 1) * B] = value
+
+
+def select_few_kernel(pos, order, chunk0, chunk1, chunk2, chunk3, out):
+    z = pos[2]
+    x = pos[3]
+    for k in range(PANELS):
+        p = order[k]
+        source = lax.rem(p, N_PCOL)
         value = jnp.zeros((CHUNK, B), F32)
         for u, chunk in enumerate((chunk0, chunk1, chunk2, chunk3)):
             here = source == z * NX + lax.rem(x - u + NX, NX)
             value = jnp.where(here & (p < N_PCOL), chunk[:, :B], value)
             value = jnp.where(here & (p >= N_PCOL), chunk[:, B:], value)
-        for j in range(NZ):
-            out[j, CHUNK:, cols] = value
-
-
-def split_kernel(pieces, strips, rows):
-    value = pieces[0, CHUNK:, :]
-    for i in range(1, NZ):
-        value = value + pieces[i, CHUNK:, :]
-    rows[...] = value
-    for i in range(NZ):
-        strips[i] = pieces[i, :CHUNK, :]
+        out[:, k * B : (k + 1) * B] = value
+
+
+def add_two_kernel(a, b, out):
+    out[...] = a[...] + b[...]
+
+
+def add_four_kernel(a, b, c, d, out):
+    out[...] = (a[...] + b[...]) + (c[...] + d[...])
 
 
 def panel_order_rows(pos, same_core, other_core, first, out):
@@ -169,11 +172,12 @@
         for core, group in ((c, same_core), (1 - c, other_core)):
             for j in range(NX):
                 other_x = lax.rem(x - j + NX, NX)
-                start = ((other_y * NC + core) * NX + other_x) * count
-                out[pl.ds(pl.multiple_of(start, count), count), :] = group[u, j, first : first + count, :]
-
-
-def prow_order(pos, same_core, other_core, first, out):
+                start = pl.multiple_of(((other_y * NC + core) * NX + other_x) * count, count)
+                rows = slice(j * CHUNK + first, j * CHUNK + first + count)
+                out[pl.ds(start, count), :] = group[u, rows, :S]
+
+
+def own_order_rows(pos, same_core, other_core, first, out):
     c = pos[4]
     y = lax.div(pos[0], NC)
     part = S // N_PROW
@@ -181,7 +185,7 @@
         other_y = lax.rem(y - u + NY, NY)
         for core, group in ((c, same_core), (1 - c, other_core)):
             start = pl.multiple_of((other_y * NC + core) * part, part)
-            out[pl.ds(start, part), :] = group[u, first : first + part, :]
+            out[pl.ds(start, part), :] = group[u, first : first + part, S:]
 
 
 def panels_here(pos, order):
@@ -260,12 +264,12 @@
 
 
 def corner_kernel(
-    pos, order, few, few_other, owns, owns_other,
+    pos, order, few, few_other,
     factor, upper, steps_high, steps_low, inverses, work, solver, steps, pivot_rows,
 ):
     def eliminate(invert_block):
         panel_order_rows(pos, few, few_other, 0, factor)
-        prow_order(pos, owns, owns_other, 0, upper)
+        own_order_rows(pos, few, few_other, 0, upper)
         solver[...] = jnp.zeros((S, S), F32)
         error = jnp.float32(0.0)
         for k in range(PANELS):
@@ -311,7 +315,7 @@
 
 
 def update_kernel(
-    pos, order, target_row, rows, part0, part1, part2, part3, few, few_other, owns, owns_other,
+    pos, order, target_row, rows, part0, part1, part2a, part2b, part3, few, few_other,
     factor, upper, steps_high, steps_low,
     out, taken, home_rows, homes,
 ):
@@ -321,7 +325,7 @@
     steps_parts = (steps_high[...], steps_low[...])
     found = panels_here(pos, order)
     panel_order_rows(pos, few, few_other, CHUNK // 2, home_rows)
-    prow_order(pos, owns, owns_other, S // N_PROW, homes)
+    own_order_rows(pos, few, few_other, S // N_PROW, homes)
 
     for i in range(2):
         here = slice(i * half, (i + 1) * half)
@@ -329,8 +333,9 @@
         for s in range(2):
             cols = slice(s * B, (s + 1) * B)
             homes[here, cols] = jnp.where(found[s] >= 0, 0.0, homes[here, cols]) - product[:, cols]
-    for u, part in enumerate((part0, part1, part2, part3)):
-        product = dot3(split2(part[...].reshape(NZ * CHUNK, S)), steps_parts)
+    part2 = jnp.concatenate([part2a[...], part2b[...]], axis=0)
+    for u, part in enumerate((part0[...], part1[...], part2, part3[...])):
+        product = dot3(split2(part.reshape(NZ * CHUNK, S)), steps_parts)
         other_x = lax.rem(x - u + NX, NX)
         for i in range(NZ):
             place = pl.ds(pl.multiple_of(i * B + other_x * CHUNK, CHUNK), CHUNK)
@@ -415,23 +420,29 @@
         [],
     )
     chunks = [chunks[0]] + [shift(chunks[u], "x", NX, u) for u in range(1, NX)]
-    owns = gather(total, "y", NY)
-    owns_other = shift(owns, "c", NC, 1)
-
-    (pieces,) = call(
-        select_kernel, where, [target_row, spread, *chunks], [(F32, (NZ, 2 * CHUNK, S))], []
-    )
-    pieces = lax.all_to_all(pieces, "z", 0, 0)
-    pieces, owns_other = lax.optimization_barrier((pieces, owns_other))
-    strips, few = call(split_kernel, [], [pieces], [(F32, (NZ, CHUNK, S)), (F32, (CHUNK, S))], [])
-    parts = [strips] + [shift(strips, "x", NX, u) for u in range(1, NX)]
-    few = gather(gather(few, "x", NX), "y", NY)
-    few, parts[1], parts[3] = lax.optimization_barrier((few, parts[1], parts[3]))
+
+    (few,) = call(select_few_kernel, [pos, panel_order], chunks, [(F32, (CHUNK, S))], [])
+    near = lax.ppermute(few, "z", [(i, i ^ 1) for i in range(NZ)])
+    (few,) = call(add_two_kernel, [], [few, near], [(F32, (CHUNK, S))], [])
+    (strip,) = call(select_kernel, where, [target_row, spread], [(F32, (NZ, CHUNK, S))], [])
+    few, strip = lax.optimization_barrier((few, strip))
+    far = [shift(few, "z", NZ, i) for i in (2, 4, 6)]
+    (few,) = call(add_four_kernel, [], [few, *far], [(F32, (CHUNK, S))], [])
+    few, strip = lax.optimization_barrier((few, strip))
+    strips = lax.all_to_all(strip, "z", 0, 0)
+    few = gather(few, "x", NX)
+    part1 = shift(strips, "x", NX, 1)
+    part3 = shift(strips, "x", NX, 3)
+    few = jnp.concatenate([few.reshape(NX * CHUNK, S), total], axis=1)
+    few = gather(few, "y", NY)
+    few, part1, part3 = lax.optimization_barrier((few, part1, part3))
     few_other = shift(few, "c", NC, 1)
+    half = NZ // 2
+    parts = [strips, part1, shift(part1[:half], "x", NX, 1), shift(part3[half:], "x", NX, 3), part3]
     solved = call(
         corner_kernel,
         [pos, panel_order],
-        [few, few_other, owns, owns_other],
+        [few, few_other],
         [(F32, (S, S)), (F32, (S, 2 * B)), (BF16, (S, 2 * B)), (BF16, (S, 2 * B))],
         [
             pltpu.VMEM((B, B), F32),
@@ -444,7 +455,7 @@
     (out,) = call(
         update_kernel,
         [pos, panel_order],
-        [target_row, rows, *parts, few, few_other, owns, owns_other, *solved],
+        [target_row, rows, *parts, few, few_other, *solved],
         [(F32, (ROWS * 2, B))],
         [pltpu.VMEM((ROWS, 2 * B), F32), pltpu.VMEM((S, S), F32), pltpu.VMEM((S, 2 * B), F32)],
     )

time: 119 us -> 103 us (0.87)
  waiting for transfers between devices: 42.9 us -> 31.6 us
  Pallas kernels: 23 us -> 16.3 us
  starting transfers between devices: 50 us -> 53.6 us
  local copies, waits for them, and re-layouts: 1.58 us -> 0.29 us
    all_to_all x1, waiting for transfers between devices: 13.3 us -> 0.01 us  [body(): strips = lax.all_to_all(strip, 'z', 0, 0)]
    pallas_call x7 -> x9, Pallas kernels: 23 us -> 16.3 us  [call(): pl.pallas_call(kernel, out_shape=[jax.ShapeDtypeStruct(shape, kind) for k...]
    ppermute x21, starting transfers between devices: 32.7 us -> 36.8 us  [shift(): lax.ppermute(value, axis, [(i, (i + by) % size) for i in range(size)])]
    ppermute x0 -> x1, waiting for transfers between devices: none -> 2.32 us  [body(): near = lax.ppermute(few, 'z', [(i, i ^ 1) for i in range(NZ)])]
    all_to_all x1, starting transfers between devices: 5.31 us -> 3.57 us  [body(): strips = lax.all_to_all(strip, 'z', 0, 0)]
    unnamed x10, local copies, waits for them, and re-layouts: 1.35 us -> 0.02 us
  transfers between devices with their start and end apart: 23 -> 24, of which waited for: 15 -> 16; matrix products, arithmetic and copies ran while one was open for 0% -> 1% of each run, Pallas kernels for 14% -> 10%
where the time goes in v4:
time: 103 us
  starting transfers between devices  53.6 us (52%)
  waiting for transfers between devices  31.6 us (31%)
  Pallas kernels  16.3 us (16%)
    ppermute x21, starting transfers between devices, shift(): lax.ppermute(value, axis, [(i, (i + by) % size) for i in range(size)])  36.8 us
    ppermute x21, waiting for transfers between devices, shift(): lax.ppermute(value, axis, [(i, (i + by) % size) for i in range(size)])  29.3 us
    pallas_call x9, Pallas kernels, call(): pl.pallas_call(kernel, out_shape=[jax.ShapeDtypeStruct(shape, kind) for k...  16.3 us
    all_to_all x1, starting transfers between devices, body(): spread = lax.all_to_all(raw.reshape(N_PCOL, CHUNK * 2, B), ('z', 'x'), 0, 0)  12 us
    all_to_all x1, starting transfers between devices, body(): strips = lax.all_to_all(strip, 'z', 0, 0)  3.57 us
    ppermute x1, waiting for transfers between devices, body(): near = lax.ppermute(few, 'z', [(i, i ^ 1) for i in range(NZ)])  2.32 us
  transfers between devices with their start and end apart: 24, of which 16 were waited for; matrix products, arithmetic and copies ran while one was open for 1% of the time, Pallas kernels for 10%

profile of v4, /device:TPU:1, one launch (start us, length us, event | category | flops | bytes accessed | tf_op | source)
XLA Modules:
  0.0 102.9 jit_solution(9650517704095163352)
XLA Ops:
  0.0 12.0 %all-to-all-start = ((f32[32,64,128]{2,1,0:T(8,128)}), f32[32,64,128]{2,1,0:T(8,128)S(1)}, u32[]{:S(2)}, u32[]{:S(2)}) async-start(f32[32,64,128]{2,1,0:T(8,128)} %bitcast.22), calls=%async_computation | async-start | bytes 2097152 | tf_op jit(solution)/shard_map/all_to_all | solution.py:403
  12.3 2.7 %shard_map.55 = (f32[4,128,256]{2,1,0:T(8,128)S(1)}, f32[4,128,256]{2,1,0:T(8,128)S(1)}, f32[1024,256]{1,0:T(8,128)S(1)}) custom-call(s32[5]{0:T(128)S(1)} %stack.53.pos, s32[4]{0:T(128)S(1)} %copy-done.3, s32[64]{0:T(128)S(1)} %copy-done.4, s32[64,64]{1,0:T(8,128)S(1)} %copy-done.1, s32[512,1]{1,0:T(8,128)S(1)} %copy.7.target_col, s32[1,512]{1,0:T(1,128)S(1)} %bitcast.26, ...), custom_call_target="tpu_custom_call" | custom-call | tf_op jit(solution)/shard_map/pallas_call | solution.py:373
  19.0 2.6 %collective-permute-start.2 = (f32[128,256]{1,0:T(8,128)S(1)}, f32[128,256]{1,0:T(8,128)S(1)}, u32[]{:S(2)}, u32[]{:S(2)}) collective-permute-start(f32[128,256]{1,0:T(8,128)S(1)} %get-tuple-element.33), channel_id=1, source_target_pairs={{0,4},{2,6},{4,0},{6,2},{1,5},{3,7},{5,1},{7,3},{8,12},{10,14},{12... | collective-permute-start | bytes 393224 | tf_op jit(solution)/shard_map/ppermute | solution.py:384
  23.8 3.9 %collective-permute-done.2.part2 = f32[128,256]{1,0:T(8,128)S(1)} collective-permute-done((f32[128,256]{1,0:T(8,128)S(1)}, f32[128,256]{1,0:T(8,128)S(1)}, u32[]{:S(2)}, u32[]{:S(2)}) %collective-permute-start.2) | collective-permute-done | bytes 131104 | tf_op jit(solution)/shard_map/ppermute | solution.py:384
  28.3 1.6 %collective-permute-start.4 = (f32[32,256]{1,0:T(8,128)S(1)}, f32[32,256]{1,0:T(8,128)S(1)}, u32[]{:S(2)}, u32[]{:S(2)}) collective-permute-start(f32[32,256]{1,0:T(8,128)S(1)} %get-tuple-element.36), channel_id=1, source_target_pairs={{0,8},{8,16},{16,24},{24,0},{1,9},{9,17},{17,25},{25,1},{2,10},{10... | collective-permute-start | bytes 98312 | tf_op jit(solution)/shard_map/ppermute | solution.py:384
  29.9 2.4 %collective-permute-start.5 = (f32[32,256]{1,0:T(8,128)S(1)}, f32[32,256]{1,0:T(8,128)S(1)}, u32[]{:S(2)}, u32[]{:S(2)}) collective-permute-start(f32[32,256]{1,0:T(8,128)S(1)} %get-tuple-element.37), channel_id=1, source_target_pairs={{0,16},{8,24},{16,0},{24,8},{1,17},{9,25},{17,1},{25,9},{2,18},{10... | collective-permute-start | bytes 98312 | tf_op jit(solution)/shard_map/ppermute | solution.py:384
  37.4 2.3 %collective-permute-done.7.b = f32[32,512]{1,0:T(8,128)S(1)} collective-permute-done((f32[32,512]{1,0:T(8,128)S(1)}, f32[32,512]{1,0:T(8,128)S(1)}, u32[]{:S(2)}, u32[]{:S(2)}) %collective-permute-start.7) | collective-permute-done | bytes 65568 | tf_op jit(solution)/shard_map/ppermute | solution.py:425
  39.8 2.0 %shard_map.60 = f32[8,32,512]{2,1,0:T(8,128)} custom-call(s32[5]{0:T(128)S(1)} %stack.53.pos, s32[4]{0:T(128)S(1)} %copy-done.3, s32[64]{0:T(128)S(1)} %copy-done.4, s32[64,64]{1,0:T(8,128)S(1)} %copy-done.1, s32[1,512]{1,0:T(1,128)S(1)} %bitcast.27, f32[32,64,128]{2,1,0:T(8,128)S(1)} %all-to-all-done.spread), custom_call_target="tpu_custom_call" | custom-call | tf_op jit(solution)/shard_map/pallas_call | solution.py:373
  41.8 3.1 %collective-permute-start.10 = (f32[32,512]{1,0:T(8,128)S(1)}, f32[32,512]{1,0:T(8,128)S(1)}, u32[]{:S(2)}, u32[]{:S(2)}) collective-permute-start(f32[32,512]{1,0:T(8,128)S(1)} %shard_map.59.a), channel_id=1, source_target_pairs={{0,192},{32,224},{64,0},{96,32},{128,64},{160,96},{192,128},{224,1... | collective-permute-start | bytes 196616 | tf_op jit(solution)/shard_map/ppermute | solution.py:384
  44.9 3.5 %collective-permute-start.9 = (f32[32,512]{1,0:T(8,128)S(1)}, f32[32,512]{1,0:T(8,128)S(1)}, u32[]{:S(2)}, u32[]{:S(2)}) collective-permute-start(f32[32,512]{1,0:T(8,128)S(1)} %shard_map.59.a), channel_id=1, source_target_pairs={{0,128},{32,160},{64,192},{96,224},{128,0},{160,32},{192,64},{224,... | collective-permute-start | bytes 196616 | tf_op jit(solution)/shard_map/ppermute | solution.py:384
  49.2 2.9 %collective-permute-done.9.c = f32[32,512]{1,0:T(8,128)S(1)} collective-permute-done((f32[32,512]{1,0:T(8,128)S(1)}, f32[32,512]{1,0:T(8,128)S(1)}, u32[]{:S(2)}, u32[]{:S(2)}) %collective-permute-start.9) | collective-permute-done | bytes 65568 | tf_op jit(solution)/shard_map/ppermute | solution.py:384
  52.0 2.4 %collective-permute-done.8.b = f32[32,512]{1,0:T(8,128)S(1)} collective-permute-done((f32[32,512]{1,0:T(8,128)S(1)}, f32[32,512]{1,0:T(8,128)S(1)}, u32[]{:S(2)}, u32[]{:S(2)}) %collective-permute-start.8) | collective-permute-done | bytes 65568 | tf_op jit(solution)/shard_map/ppermute | solution.py:384
  54.4 3.6 %all-to-all-start.1 = ((f32[8,32,512]{2,1,0:T(8,128)}), f32[8,32,512]{2,1,0:T(8,128)S(1)}, u32[]{:S(2)}, u32[]{:S(2)}) async-start(f32[8,32,512]{2,1,0:T(8,128)} %shard_map.60), calls=%async_computation.1 | async-start | bytes 1048576 | tf_op jit(solution)/shard_map/all_to_all | solution.py:432
  58.0 1.6 %collective-permute-start.13 = (f32[32,512]{1,0:T(8,128)S(1)}, f32[32,512]{1,0:T(8,128)S(1)}, u32[]{:S(2)}, u32[]{:S(2)}) collective-permute-start(f32[32,512]{1,0:T(8,128)S(1)} %shard_map.61), channel_id=1, source_target_pairs={{0,24},{8,0},{16,8},{24,16},{1,25},{9,1},{17,9},{25,17},{2,26},{10... | collective-permute-start | bytes 196616 | tf_op jit(solution)/shard_map/ppermute | solution.py:384
  61.5 2.8 %collective-permute-done.12 = f32[32,512]{1,0:T(8,128)S(1)} collective-permute-done((f32[32,512]{1,0:T(8,128)S(1)}, f32[32,512]{1,0:T(8,128)S(1)}, u32[]{:S(2)}, u32[]{:S(2)}) %collective-permute-start.12) | collective-permute-done | bytes 65568 | tf_op jit(solution)/shard_map/ppermute | solution.py:384
  65.5 2.1 %collective-permute-start.15 = (f32[128,768]{1,0:T(8,128)}, f32[128,768]{1,0:T(8,128)S(1)}, u32[]{:S(2)}, u32[]{:S(2)}) collective-permute-start(f32[128,768]{1,0:T(8,128)} %get-tuple-element.52), channel_id=1, source_target_pairs={{0,4},{2,6},{4,0},{6,2},{1,5},{3,7},{5,1},{7,3},{8,12},{10,14},{12... | collective-permute-start | bytes 1179656 | tf_op jit(solution)/shard_map/ppermute | solution.py:384
  68.4 1.8 %collective-permute-start.16 = (f32[128,768]{1,0:T(8,128)}, f32[128,768]{1,0:T(8,128)S(1)}, u32[]{:S(2)}, u32[]{:S(2)}) collective-permute-start(f32[128,768]{1,0:T(8,128)} %get-tuple-element.52), channel_id=1, source_target_pairs={{0,6},{2,0},{4,2},{6,4},{1,7},{3,1},{5,3},{7,5},{8,14},{10,8},{12,... | collective-permute-start | bytes 1179656 | tf_op jit(solution)/shard_map/ppermute | solution.py:384
  70.2 1.6 %collective-permute-start.18 = (f32[8,32,512]{2,1,0:T(8,128)S(1)}, f32[8,32,512]{2,1,0:T(8,128)S(1)}, u32[]{:S(2)}, u32[]{:S(2)}) collective-permute-start(f32[8,32,512]{2,1,0:T(8,128)S(1)} %all-to-all-done.1.part0), channel_id=1, source_target_pairs={{0,24},{8,0},{16,8},{24,16},{1,25},{9,1},{17,9},{25,17},{2,26},{10... | collective-permute-start | bytes 1572872 | tf_op jit(solution)/shard_map/ppermute | solution.py:384
  71.8 2.1 %collective-permute-done.15 = f32[128,768]{1,0:T(8,128)S(1)} collective-permute-done((f32[128,768]{1,0:T(8,128)}, f32[128,768]{1,0:T(8,128)S(1)}, u32[]{:S(2)}, u32[]{:S(2)}) %collective-permute-start.15) | collective-permute-done | bytes 393248 | tf_op jit(solution)/shard_map/ppermute | solution.py:384
  73.9 5.2 %collective-permute-done.14 = f32[128,768]{1,0:T(8,128)S(1)} collective-permute-done((f32[128,768]{1,0:T(8,128)}, f32[128,768]{1,0:T(8,128)S(1)}, u32[]{:S(2)}, u32[]{:S(2)}) %collective-permute-start.14) | collective-permute-done | bytes 393248 | tf_op jit(solution)/shard_map/ppermute | solution.py:384
  79.8 1.6 %collective-permute-done.17.part1 = f32[8,32,512]{2,1,0:T(8,128)S(1)} collective-permute-done((f32[8,32,512]{2,1,0:T(8,128)S(1)}, f32[8,32,512]{2,1,0:T(8,128)S(1)}, u32[]{:S(2)}, u32[]{:S(2)}) %collective-permute-start.17) | collective-permute-done | bytes 524320 | tf_op jit(solution)/shard_map/ppermute | solution.py:384
  81.4 8.1 %collective-permute-start.21 = (f32[4,128,768]{2,1,0:T(8,128)S(1)}, f32[4,128,768]{2,1,0:T(8,128)S(1)}, u32[]{:S(2)}, u32[]{:S(2)}) collective-permute-start(f32[4,128,768]{2,1,0:T(8,128)S(1)} %pad_maximum_fusion.few), channel_id=1, source_target_pairs={{0,1},{1,0},{2,3},{3,2},{4,5},{5,4},{6,7},{7,6},{8,9},{9,8},{10,11... | collective-permute-start | bytes 4718600 | tf_op jit(solution)/shard_map/ppermute | solution.py:384
  92.5 6.5 %shard_map.62 = (f32[512,512]{1,0:T(8,128)S(1)}, f32[512,256]{1,0:T(8,128)S(1)}, bf16[512,256]{1,0:T(8,128)(2,1)S(1)}, bf16[512,256]{1,0:T(8,128)(2,1)S(1)}) custom-call(s32[5]{0:T(128)S(1)} %stack.53.pos, s32[4]{0:T(128)S(1)} %copy-done.3, f32[4,128,768]{2,1,0:T(8,128)S(1)} %pad_maximum_fusion.few, f32[4,128,768]{2,1,0:T(8,128)S(1)} %collective-permute-done.21.few_other), custom_call_target="tpu_custom_call" | custom-call | tf_op jit(solution)/shard_map/pallas_call | solution.py:373
  99.1 3.9 %shard_map.63 = f32[2048,128]{1,0:T(8,128)} custom-call(s32[5]{0:T(128)S(1)} %stack.53.pos, s32[4]{0:T(128)S(1)} %copy-done.3, s32[1,512]{1,0:T(1,128)S(1)} %bitcast.28, f32[1024,256]{1,0:T(8,128)S(1)} %get-tuple-element.28.rows, f32[8,32,512]{2,1,0:T(8,128)S(1)} %all-to-all-done.1.part0, f32[8,32,512]{2,1,0:T(8,128)S(1)} %collective-permute-done.17.part1, ...), custom_call_target="tpu_custom_call" | custom-call | tf_op jit(solution)/shard_map/pallas_call | solution.py:373
  (50 shorter events, 20.6 us)
Async XLA Ops:
  0.0 39.8 %all-to-all-start = ((f32[32,64,128]{2,1,0:T(8,128)}), f32[32,64,128]{2,1,0:T(8,128)S(1)}, u32[]{:S(2)}, u32[]{:S(2)}) async-start(f32[32,64,128]{2,1,0:T(8,128)} %bitcast.22), calls=%async_computation | async-start | bytes 2097152 | tf_op jit(solution)/shard_map/all_to_all | solution.py:403
  15.0 2.6 %collective-permute-start = (f32[4,128,256]{2,1,0:T(8,128)S(1)}, f32[4,128,256]{2,1,0:T(8,128)S(1)}, u32[]{:S(2)}, u32[]{:S(2)}) collective-permute-start(f32[4,128,256]{2,1,0:T(8,128)S(1)} %get-tuple-element.30), channel_id=1, source_target_pairs={{0,1},{1,0},{2,3},{3,2},{4,5},{5,4},{6,7},{7,6},{8,9},{9,8},{10,11... | collective-permute-start | bytes 1572872 | tf_op jit(solution)/shard_map/ppermute | solution.py:384
  17.6 6.1 %collective-permute-start.1 = (f32[128,256]{1,0:T(8,128)S(1)}, f32[128,256]{1,0:T(8,128)S(1)}, u32[]{:S(2)}, u32[]{:S(2)}) collective-permute-start(f32[128,256]{1,0:T(8,128)S(1)} %get-tuple-element.32), channel_id=1, source_target_pairs={{0,2},{2,4},{4,6},{6,0},{1,3},{3,5},{5,7},{7,1},{8,10},{10,12},{12... | collective-permute-start | bytes 393224 | tf_op jit(solution)/shard_map/ppermute | solution.py:384
  19.0 8.7 %collective-permute-start.2 = (f32[128,256]{1,0:T(8,128)S(1)}, f32[128,256]{1,0:T(8,128)S(1)}, u32[]{:S(2)}, u32[]{:S(2)}) collective-permute-start(f32[128,256]{1,0:T(8,128)S(1)} %get-tuple-element.33), channel_id=1, source_target_pairs={{0,4},{2,6},{4,0},{6,2},{1,5},{3,7},{5,1},{7,3},{8,12},{10,14},{12... | collective-permute-start | bytes 393224 | tf_op jit(solution)/shard_map/ppermute | solution.py:384
  21.6 6.1 %collective-permute-start.3 = (f32[128,256]{1,0:T(8,128)S(1)}, f32[128,256]{1,0:T(8,128)S(1)}, u32[]{:S(2)}, u32[]{:S(2)}) collective-permute-start(f32[128,256]{1,0:T(8,128)S(1)} %get-tuple-element.34), channel_id=1, source_target_pairs={{0,6},{2,0},{4,2},{6,4},{1,7},{3,1},{5,3},{7,5},{8,14},{10,8},{12,... | collective-permute-start | bytes 393224 | tf_op jit(solution)/shard_map/ppermute | solution.py:384
  28.3 5.2 %collective-permute-start.4 = (f32[32,256]{1,0:T(8,128)S(1)}, f32[32,256]{1,0:T(8,128)S(1)}, u32[]{:S(2)}, u32[]{:S(2)}) collective-permute-start(f32[32,256]{1,0:T(8,128)S(1)} %get-tuple-element.36), channel_id=1, source_target_pairs={{0,8},{8,16},{16,24},{24,0},{1,9},{9,17},{17,25},{25,1},{2,10},{10... | collective-permute-start | bytes 98312 | tf_op jit(solution)/shard_map/ppermute | solution.py:384
  29.9 4.6 %collective-permute-start.5 = (f32[32,256]{1,0:T(8,128)S(1)}, f32[32,256]{1,0:T(8,128)S(1)}, u32[]{:S(2)}, u32[]{:S(2)}) collective-permute-start(f32[32,256]{1,0:T(8,128)S(1)} %get-tuple-element.37), channel_id=1, source_target_pairs={{0,16},{8,24},{16,0},{24,8},{1,17},{9,25},{17,1},{25,9},{2,18},{10... | collective-permute-start | bytes 98312 | tf_op jit(solution)/shard_map/ppermute | solution.py:384
  32.3 3.4 %collective-permute-start.6 = (f32[32,256]{1,0:T(8,128)S(1)}, f32[32,256]{1,0:T(8,128)S(1)}, u32[]{:S(2)}, u32[]{:S(2)}) collective-permute-start(f32[32,256]{1,0:T(8,128)S(1)} %get-tuple-element.38), channel_id=1, source_target_pairs={{0,24},{8,0},{16,8},{24,16},{1,25},{9,1},{17,9},{25,17},{2,26},{10... | collective-permute-start | bytes 98312 | tf_op jit(solution)/shard_map/ppermute | solution.py:384
  36.3 3.5 %collective-permute-start.7 = (f32[32,512]{1,0:T(8,128)S(1)}, f32[32,512]{1,0:T(8,128)S(1)}, u32[]{:S(2)}, u32[]{:S(2)}) collective-permute-start(f32[32,512]{1,0:T(8,128)S(1)} %shard_map.58.a), channel_id=1, source_target_pairs={{0,32},{32,0},{64,96},{96,64},{128,160},{160,128},{192,224},{224,1... | collective-permute-start | bytes 196616 | tf_op jit(solution)/shard_map/ppermute | solution.py:425
  41.8 7.4 %collective-permute-start.10 = (f32[32,512]{1,0:T(8,128)S(1)}, f32[32,512]{1,0:T(8,128)S(1)}, u32[]{:S(2)}, u32[]{:S(2)}) collective-permute-start(f32[32,512]{1,0:T(8,128)S(1)} %shard_map.59.a), channel_id=1, source_target_pairs={{0,192},{32,224},{64,0},{96,32},{128,64},{160,96},{192,128},{224,1... | collective-permute-start | bytes 196616 | tf_op jit(solution)/shard_map/ppermute | solution.py:384
  44.9 7.1 %collective-permute-start.9 = (f32[32,512]{1,0:T(8,128)S(1)}, f32[32,512]{1,0:T(8,128)S(1)}, u32[]{:S(2)}, u32[]{:S(2)}) collective-permute-start(f32[32,512]{1,0:T(8,128)S(1)} %shard_map.59.a), channel_id=1, source_target_pairs={{0,128},{32,160},{64,192},{96,224},{128,0},{160,32},{192,64},{224,... | collective-permute-start | bytes 196616 | tf_op jit(solution)/shard_map/ppermute | solution.py:384
  48.3 6.1 %collective-permute-start.8 = (f32[32,512]{1,0:T(8,128)S(1)}, f32[32,512]{1,0:T(8,128)S(1)}, u32[]{:S(2)}, u32[]{:S(2)}) collective-permute-start(f32[32,512]{1,0:T(8,128)S(1)} %shard_map.59.a), channel_id=1, source_target_pairs={{0,64},{32,96},{64,128},{96,160},{128,192},{160,224},{192,0},{224,... | collective-permute-start | bytes 196616 | tf_op jit(solution)/shard_map/ppermute | solution.py:384
  54.4 15.8 %all-to-all-start.1 = ((f32[8,32,512]{2,1,0:T(8,128)}), f32[8,32,512]{2,1,0:T(8,128)S(1)}, u32[]{:S(2)}, u32[]{:S(2)}) async-start(f32[8,32,512]{2,1,0:T(8,128)} %shard_map.60), calls=%async_computation.1 | async-start | bytes 1048576 | tf_op jit(solution)/shard_map/all_to_all | solution.py:432
  58.0 3.5 %collective-permute-start.13 = (f32[32,512]{1,0:T(8,128)S(1)}, f32[32,512]{1,0:T(8,128)S(1)}, u32[]{:S(2)}, u32[]{:S(2)}) collective-permute-start(f32[32,512]{1,0:T(8,128)S(1)} %shard_map.61), channel_id=1, source_target_pairs={{0,24},{8,0},{16,8},{24,16},{1,25},{9,1},{17,9},{25,17},{2,26},{10... | collective-permute-start | bytes 196616 | tf_op jit(solution)/shard_map/ppermute | solution.py:384
  59.6 4.7 %collective-permute-start.12 = (f32[32,512]{1,0:T(8,128)S(1)}, f32[32,512]{1,0:T(8,128)S(1)}, u32[]{:S(2)}, u32[]{:S(2)}) collective-permute-start(f32[32,512]{1,0:T(8,128)S(1)} %shard_map.61), channel_id=1, source_target_pairs={{0,16},{8,24},{16,0},{24,8},{1,17},{9,25},{17,1},{25,9},{2,18},{10... | collective-permute-start | bytes 196616 | tf_op jit(solution)/shard_map/ppermute | solution.py:384
  59.6 5.0 %collective-permute-start.11 = (f32[32,512]{1,0:T(8,128)S(1)}, f32[32,512]{1,0:T(8,128)S(1)}, u32[]{:S(2)}, u32[]{:S(2)}) collective-permute-start(f32[32,512]{1,0:T(8,128)S(1)} %shard_map.61), channel_id=1, source_target_pairs={{0,8},{8,16},{16,24},{24,0},{1,9},{9,17},{17,25},{25,1},{2,10},{10... | collective-permute-start | bytes 196616 | tf_op jit(solution)/shard_map/ppermute | solution.py:384
  65.5 8.4 %collective-permute-start.15 = (f32[128,768]{1,0:T(8,128)}, f32[128,768]{1,0:T(8,128)S(1)}, u32[]{:S(2)}, u32[]{:S(2)}) collective-permute-start(f32[128,768]{1,0:T(8,128)} %get-tuple-element.52), channel_id=1, source_target_pairs={{0,4},{2,6},{4,0},{6,2},{1,5},{3,7},{5,1},{7,3},{8,12},{10,14},{12... | collective-permute-start | bytes 1179656 | tf_op jit(solution)/shard_map/ppermute | solution.py:384
  67.5 11.6 %collective-permute-start.14 = (f32[128,768]{1,0:T(8,128)}, f32[128,768]{1,0:T(8,128)S(1)}, u32[]{:S(2)}, u32[]{:S(2)}) collective-permute-start(f32[128,768]{1,0:T(8,128)} %get-tuple-element.52), channel_id=1, source_target_pairs={{0,2},{2,4},{4,6},{6,0},{1,3},{3,5},{5,7},{7,1},{8,10},{10,12},{12... | collective-permute-start | bytes 1179656 | tf_op jit(solution)/shard_map/ppermute | solution.py:384
  68.4 11.2 %collective-permute-start.16 = (f32[128,768]{1,0:T(8,128)}, f32[128,768]{1,0:T(8,128)S(1)}, u32[]{:S(2)}, u32[]{:S(2)}) collective-permute-start(f32[128,768]{1,0:T(8,128)} %get-tuple-element.52), channel_id=1, source_target_pairs={{0,6},{2,0},{4,2},{6,4},{1,7},{3,1},{5,3},{7,5},{8,14},{10,8},{12,... | collective-permute-start | bytes 1179656 | tf_op jit(solution)/shard_map/ppermute | solution.py:384
  70.2 9.6 %collective-permute-start.18 = (f32[8,32,512]{2,1,0:T(8,128)S(1)}, f32[8,32,512]{2,1,0:T(8,128)S(1)}, u32[]{:S(2)}, u32[]{:S(2)}) collective-permute-start(f32[8,32,512]{2,1,0:T(8,128)S(1)} %all-to-all-done.1.part0), channel_id=1, source_target_pairs={{0,24},{8,0},{16,8},{24,16},{1,25},{9,1},{17,9},{25,17},{2,26},{10... | collective-permute-start | bytes 1572872 | tf_op jit(solution)/shard_map/ppermute | solution.py:384
  71.8 9.5 %collective-permute-start.17 = (f32[8,32,512]{2,1,0:T(8,128)S(1)}, f32[8,32,512]{2,1,0:T(8,128)S(1)}, u32[]{:S(2)}, u32[]{:S(2)}) collective-permute-start(f32[8,32,512]{2,1,0:T(8,128)S(1)} %all-to-all-done.1.part0), channel_id=1, source_target_pairs={{0,8},{8,16},{16,24},{24,0},{1,9},{9,17},{17,25},{25,1},{2,10},{10... | collective-permute-start | bytes 1572872 | tf_op jit(solution)/shard_map/ppermute | solution.py:384
  81.4 11.1 %collective-permute-start.21 = (f32[4,128,768]{2,1,0:T(8,128)S(1)}, f32[4,128,768]{2,1,0:T(8,128)S(1)}, u32[]{:S(2)}, u32[]{:S(2)}) collective-permute-start(f32[4,128,768]{2,1,0:T(8,128)S(1)} %pad_maximum_fusion.few), channel_id=1, source_target_pairs={{0,1},{1,0},{2,3},{3,2},{4,5},{5,4},{6,7},{7,6},{8,9},{9,8},{10,11... | collective-permute-start | bytes 4718600 | tf_op jit(solution)/shard_map/ppermute | solution.py:384
  89.5 9.5 %collective-permute-start.20 = (f32[4,32,512]{2,1,0:T(8,128)S(1)}, f32[4,32,512]{2,1,0:T(8,128)S(1)}, u32[]{:S(2)}, u32[]{:S(2)}) collective-permute-start(f32[4,32,512]{2,1,0:T(8,128)S(1)} %slice.7), channel_id=1, source_target_pairs={{0,24},{8,0},{16,8},{24,16},{1,25},{9,1},{17,9},{25,17},{2,26},{10... | collective-permute-start | bytes 786440 | tf_op jit(solution)/shard_map/ppermute | solution.py:384
  89.6 9.5 %collective-permute-start.19 = (f32[4,32,512]{2,1,0:T(8,128)S(1)}, f32[4,32,512]{2,1,0:T(8,128)S(1)}, u32[]{:S(2)}, u32[]{:S(2)}) collective-permute-start(f32[4,32,512]{2,1,0:T(8,128)S(1)} %slice.6), channel_id=1, source_target_pairs={{0,8},{8,16},{16,24},{24,0},{1,9},{9,17},{17,25},{25,1},{2,10},{10... | collective-permute-start | bytes 786440 | tf_op jit(solution)/shard_map/ppermute | solution.py:384
  (5 other events, 61.3 us)

commit v5 on v4

--- a/solution.py
+++ b/solution.py
@@ -425,8 +425,8 @@
     near = lax.ppermute(few, "z", [(i, i ^ 1) for i in range(NZ)])
     (few,) = call(add_two_kernel, [], [few, near], [(F32, (CHUNK, S))], [])
     (strip,) = call(select_kernel, where, [target_row, spread], [(F32, (NZ, CHUNK, S))], [])
-    few, strip = lax.optimization_barrier((few, strip))
     far = [shift(few, "z", NZ, i) for i in (2, 4, 6)]
+    far, strip = lax.optimization_barrier((far, strip))
     (few,) = call(add_four_kernel, [], [few, *far], [(F32, (CHUNK, S))], [])
     few, strip = lax.optimization_barrier((few, strip))
     strips = lax.all_to_all(strip, "z", 0, 0)

time: 103 us -> 102 us (level)
  waiting for transfers between devices: 31.6 us -> 29.5 us
    ppermute x21, waiting for transfers between devices: 29.3 us -> 27.2 us  [shift(): lax.ppermute(value, axis, [(i, (i + by) % size) for i in range(size)])]
  transfers between devices with their start and end apart: 24 -> 24, of which waited for: 16 -> 16; matrix products, arithmetic and copies ran while one was open for 1% -> 1% of each run, Pallas kernels for 10% -> 12%
where the time goes in v5:
time: 102 us; the launch traced here: 101 us
  starting transfers between devices  54.2 us (53%)
  waiting for transfers between devices  29.5 us (29%)
  Pallas kernels  16.3 us (16%)
    ppermute x21, starting transfers between devices, shift(): lax.ppermute(value, axis, [(i, (i + by) % size) for i in range(size)])  37.4 us
    ppermute x21, waiting for transfers between devices, shift(): lax.ppermute(value, axis, [(i, (i + by) % size) for i in range(size)])  27.2 us
    pallas_call x9, Pallas kernels, call(): pl.pallas_call(kernel, out_shape=[jax.ShapeDtypeStruct(shape, kind) for k...  16.3 us
    all_to_all x1, starting transfers between devices, body(): spread = lax.all_to_all(raw.reshape(N_PCOL, CHUNK * 2, B), ('z', 'x'), 0, 0)  12 us
    all_to_all x1, starting transfers between devices, body(): strips = lax.all_to_all(strip, 'z', 0, 0)  3.57 us
    ppermute x1, waiting for transfers between devices, body(): near = lax.ppermute(few, 'z', [(i, i ^ 1) for i in range(NZ)])  2.32 us
  transfers between devices with their start and end apart: 24, of which 16 were waited for; matrix products, arithmetic and copies ran while one was open for 1% of the time, Pallas kernels for 12%

profile of v5, /device:TPU:1, one launch (start us, length us, event | category | flops | bytes accessed | tf_op | source)
XLA Modules:
  0.0 101.5 jit_solution(6735069583748778834)
XLA Ops:
  0.0 12.0 %all-to-all-start = ((f32[32,64,128]{2,1,0:T(8,128)}), f32[32,64,128]{2,1,0:T(8,128)S(1)}, u32[]{:S(2)}, u32[]{:S(2)}) async-start(f32[32,64,128]{2,1,0:T(8,128)} %bitcast.22), calls=%async_computation | async-start | bytes 2097152 | tf_op jit(solution)/shard_map/all_to_all | solution.py:403
  12.3 2.7 %shard_map.55 = (f32[4,128,256]{2,1,0:T(8,128)S(1)}, f32[4,128,256]{2,1,0:T(8,128)S(1)}, f32[1024,256]{1,0:T(8,128)S(1)}) custom-call(s32[5]{0:T(128)S(1)} %stack.53.pos, s32[4]{0:T(128)S(1)} %copy-done.3, s32[64]{0:T(128)S(1)} %copy-done.4, s32[64,64]{1,0:T(8,128)S(1)} %copy-done.1, s32[512,1]{1,0:T(8,128)S(1)} %copy.7.target_col, s32[1,512]{1,0:T(1,128)S(1)} %bitcast.26, ...), custom_call_target="tpu_custom_call" | custom-call | tf_op jit(solution)/shard_map/pallas_call | solution.py:373
  16.0 1.5 %collective-permute-done.received = f32[4,128,256]{2,1,0:T(8,128)S(1)} collective-permute-done((f32[4,128,256]{2,1,0:T(8,128)S(1)}, f32[4,128,256]{2,1,0:T(8,128)S(1)}, u32[]{:S(2)}, u32[]{:S(2)}) %collective-permute-start) | collective-permute-done | bytes 524320 | tf_op jit(solution)/shard_map/ppermute | solution.py:384
  19.0 2.6 %collective-permute-start.2 = (f32[128,256]{1,0:T(8,128)S(1)}, f32[128,256]{1,0:T(8,128)S(1)}, u32[]{:S(2)}, u32[]{:S(2)}) collective-permute-start(f32[128,256]{1,0:T(8,128)S(1)} %get-tuple-element.35), channel_id=1, source_target_pairs={{0,4},{2,6},{4,0},{6,2},{1,5},{3,7},{5,1},{7,3},{8,12},{10,14},{12... | collective-permute-start | bytes 393224 | tf_op jit(solution)/shard_map/ppermute | solution.py:384
  23.8 3.9 %collective-permute-done.2.part2 = f32[128,256]{1,0:T(8,128)S(1)} collective-permute-done((f32[128,256]{1,0:T(8,128)S(1)}, f32[128,256]{1,0:T(8,128)S(1)}, u32[]{:S(2)}, u32[]{:S(2)}) %collective-permute-start.2) | collective-permute-done | bytes 131104 | tf_op jit(solution)/shard_map/ppermute | solution.py:384
  28.3 1.6 %collective-permute-start.4 = (f32[32,256]{1,0:T(8,128)S(1)}, f32[32,256]{1,0:T(8,128)S(1)}, u32[]{:S(2)}, u32[]{:S(2)}) collective-permute-start(f32[32,256]{1,0:T(8,128)S(1)} %get-tuple-element.38), channel_id=1, source_target_pairs={{0,8},{8,16},{16,24},{24,0},{1,9},{9,17},{17,25},{25,1},{2,10},{10... | collective-permute-start | bytes 98312 | tf_op jit(solution)/shard_map/ppermute | solution.py:384
  29.9 2.4 %collective-permute-start.5 = (f32[32,256]{1,0:T(8,128)S(1)}, f32[32,256]{1,0:T(8,128)S(1)}, u32[]{:S(2)}, u32[]{:S(2)}) collective-permute-start(f32[32,256]{1,0:T(8,128)S(1)} %get-tuple-element.39), channel_id=1, source_target_pairs={{0,16},{8,24},{16,0},{24,8},{1,17},{9,25},{17,1},{25,9},{2,18},{10... | collective-permute-start | bytes 98312 | tf_op jit(solution)/shard_map/ppermute | solution.py:384
  37.4 2.3 %collective-permute-done.7.b = f32[32,512]{1,0:T(8,128)S(1)} collective-permute-done((f32[32,512]{1,0:T(8,128)S(1)}, f32[32,512]{1,0:T(8,128)S(1)}, u32[]{:S(2)}, u32[]{:S(2)}) %collective-permute-start.7) | collective-permute-done | bytes 65568 | tf_op jit(solution)/shard_map/ppermute | solution.py:425
  39.8 3.2 %collective-permute-start.10 = (f32[32,512]{1,0:T(8,128)S(1)}, f32[32,512]{1,0:T(8,128)S(1)}, u32[]{:S(2)}, u32[]{:S(2)}) collective-permute-start(f32[32,512]{1,0:T(8,128)S(1)} %shard_map.59.a), channel_id=1, source_target_pairs={{0,192},{32,224},{64,0},{96,32},{128,64},{160,96},{192,128},{224,1... | collective-permute-start | bytes 196616 | tf_op jit(solution)/shard_map/ppermute | solution.py:384
  42.9 3.5 %collective-permute-start.9 = (f32[32,512]{1,0:T(8,128)S(1)}, f32[32,512]{1,0:T(8,128)S(1)}, u32[]{:S(2)}, u32[]{:S(2)}) collective-permute-start(f32[32,512]{1,0:T(8,128)S(1)} %shard_map.59.a), channel_id=1, source_target_pairs={{0,128},{32,160},{64,192},{96,224},{128,0},{160,32},{192,64},{224,... | collective-permute-start | bytes 196616 | tf_op jit(solution)/shard_map/ppermute | solution.py:384
  47.2 2.0 %shard_map.60 = f32[8,32,512]{2,1,0:T(8,128)} custom-call(s32[5]{0:T(128)S(1)} %stack.53.pos, s32[4]{0:T(128)S(1)} %copy-done.3, s32[64]{0:T(128)S(1)} %copy-done.4, s32[64,64]{1,0:T(8,128)S(1)} %copy-done.1, s32[1,512]{1,0:T(1,128)S(1)} %bitcast.27, f32[32,64,128]{2,1,0:T(8,128)S(1)} %all-to-all-done.spread), custom_call_target="tpu_custom_call" | custom-call | tf_op jit(solution)/shard_map/pallas_call | solution.py:373
  50.1 2.4 %collective-permute-done.8.b = f32[32,512]{1,0:T(8,128)S(1)} collective-permute-done((f32[32,512]{1,0:T(8,128)S(1)}, f32[32,512]{1,0:T(8,128)S(1)}, u32[]{:S(2)}, u32[]{:S(2)}) %collective-permute-start.8) | collective-permute-done | bytes 65568 | tf_op jit(solution)/shard_map/ppermute | solution.py:384
  52.5 3.6 %all-to-all-start.1 = ((f32[8,32,512]{2,1,0:T(8,128)}), f32[8,32,512]{2,1,0:T(8,128)S(1)}, u32[]{:S(2)}, u32[]{:S(2)}) async-start(f32[8,32,512]{2,1,0:T(8,128)} %shard_map.60), calls=%async_computation.1 | async-start | bytes 1048576 | tf_op jit(solution)/shard_map/all_to_all | solution.py:432
  56.1 1.6 %collective-permute-start.13 = (f32[32,512]{1,0:T(8,128)S(1)}, f32[32,512]{1,0:T(8,128)S(1)}, u32[]{:S(2)}, u32[]{:S(2)}) collective-permute-start(f32[32,512]{1,0:T(8,128)S(1)} %shard_map.61), channel_id=1, source_target_pairs={{0,24},{8,0},{16,8},{24,16},{1,25},{9,1},{17,9},{25,17},{2,26},{10... | collective-permute-start | bytes 196616 | tf_op jit(solution)/shard_map/ppermute | solution.py:384
  59.5 2.8 %collective-permute-done.12 = f32[32,512]{1,0:T(8,128)S(1)} collective-permute-done((f32[32,512]{1,0:T(8,128)S(1)}, f32[32,512]{1,0:T(8,128)S(1)}, u32[]{:S(2)}, u32[]{:S(2)}) %collective-permute-start.12) | collective-permute-done | bytes 65568 | tf_op jit(solution)/shard_map/ppermute | solution.py:384
  63.5 2.3 %collective-permute-start.15 = (f32[128,768]{1,0:T(8,128)}, f32[128,768]{1,0:T(8,128)S(1)}, u32[]{:S(2)}, u32[]{:S(2)}) collective-permute-start(f32[128,768]{1,0:T(8,128)} %get-tuple-element.56), channel_id=1, source_target_pairs={{0,4},{2,6},{4,0},{6,2},{1,5},{3,7},{5,1},{7,3},{8,12},{10,14},{12... | collective-permute-start | bytes 1179656 | tf_op jit(solution)/shard_map/ppermute | solution.py:384
  66.5 2.0 %collective-permute-start.16 = (f32[128,768]{1,0:T(8,128)}, f32[128,768]{1,0:T(8,128)S(1)}, u32[]{:S(2)}, u32[]{:S(2)}) collective-permute-start(f32[128,768]{1,0:T(8,128)} %get-tuple-element.56), channel_id=1, source_target_pairs={{0,6},{2,0},{4,2},{6,4},{1,7},{3,1},{5,3},{7,5},{8,14},{10,8},{12,... | collective-permute-start | bytes 1179656 | tf_op jit(solution)/shard_map/ppermute | solution.py:384
  70.0 2.0 %collective-permute-done.15 = f32[128,768]{1,0:T(8,128)S(1)} collective-permute-done((f32[128,768]{1,0:T(8,128)}, f32[128,768]{1,0:T(8,128)S(1)}, u32[]{:S(2)}, u32[]{:S(2)}) %collective-permute-start.15) | collective-permute-done | bytes 393248 | tf_op jit(solution)/shard_map/ppermute | solution.py:384
  72.0 4.8 %collective-permute-done.14 = f32[128,768]{1,0:T(8,128)S(1)} collective-permute-done((f32[128,768]{1,0:T(8,128)}, f32[128,768]{1,0:T(8,128)S(1)}, u32[]{:S(2)}, u32[]{:S(2)}) %collective-permute-start.14) | collective-permute-done | bytes 393248 | tf_op jit(solution)/shard_map/ppermute | solution.py:384
  77.8 1.6 %collective-permute-done.17.part1 = f32[8,32,512]{2,1,0:T(8,128)S(1)} collective-permute-done((f32[8,32,512]{2,1,0:T(8,128)S(1)}, f32[8,32,512]{2,1,0:T(8,128)S(1)}, u32[]{:S(2)}, u32[]{:S(2)}) %collective-permute-start.17) | collective-permute-done | bytes 524320 | tf_op jit(solution)/shard_map/ppermute | solution.py:384
  79.5 8.5 %collective-permute-start.21 = (f32[4,128,768]{2,1,0:T(8,128)S(1)}, f32[4,128,768]{2,1,0:T(8,128)S(1)}, u32[]{:S(2)}, u32[]{:S(2)}) collective-permute-start(f32[4,128,768]{2,1,0:T(8,128)S(1)} %pad_maximum_fusion.few), channel_id=1, source_target_pairs={{0,1},{1,0},{2,3},{3,2},{4,5},{5,4},{6,7},{7,6},{8,9},{9,8},{10,11... | collective-permute-start | bytes 4718600 | tf_op jit(solution)/shard_map/ppermute | solution.py:384
  88.1 1.5 %collective-permute-start.19 = (f32[4,32,512]{2,1,0:T(8,128)S(1)}, f32[4,32,512]{2,1,0:T(8,128)S(1)}, u32[]{:S(2)}, u32[]{:S(2)}) collective-permute-start(f32[4,32,512]{2,1,0:T(8,128)S(1)} %slice.6), channel_id=1, source_target_pairs={{0,8},{8,16},{16,24},{24,0},{1,9},{9,17},{17,25},{25,1},{2,10},{10... | collective-permute-start | bytes 786440 | tf_op jit(solution)/shard_map/ppermute | solution.py:384
  91.0 6.5 %shard_map.62 = (f32[512,512]{1,0:T(8,128)S(1)}, f32[512,256]{1,0:T(8,128)S(1)}, bf16[512,256]{1,0:T(8,128)(2,1)S(1)}, bf16[512,256]{1,0:T(8,128)(2,1)S(1)}) custom-call(s32[5]{0:T(128)S(1)} %stack.53.pos, s32[4]{0:T(128)S(1)} %copy-done.3, f32[4,128,768]{2,1,0:T(8,128)S(1)} %pad_maximum_fusion.few, f32[4,128,768]{2,1,0:T(8,128)S(1)} %collective-permute-done.21.few_other), custom_call_target="tpu_custom_call" | custom-call | tf_op jit(solution)/shard_map/pallas_call | solution.py:373
  97.6 3.9 %shard_map.63 = f32[2048,128]{1,0:T(8,128)} custom-call(s32[5]{0:T(128)S(1)} %stack.53.pos, s32[4]{0:T(128)S(1)} %copy-done.3, s32[1,512]{1,0:T(1,128)S(1)} %bitcast.28, f32[1024,256]{1,0:T(8,128)S(1)} %get-tuple-element.30.rows, f32[8,32,512]{2,1,0:T(8,128)S(1)} %all-to-all-done.1.part0, f32[8,32,512]{2,1,0:T(8,128)S(1)} %collective-permute-done.17.part1, ...), custom_call_target="tpu_custom_call" | custom-call | tf_op jit(solution)/shard_map/pallas_call | solution.py:373
  (50 shorter events, 20.2 us)
Async XLA Ops:
  0.0 47.2 %all-to-all-start = ((f32[32,64,128]{2,1,0:T(8,128)}), f32[32,64,128]{2,1,0:T(8,128)S(1)}, u32[]{:S(2)}, u32[]{:S(2)}) async-start(f32[32,64,128]{2,1,0:T(8,128)} %bitcast.22), calls=%async_computation | async-start | bytes 2097152 | tf_op jit(solution)/shard_map/all_to_all | solution.py:403
  15.0 2.6 %collective-permute-start = (f32[4,128,256]{2,1,0:T(8,128)S(1)}, f32[4,128,256]{2,1,0:T(8,128)S(1)}, u32[]{:S(2)}, u32[]{:S(2)}) collective-permute-start(f32[4,128,256]{2,1,0:T(8,128)S(1)} %get-tuple-element.32), channel_id=1, source_target_pairs={{0,1},{1,0},{2,3},{3,2},{4,5},{5,4},{6,7},{7,6},{8,9},{9,8},{10,11... | collective-permute-start | bytes 1572872 | tf_op jit(solution)/shard_map/ppermute | solution.py:384
  17.6 6.1 %collective-permute-start.1 = (f32[128,256]{1,0:T(8,128)S(1)}, f32[128,256]{1,0:T(8,128)S(1)}, u32[]{:S(2)}, u32[]{:S(2)}) collective-permute-start(f32[128,256]{1,0:T(8,128)S(1)} %get-tuple-element.34), channel_id=1, source_target_pairs={{0,2},{2,4},{4,6},{6,0},{1,3},{3,5},{5,7},{7,1},{8,10},{10,12},{12... | collective-permute-start | bytes 393224 | tf_op jit(solution)/shard_map/ppermute | solution.py:384
  19.0 8.7 %collective-permute-start.2 = (f32[128,256]{1,0:T(8,128)S(1)}, f32[128,256]{1,0:T(8,128)S(1)}, u32[]{:S(2)}, u32[]{:S(2)}) collective-permute-start(f32[128,256]{1,0:T(8,128)S(1)} %get-tuple-element.35), channel_id=1, source_target_pairs={{0,4},{2,6},{4,0},{6,2},{1,5},{3,7},{5,1},{7,3},{8,12},{10,14},{12... | collective-permute-start | bytes 393224 | tf_op jit(solution)/shard_map/ppermute | solution.py:384
  21.6 6.1 %collective-permute-start.3 = (f32[128,256]{1,0:T(8,128)S(1)}, f32[128,256]{1,0:T(8,128)S(1)}, u32[]{:S(2)}, u32[]{:S(2)}) collective-permute-start(f32[128,256]{1,0:T(8,128)S(1)} %get-tuple-element.36), channel_id=1, source_target_pairs={{0,6},{2,0},{4,2},{6,4},{1,7},{3,1},{5,3},{7,5},{8,14},{10,8},{12,... | collective-permute-start | bytes 393224 | tf_op jit(solution)/shard_map/ppermute | solution.py:384
  28.3 5.2 %collective-permute-start.4 = (f32[32,256]{1,0:T(8,128)S(1)}, f32[32,256]{1,0:T(8,128)S(1)}, u32[]{:S(2)}, u32[]{:S(2)}) collective-permute-start(f32[32,256]{1,0:T(8,128)S(1)} %get-tuple-element.38), channel_id=1, source_target_pairs={{0,8},{8,16},{16,24},{24,0},{1,9},{9,17},{17,25},{25,1},{2,10},{10... | collective-permute-start | bytes 98312 | tf_op jit(solution)/shard_map/ppermute | solution.py:384
  29.9 4.6 %collective-permute-start.5 = (f32[32,256]{1,0:T(8,128)S(1)}, f32[32,256]{1,0:T(8,128)S(1)}, u32[]{:S(2)}, u32[]{:S(2)}) collective-permute-start(f32[32,256]{1,0:T(8,128)S(1)} %get-tuple-element.39), channel_id=1, source_target_pairs={{0,16},{8,24},{16,0},{24,8},{1,17},{9,25},{17,1},{25,9},{2,18},{10... | collective-permute-start | bytes 98312 | tf_op jit(solution)/shard_map/ppermute | solution.py:384
  32.3 3.4 %collective-permute-start.6 = (f32[32,256]{1,0:T(8,128)S(1)}, f32[32,256]{1,0:T(8,128)S(1)}, u32[]{:S(2)}, u32[]{:S(2)}) collective-permute-start(f32[32,256]{1,0:T(8,128)S(1)} %get-tuple-element.40), channel_id=1, source_target_pairs={{0,24},{8,0},{16,8},{24,16},{1,25},{9,1},{17,9},{25,17},{2,26},{10... | collective-permute-start | bytes 98312 | tf_op jit(solution)/shard_map/ppermute | solution.py:384
  36.3 3.5 %collective-permute-start.7 = (f32[32,512]{1,0:T(8,128)S(1)}, f32[32,512]{1,0:T(8,128)S(1)}, u32[]{:S(2)}, u32[]{:S(2)}) collective-permute-start(f32[32,512]{1,0:T(8,128)S(1)} %shard_map.58.a), channel_id=1, source_target_pairs={{0,32},{32,0},{64,96},{96,64},{128,160},{160,128},{192,224},{224,1... | collective-permute-start | bytes 196616 | tf_op jit(solution)/shard_map/ppermute | solution.py:425
  39.8 9.5 %collective-permute-start.10 = (f32[32,512]{1,0:T(8,128)S(1)}, f32[32,512]{1,0:T(8,128)S(1)}, u32[]{:S(2)}, u32[]{:S(2)}) collective-permute-start(f32[32,512]{1,0:T(8,128)S(1)} %shard_map.59.a), channel_id=1, source_target_pairs={{0,192},{32,224},{64,0},{96,32},{128,64},{160,96},{192,128},{224,1... | collective-permute-start | bytes 196616 | tf_op jit(solution)/shard_map/ppermute | solution.py:384
  42.9 7.1 %collective-permute-start.9 = (f32[32,512]{1,0:T(8,128)S(1)}, f32[32,512]{1,0:T(8,128)S(1)}, u32[]{:S(2)}, u32[]{:S(2)}) collective-permute-start(f32[32,512]{1,0:T(8,128)S(1)} %shard_map.59.a), channel_id=1, source_target_pairs={{0,128},{32,160},{64,192},{96,224},{128,0},{160,32},{192,64},{224,... | collective-permute-start | bytes 196616 | tf_op jit(solution)/shard_map/ppermute | solution.py:384
  46.4 6.1 %collective-permute-start.8 = (f32[32,512]{1,0:T(8,128)S(1)}, f32[32,512]{1,0:T(8,128)S(1)}, u32[]{:S(2)}, u32[]{:S(2)}) collective-permute-start(f32[32,512]{1,0:T(8,128)S(1)} %shard_map.59.a), channel_id=1, source_target_pairs={{0,64},{32,96},{64,128},{96,160},{128,192},{160,224},{192,0},{224,... | collective-permute-start | bytes 196616 | tf_op jit(solution)/shard_map/ppermute | solution.py:384
  52.5 16.0 %all-to-all-start.1 = ((f32[8,32,512]{2,1,0:T(8,128)}), f32[8,32,512]{2,1,0:T(8,128)S(1)}, u32[]{:S(2)}, u32[]{:S(2)}) async-start(f32[8,32,512]{2,1,0:T(8,128)} %shard_map.60), calls=%async_computation.1 | async-start | bytes 1048576 | tf_op jit(solution)/shard_map/all_to_all | solution.py:432
  56.1 3.5 %collective-permute-start.13 = (f32[32,512]{1,0:T(8,128)S(1)}, f32[32,512]{1,0:T(8,128)S(1)}, u32[]{:S(2)}, u32[]{:S(2)}) collective-permute-start(f32[32,512]{1,0:T(8,128)S(1)} %shard_map.61), channel_id=1, source_target_pairs={{0,24},{8,0},{16,8},{24,16},{1,25},{9,1},{17,9},{25,17},{2,26},{10... | collective-permute-start | bytes 196616 | tf_op jit(solution)/shard_map/ppermute | solution.py:384
  57.6 4.7 %collective-permute-start.12 = (f32[32,512]{1,0:T(8,128)S(1)}, f32[32,512]{1,0:T(8,128)S(1)}, u32[]{:S(2)}, u32[]{:S(2)}) collective-permute-start(f32[32,512]{1,0:T(8,128)S(1)} %shard_map.61), channel_id=1, source_target_pairs={{0,16},{8,24},{16,0},{24,8},{1,17},{9,25},{17,1},{25,9},{2,18},{10... | collective-permute-start | bytes 196616 | tf_op jit(solution)/shard_map/ppermute | solution.py:384
  57.7 5.0 %collective-permute-start.11 = (f32[32,512]{1,0:T(8,128)S(1)}, f32[32,512]{1,0:T(8,128)S(1)}, u32[]{:S(2)}, u32[]{:S(2)}) collective-permute-start(f32[32,512]{1,0:T(8,128)S(1)} %shard_map.61), channel_id=1, source_target_pairs={{0,8},{8,16},{16,24},{24,0},{1,9},{9,17},{17,25},{25,1},{2,10},{10... | collective-permute-start | bytes 196616 | tf_op jit(solution)/shard_map/ppermute | solution.py:384
  63.5 8.4 %collective-permute-start.15 = (f32[128,768]{1,0:T(8,128)}, f32[128,768]{1,0:T(8,128)S(1)}, u32[]{:S(2)}, u32[]{:S(2)}) collective-permute-start(f32[128,768]{1,0:T(8,128)} %get-tuple-element.56), channel_id=1, source_target_pairs={{0,4},{2,6},{4,0},{6,2},{1,5},{3,7},{5,1},{7,3},{8,12},{10,14},{12... | collective-permute-start | bytes 1179656 | tf_op jit(solution)/shard_map/ppermute | solution.py:384
  65.8 10.9 %collective-permute-start.14 = (f32[128,768]{1,0:T(8,128)}, f32[128,768]{1,0:T(8,128)S(1)}, u32[]{:S(2)}, u32[]{:S(2)}) collective-permute-start(f32[128,768]{1,0:T(8,128)} %get-tuple-element.56), channel_id=1, source_target_pairs={{0,2},{2,4},{4,6},{6,0},{1,3},{3,5},{5,7},{7,1},{8,10},{10,12},{12... | collective-permute-start | bytes 1179656 | tf_op jit(solution)/shard_map/ppermute | solution.py:384
  66.5 11.2 %collective-permute-start.16 = (f32[128,768]{1,0:T(8,128)}, f32[128,768]{1,0:T(8,128)S(1)}, u32[]{:S(2)}, u32[]{:S(2)}) collective-permute-start(f32[128,768]{1,0:T(8,128)} %get-tuple-element.56), channel_id=1, source_target_pairs={{0,6},{2,0},{4,2},{6,4},{1,7},{3,1},{5,3},{7,5},{8,14},{10,8},{12,... | collective-permute-start | bytes 1179656 | tf_op jit(solution)/shard_map/ppermute | solution.py:384
  68.5 9.3 %collective-permute-start.18 = (f32[8,32,512]{2,1,0:T(8,128)S(1)}, f32[8,32,512]{2,1,0:T(8,128)S(1)}, u32[]{:S(2)}, u32[]{:S(2)}) collective-permute-start(f32[8,32,512]{2,1,0:T(8,128)S(1)} %all-to-all-done.1.part0), channel_id=1, source_target_pairs={{0,24},{8,0},{16,8},{24,16},{1,25},{9,1},{17,9},{25,17},{2,26},{10... | collective-permute-start | bytes 1572872 | tf_op jit(solution)/shard_map/ppermute | solution.py:384
  69.9 9.5 %collective-permute-start.17 = (f32[8,32,512]{2,1,0:T(8,128)S(1)}, f32[8,32,512]{2,1,0:T(8,128)S(1)}, u32[]{:S(2)}, u32[]{:S(2)}) collective-permute-start(f32[8,32,512]{2,1,0:T(8,128)S(1)} %all-to-all-done.1.part0), channel_id=1, source_target_pairs={{0,8},{8,16},{16,24},{24,0},{1,9},{9,17},{17,25},{25,1},{2,10},{10... | collective-permute-start | bytes 1572872 | tf_op jit(solution)/shard_map/ppermute | solution.py:384
  79.5 11.5 %collective-permute-start.21 = (f32[4,128,768]{2,1,0:T(8,128)S(1)}, f32[4,128,768]{2,1,0:T(8,128)S(1)}, u32[]{:S(2)}, u32[]{:S(2)}) collective-permute-start(f32[4,128,768]{2,1,0:T(8,128)S(1)} %pad_maximum_fusion.few), channel_id=1, source_target_pairs={{0,1},{1,0},{2,3},{3,2},{4,5},{5,4},{6,7},{7,6},{8,9},{9,8},{10,11... | collective-permute-start | bytes 4718600 | tf_op jit(solution)/shard_map/ppermute | solution.py:384
  88.0 9.5 %collective-permute-start.20 = (f32[4,32,512]{2,1,0:T(8,128)S(1)}, f32[4,32,512]{2,1,0:T(8,128)S(1)}, u32[]{:S(2)}, u32[]{:S(2)}) collective-permute-start(f32[4,32,512]{2,1,0:T(8,128)S(1)} %slice.7), channel_id=1, source_target_pairs={{0,24},{8,0},{16,8},{24,16},{1,25},{9,1},{17,9},{25,17},{2,26},{10... | collective-permute-start | bytes 786440 | tf_op jit(solution)/shard_map/ppermute | solution.py:384
  88.1 9.5 %collective-permute-start.19 = (f32[4,32,512]{2,1,0:T(8,128)S(1)}, f32[4,32,512]{2,1,0:T(8,128)S(1)}, u32[]{:S(2)}, u32[]{:S(2)}) collective-permute-start(f32[4,32,512]{2,1,0:T(8,128)S(1)} %slice.6), channel_id=1, source_target_pairs={{0,8},{8,16},{16,24},{24,0},{1,9},{9,17},{17,25},{25,1},{2,10},{10... | collective-permute-start | bytes 786440 | tf_op jit(solution)/shard_map/ppermute | solution.py:384
  (5 other events, 61.3 us)
